TPU v7x, 512 devices: a whole 4x8x8 slice. The times are simulated.
512 devices in a mesh: dp: 32 (over y_hi, z, core), cent: 16 (over y_lo, x).
Axes of the slice: x: 4, y: 8 (y_hi: 2, y_lo: 4; y = y_hi * 4 + y_lo), z: 8, core: 2. Of those that a mesh axis runs over, the one named last changes fastest.
Arguments:
- points: bfloat16 [32768, 1024], P('dp'), may hold values from -64 to 64
- centroids: bfloat16 [12288, 1024], P('cent', 'dp'), may hold values from -50 to 50
- groups: bfloat16 [4096, 1024], P('dp'), may hold values from -50 to 50
Outputs:
- fresh: bfloat16 [12288, 1024], P('cent')
- new_groups: bfloat16 [4096, 1024], P('dp')
All inputs are finite; a program needn't handle non-finite values.
Results may differ from a plain program's by a relative error of at most 0.0065.
Values may be sent and summed in bfloat16 or wider, within the bound.
No kernel may reach another device: no remote copies, remote signals or barrier semaphores. Data moves between devices by JAX's collectives and lax.ppermute only.
A program may use at most 64 MiB of HBM per device.

v0:
```python
import jax
import jax.numpy as jnp
from jax import lax
from jax.sharding import PartitionSpec as P

temper = 20.0


def on_device(points, centroids, groups):
    piece = lax.all_gather(centroids, "dp", axis=1, tiled=True)
    product_acc = lax.dot_general(
        points, piece, (((1,), (1,)), ((), ())), preferred_element_type=jnp.float32
    )
    piece_wide = piece.astype(jnp.float32)
    norm_acc = jnp.sum(piece_wide * piece_wide, axis=1)
    scores_one = (2.0 * product_acc - norm_acc[None, :]) / temper
    peak_one = lax.pmax(jnp.max(scores_one, axis=1), "cent")
    expo_one = jnp.exp(scores_one - peak_one[:, None])
    total_one = lax.psum(jnp.sum(expo_one, axis=1), "cent")
    resp_one = (expo_one / total_one[:, None]).astype(jnp.bfloat16)
    sums_one = lax.dot_general(
        resp_one, points, (((0,), (0,)), ((), ())), preferred_element_type=jnp.float32
    )
    counts_one = jnp.sum(resp_one.astype(jnp.float32), axis=0)
    sums_one, counts_one = lax.psum((sums_one, counts_one), "dp")
    fresh = ((sums_one + piece.astype(jnp.float32)) / (counts_one[:, None] + 1.0)).astype(
        jnp.bfloat16
    )
    group_wide = groups.astype(jnp.float32)
    gnorm = jnp.sum(group_wide * group_wide, axis=1)
    product_two = lax.dot_general(
        fresh, groups, (((1,), (1,)), ((), ())), preferred_element_type=jnp.float32
    )
    scores_two = (2.0 * product_two - gnorm[None, :]) / temper
    peak_two = lax.pmax(jnp.max(scores_two, axis=1), "dp")
    expo_two = jnp.exp(scores_two - peak_two[:, None])
    total_two = lax.psum(jnp.sum(expo_two, axis=1), "dp")
    resp_two = (expo_two / total_two[:, None]).astype(jnp.bfloat16)
    weighted = (counts_one[:, None] * resp_two.astype(jnp.float32)).astype(jnp.bfloat16)
    sums_two = lax.dot_general(
        weighted, fresh, (((0,), (0,)), ((), ())), preferred_element_type=jnp.float32
    )
    counts_two = jnp.sum(weighted.astype(jnp.float32), axis=0)
    sums_two, counts_two = lax.psum((sums_two, counts_two), "cent")
    new_groups = ((sums_two + group_wide) / (counts_two[:, None] + 1.0)).astype(jnp.bfloat16)
    return (fresh, new_groups)


def solution(mesh):
    return jax.shard_map(
        on_device,
        mesh=mesh,
        in_specs=(P("dp", None), P("cent", "dp"), P("dp", None)),
        out_specs=(P("cent", None), P("dp", None)),
        check_vma=False,
    )
```

profile of v0, /device:TPU:1, one launch (start us, length us, event | category | flops | bytes accessed | tf_op | source)
XLA Modules:
  0.0 890.0 jit_solution(10247600298834297205)
XLA Ops:
  7.2 0.0 copy-start
  7.2 0.0 all-gather.2.cloned.1.call-start
  7.2 0.7 all-gather.2.cloned.1.call-update
  7.9 0.0 all-reduce.3.cloned.1.call-start
  8.0 98.0 %all-gather.2.cloned.1.call-done = bf16[768,1024]{0,1:T(8,128)(2,1)} async-done(((bf16[768,32]{0,1:T(8,128)(2,1)}), bf16[768,1024]{0,1:T(8,128)(2,1)}) %all-gather.2.cloned.1.call-update) | async-done | bytes 1572880 | tf_op jit(solution)/shard_map/all_gather | solution.py:10
  105.9 2.6 copy.6
  108.5 1.8 fusion
  110.3 5.1 fusion.4
  115.3 35.2 %pmax.14 = f32[1024]{0:T(1024)S(1)} all-reduce(f32[1024]{0:T(1024)S(1)} %get-tuple-element.6), channel_id=1, replica_groups=mesh['dp'=32,'cent'=16] {'cent'}, use_global_device_ids=true, to_apply=%region_2.0 | all-reduce | flops 1024 | bytes 8192 | tf_op jit(solution)/shard_map/pmax | solution.py:17
  150.6 2.7 fusion.3
  153.2 30.9 %psum.42 = f32[1024]{0:T(1024)S(1)} all-reduce(f32[1024]{0:T(1024)S(1)} %fusion.3), channel_id=1, replica_groups=mesh['dp'=32,'cent'=16] {'cent'}, use_global_device_ids=true, to_apply=%region_4.0 | all-reduce | flops 1024 | bytes 8192 | tf_op jit(solution)/shard_map/psum | solution.py:19
  184.1 3.0 convert_reduce_fusion
  187.1 3.5 fusion.12
  190.7 0.0 all-reduce.3.cloned.1.call-update
  190.7 0.0 all-reduce.5.cloned.1.call-start
  190.7 0.9 copy-done.2
  191.6 0.1 fusion.7
  191.7 98.2 %psum.44 = f32[768]{0:T(1024)S(1)} all-reduce(f32[768]{0:T(1024)S(1)} %get-tuple-element.4), channel_id=1, replica_groups=mesh['dp'=32,'cent'=16] {'dp'}, use_global_device_ids=true, to_apply=%region_7.0 | all-reduce | flops 768 | bytes 6144 | tf_op jit(solution)/shard_map/psum | solution.py:25
  289.9 260.3 %all-reduce.3.cloned.1.call-done = f32[768,1024]{1,0:T(8,128)} async-done(((f32[768,1024]{1,0:T(8,128)}), f32[768,1024]{1,0:T(8,128)}) %all-reduce.3.cloned.1.call-update) | async-done | bytes 3145744 | tf_op jit(solution)/shard_map/psum | solution.py:25
  550.2 3.0 fusion.2
  553.3 0.0 copy-start.1
  553.3 1.1 copy-done.1
  554.4 0.7 fusion.11
  555.1 84.3 %pmax.15 = f32[768]{0:T(1024)S(1)} all-reduce(f32[768]{0:T(1024)S(1)} %get-tuple-element.8), channel_id=1, replica_groups=mesh['dp'=32,'cent'=16] {'dp'}, use_global_device_ids=true, to_apply=%region_10.0 | all-reduce | flops 768 | bytes 6144 | tf_op jit(solution)/shard_map/pmax | solution.py:35
  639.4 0.1 fusion.10
  639.5 92.0 %psum.45 = f32[768]{0:T(1024)S(1)} all-reduce(f32[768]{0:T(1024)S(1)} %fusion.10), channel_id=1, replica_groups=mesh['dp'=32,'cent'=16] {'dp'}, use_global_device_ids=true, to_apply=%region_12.0 | all-reduce | flops 768 | bytes 6144 | tf_op jit(solution)/shard_map/psum | solution.py:37
  731.5 0.2 convert_reduce_fusion.1
  731.6 2.6 fusion.13
  734.2 0.0 all-reduce.5.cloned.1.call-update
  734.3 33.6 %psum.47 = f32[128]{0:T(128)S(1)} all-reduce(f32[128]{0:T(128)S(1)} %get-tuple-element.2), channel_id=1, replica_groups=mesh['dp'=32,'cent'=16] {'cent'}, use_global_device_ids=true, to_apply=%region_15.0 | all-reduce | flops 128 | bytes 1024 | tf_op jit(solution)/shard_map/psum | solution.py:44
  767.9 113.7 %all-reduce.5.cloned.1.call-done = f32[128,1024]{1,0:T(8,128)} async-done(((f32[128,1024]{1,0:T(8,128)}), f32[128,1024]{1,0:T(8,128)}) %all-reduce.5.cloned.1.call-update) | async-done | bytes 524304 | tf_op jit(solution)/shard_map/psum | solution.py:44
  881.6 1.9 fusion.9
  (4 shorter events, 0.0 us)
Async XLA Ops:
  7.2 103.1 %copy-start = (bf16[1024,1024]{1,0:T(8,128)(2,1)S(1)}, bf16[1024,1024]{1,0:T(8,128)(2,1)}, u32[]{:S(2)}) copy-start(bf16[1024,1024]{1,0:T(8,128)(2,1)} %param.3) | copy-start | bytes 6291460
  7.2 98.7 %all-gather.2.cloned.1.call-start = ((), (), s32[]{:S(2)}) async-start(), calls=%async_computation | async-start | bytes 1622016 | tf_op jit(solution)/shard_map/all_gather | solution.py:10
  7.9 542.3 %all-reduce.3.cloned.1.call-start = ((), (), s32[]{:S(2)}) async-start(), calls=%async_computation.1 | async-start | bytes 6291456 | tf_op jit(solution)/shard_map/psum | solution.py:25
  190.7 0.9 copy-start.2
  190.7 690.9 %all-reduce.5.cloned.1.call-start = ((), (), s32[]{:S(2)}) async-start(), calls=%async_computation.2 | async-start | bytes 1048576 | tf_op jit(solution)/shard_map/psum | solution.py:44
  553.3 1.1 copy-start.1
Sparse Core Ops, SparseCore 0:
  11.4 94.5 all-gather.1
  190.8 359.3 all-reduce.2
  734.4 147.1 all-reduce.4
where the time goes:
time: 900 us; the launch traced here: 890 us
  waiting for transfers between devices  473 us (53%)
  blocking collectives  374 us (42%)
  between operations  13.8 us (2%)
  other arithmetic  12.7 us (1%)
  matrix products  11.8 us (1%)
    psum x1, waiting for transfers between devices, on_device(): sums_one, counts_one = lax.psum((sums_one, counts_one), 'dp')  260 us
    psum x1, waiting for transfers between devices, on_device(): sums_two, counts_two = lax.psum((sums_two, counts_two), 'cent')  114 us
    psum x1, blocking collectives, on_device(): sums_one, counts_one = lax.psum((sums_one, counts_one), 'dp')  98.2 us
    all_gather x1, waiting for transfers between devices, on_device(): piece = lax.all_gather(centroids, 'dp', axis=1, tiled=True)  98 us
    psum x1, blocking collectives, on_device(): total_two = lax.psum(jnp.sum(expo_two, axis=1), 'dp')  92 us
    pmax x1, blocking collectives, on_device(): peak_two = lax.pmax(jnp.max(scores_two, axis=1), 'dp')  84.3 us
    pmax x1, blocking collectives, on_device(): peak_one = lax.pmax(jnp.max(scores_one, axis=1), 'cent')  35.2 us
    psum x1, blocking collectives, on_device(): sums_two, counts_two = lax.psum((sums_two, counts_two), 'cent')  33.6 us
  transfers between devices with their start and end apart: 3, of which 3 were waited for; matrix products, arithmetic and copies ran while one was open for 0% of the time, Pallas kernels for 0%

commit v1 on v0

v1 whole, which is shorter than its diff:
```python
import jax
import jax.numpy as jnp
from jax import lax
from jax.sharding import Mesh, PartitionSpec as P

temper = 20.0
f32, bf16 = jnp.float32, jnp.bfloat16
DP = ("y_hi", "z", "core")
CHIPS = ("y_hi", "z")
CENT = ("y_lo", "x")
SWAP = [(0, 1), (1, 0)]


def spread(block, axes, n):
    return lax.all_to_all(jnp.broadcast_to(block[None], (n, *block.shape)), axes, 0, 0)


def parts(count):
    high = lax.reduce_precision(count, 8, 7)
    rest = count - high
    mid = lax.reduce_precision(rest, 8, 7)
    return [p.astype(bf16) for p in (high, mid, rest - mid)]


def with_count(rows, count):
    n = rows.shape[0]
    lanes = jnp.concatenate([*parts(count), jnp.zeros((n, 125), bf16)], axis=1)
    return jnp.concatenate([rows.astype(bf16), lanes], axis=1)


def add_up(blocks):
    total = jnp.sum(blocks.astype(f32), axis=0)
    count = total[:, 1024:1025] + total[:, 1025:1026] + total[:, 1026:1027]
    return total[:, :1024], count


def combine(peaks, totals):
    peak = jnp.max(peaks, axis=0)
    return peak, jnp.sum(totals * jnp.exp(peaks - peak[None]), axis=0)


def on_device(points, centroids, groups):
    core = lax.axis_index("core")
    chip = lax.axis_index(CHIPS)
    cent = lax.axis_index(CENT)
    points_other = lax.ppermute(points, "core", SWAP)
    groups_other = lax.ppermute(groups, "core", SWAP)
    points_both = jnp.concatenate([points, points_other], axis=0)
    groups_both = jnp.concatenate(
        [
            jnp.where(core == 0, groups, groups_other),
            jnp.where(core == 0, groups_other, groups),
        ],
        axis=0,
    )

    halves = centroids.T.reshape(32, 2, 384).transpose(1, 0, 2)
    to_send = jnp.broadcast_to(halves[None], (16, 2, 32, 384)).reshape(32, 32, 384)
    piece_t = lax.all_to_all(to_send, DP, 0, 0).reshape(1024, 384)
    piece = piece_t.T
    piece_wide = piece.astype(f32)
    norm_one = jnp.sum(piece_wide * piece_wide, axis=1, keepdims=True)
    product_one = lax.dot_general(
        piece, points_both, (((1,), (1,)), ((), ())), preferred_element_type=f32
    )
    scores_one = (2.0 * product_one - norm_one) / temper
    peak_here = jnp.max(scores_one, axis=0)
    total_here = jnp.sum(jnp.exp(scores_one - peak_here[None]), axis=0)
    pairs = spread(jnp.stack([peak_here, total_here]), CENT, 16)
    pair = jnp.stack(combine(pairs[:, 0], pairs[:, 1]))
    other = lax.ppermute(pair, "core", SWAP)
    other = jnp.concatenate([other[:, 1024:], other[:, :1024]], axis=1)
    peak_one, total_one = combine(
        jnp.stack([pair[0], other[0]]), jnp.stack([pair[1], other[1]])
    )
    resp_one = (jnp.exp(scores_one - peak_one[None]) / total_one[None]).astype(bf16)
    sums_one = lax.dot_general(
        resp_one, points_both, (((1,), (0,)), ((), ())), preferred_element_type=f32
    )
    counts_one = jnp.sum(resp_one.astype(f32), axis=1, keepdims=True)
    blocks = with_count(sums_one, counts_one).reshape(16, 24, 1152)
    sums, counts = add_up(lax.all_to_all(blocks, CHIPS, 0, 0))
    piece_rows = lax.dynamic_slice_in_dim(piece, chip * 24, 24, axis=0)
    fresh_rows = ((sums + piece_rows.astype(f32)) / (counts + 1.0)).astype(bf16)
    fresh = spread(fresh_rows, CHIPS, 16).reshape(384, 1024)
    fresh_other = lax.ppermute(fresh, "core", SWAP)
    fresh_all = jnp.concatenate(
        [jnp.where(core == 0, fresh, fresh_other), jnp.where(core == 0, fresh_other, fresh)],
        axis=0,
    )

    group_wide = groups_both.astype(f32)
    norm_two = jnp.sum(group_wide * group_wide, axis=1, keepdims=True)
    product_two = lax.dot_general(
        groups_both, fresh, (((1,), (1,)), ((), ())), preferred_element_type=f32
    )
    scores_two = (2.0 * product_two - norm_two) / temper
    peak_here = jnp.max(scores_two, axis=0)
    total_here = jnp.sum(jnp.exp(scores_two - peak_here[None]), axis=0)
    lane = lax.broadcasted_iota(jnp.int32, (24, 384), 1)
    row = lax.broadcasted_iota(jnp.int32, (24, 384), 0)
    counts_lane = jnp.sum(jnp.where(lane == row + chip * 24, counts, 0.0), axis=0)
    trios = spread(jnp.stack([peak_here, total_here, counts_lane]), CHIPS, 16)
    peak_two, total_two = combine(trios[:, 0], trios[:, 1])
    counts_row = jnp.sum(trios[:, 2], axis=0)
    resp_two = (jnp.exp(scores_two - peak_two[None]) / total_two[None]).astype(bf16)
    weighted = (counts_row[None] * resp_two.astype(f32)).astype(bf16)
    sums_two = lax.dot_general(
        weighted, fresh, (((1,), (0,)), ((), ())), preferred_element_type=f32
    )
    counts_two = jnp.sum(weighted.astype(f32), axis=1, keepdims=True)
    blocks = with_count(sums_two, counts_two).reshape(32, 8, 1152)
    sums, counts = add_up(lax.all_to_all(blocks, ("core", *CENT), 0, 0))
    group_rows = lax.dynamic_slice_in_dim(groups, cent * 8, 8, axis=0)
    new_rows = ((sums + group_rows.astype(f32)) / (counts + 1.0)).astype(bf16)
    new_groups = spread(new_rows, CENT, 16).reshape(128, 1024)
    return (fresh_all, new_groups)


def solution(mesh):
    split = Mesh(mesh.devices.reshape(2, 8, 2, 4, 4), ("y_hi", "z", "core", "y_lo", "x"))
    return jax.shard_map(
        on_device,
        mesh=split,
        in_specs=(P(DP, None), P(CENT, DP), P(DP, None)),
        out_specs=(P(CENT, None), P(DP, None)),
        check_vma=False,
    )
```

time: 900 us -> 202 us (0.22); the launches traced: 890 us -> 201 us
  waiting for transfers between devices: 473 us -> 84.8 us
  blocking collectives: 374 us -> 38.4 us
  starting transfers between devices: 0.12 us -> 52.9 us
  between operations: 13.8 us -> 0.94 us
    psum x2 -> x0, waiting for transfers between devices: 374 us -> none  [the longest x1 260 us: on_device(): sums_one, counts_one = lax.psum((sums_one, counts_one), 'dp')]
    psum x4 -> x0, blocking collectives: 255 us -> none  [the longest x1 98.2 us: on_device(): sums_one, counts_one = lax.psum((sums_one, counts_one), 'dp')]
    pmax x2 -> x0, blocking collectives: 120 us -> none  [the longest x1 84.3 us: on_device(): peak_two = lax.pmax(jnp.max(scores_two, axis=1), 'dp')]
    all_gather x1 -> x0, waiting for transfers between devices: 98 us -> none  [on_device(): piece = lax.all_gather(centroids, 'dp', axis=1, tiled=True)]
    all_to_all x0 -> x5, waiting for transfers between devices: none -> 82.9 us  [the longest x2 24.8 us: spread(): lax.all_to_all(jnp.broadcast_to(block[None], (n, *block.shape)), axes, 0, 0)]
    all_to_all x0 -> x2, blocking collectives: none -> 38.4 us  [spread(): lax.all_to_all(jnp.broadcast_to(block[None], (n, *block.shape)), axes, 0, 0)]
    all_to_all x0 -> x5, starting transfers between devices: none -> 34.2 us  [the longest x2 13.8 us: spread(): lax.all_to_all(jnp.broadcast_to(block[None], (n, *block.shape)), axes, 0, 0)]
    ppermute x0 -> x4, starting transfers between devices: none -> 18.7 us  [the longest x1 8.92 us: on_device(): points_other = lax.ppermute(points, 'core', SWAP)]
  transfers between devices with their start and end apart: 3 -> 9, of which waited for: 3 -> 7; matrix products, arithmetic and copies ran while one was open for 0% -> 3% of each run, Pallas kernels for 0% -> 0%
where the time goes in v1:
time: 202 us; the launch traced here: 201 us
  waiting for transfers between devices  84.8 us (42%)
  starting transfers between devices  52.9 us (26%)
  blocking collectives  38.4 us (19%)
  local copies, waits for them, and re-layouts  12.7 us (6%)
  matrix products  6.99 us (3%)
  other arithmetic  4.75 us (2%)
    all_to_all x2, blocking collectives, spread(): lax.all_to_all(jnp.broadcast_to(block[None], (n, *block.shape)), axes, 0, 0)  38.4 us
    all_to_all x2, waiting for transfers between devices, spread(): lax.all_to_all(jnp.broadcast_to(block[None], (n, *block.shape)), axes, 0, 0)  24.8 us
    all_to_all x1, waiting for transfers between devices, on_device(): sums, counts = add_up(lax.all_to_all(blocks, CHIPS, 0, 0))  22.1 us
    all_to_all x1, waiting for transfers between devices, on_device(): piece_t = lax.all_to_all(to_send, DP, 0, 0).reshape(1024, 384)  20.6 us
    all_to_all x1, waiting for transfers between devices, on_device(): sums, counts = add_up(lax.all_to_all(blocks, ('core', *CENT), 0, 0))  15.5 us
    all_to_all x2, starting transfers between devices, spread(): lax.all_to_all(jnp.broadcast_to(block[None], (n, *block.shape)), axes, 0, 0)  13.8 us
    all_to_all x1, starting transfers between devices, on_device(): piece_t = lax.all_to_all(to_send, DP, 0, 0).reshape(1024, 384)  10.5 us
    ppermute x1, starting transfers between devices, on_device(): points_other = lax.ppermute(points, 'core', SWAP)  8.92 us
  transfers between devices with their start and end apart: 9, of which 7 were waited for; matrix products, arithmetic and copies ran while one was open for 3% of the time, Pallas kernels for 0%

profile of v1, /device:TPU:1, one launch (start us, length us, event | category | flops | bytes accessed | tf_op | source)
XLA Modules:
  0.0 201.5 jit_solution(3475492627839085512)
XLA Ops:
  0.6 8.9 %collective-permute-start = (bf16[1024,1024]{1,0:T(8,128)(2,1)}, bf16[1024,1024]{1,0:T(8,128)(2,1)}, u32[]{:S(2)}, u32[]{:S(2)}) collective-permute-start(bf16[1024,1024]{1,0:T(8,128)(2,1)} %param.3), channel_id=1, source_target_pairs={{0,16},{16,0},{1,17},{17,1},{2,18},{18,2},{3,19},{19,3},{4,20},{20... | collective-permute-start | bytes 6291464 | tf_op jit(solution)/shard_map/ppermute | solution.py:46
  9.6 0.8 reshape.161
  10.4 1.0 broadcast_in_dim.24
  11.4 10.5 %all-to-all-start = ((bf16[32,32,384]{2,1,0:T(8,128)(2,1)}), bf16[32,32,384]{2,1,0:T(8,128)(2,1)S(1)}, u32[]{:S(2)}, u32[]{:S(2)}) async-start(bf16[32,32,384]{2,1,0:T(8,128)(2,1)} %bitcast.2), calls=%async_computation | async-start | bytes 1572864 | tf_op jit(solution)/shard_map/all_to_all | solution.py:59
  21.9 1.5 constant_dynamic-update-slice_fusion.1
  23.4 20.6 %all-to-all-done = bf16[32,32,384]{2,1,0:T(8,128)(2,1)S(1)} async-done(((bf16[32,32,384]{2,1,0:T(8,128)(2,1)}), bf16[32,32,384]{2,1,0:T(8,128)(2,1)S(1)}, u32[]{:S(2)}, u32[]{:S(2)}) %all-to-all-start) | async-done | bytes 786464 | tf_op jit(solution)/shard_map/all_to_all | solution.py:59
  44.3 3.1 %constant_dynamic-update-slice_fusion = bf16[2048,1024]{1,0:T(8,128)(2,1)} fusion(bf16[2048,1024]{1,0:T(8,128)(2,1)} %constant_dynamic-update-slice_fusion.1, bf16[1024,1024]{1,0:T(8,128)(2,1)} %collective-permute-done), kind=kLoop, calls=%fused_computation.65 | loop fusion | bytes 4194304 | tf_op jit(solution)/shard_map/concatenate | solution.py:48
  47.3 4.3 %fusion.32 = (f32[2048]{0:T(1024)S(1)}, f32[2048,384]{0,1:T(8,128)S(1)}) fusion(f32[384]{0:T(512)S(1)} %multiply_reduce_fusion, bf16[2048,1024]{1,0:T(8,128)(2,1)} %constant_dynamic-update-slice_fusion, bf16[1024,384]{1,0:T(8,128)(2,1)S(1)} %bitcast.53), kind=kOutput, calls=%fused_computation.86 | convolution fusion | flops 1613756416 | bytes 8136192 | tf_op jit(solution)/shard_map/dot_general | solution.py:63
  52.2 18.1 %all_to_all.35 = f32[16,2,2048]{2,1,0:T(2,128)S(1)} all-to-all(f32[16,2,2048]{2,1,0:T(2,128)S(1)} %broadcast_in_dim.25), channel_id=1, replica_groups=mesh['y_hi'=2,'z'=8,'core'=2,'y_lo'=4,'x'=4] {'y_lo','x'}, dimensions={0} | all-to-all | bytes 524288 | tf_op jit(solution)/shard_map/all_to_all | solution.py:15
  70.6 5.0 %collective-permute-start.1 = (f32[2,2048]{1,0:T(2,128)S(1)}, f32[2,2048]{1,0:T(2,128)S(1)}, u32[]{:S(2)}, u32[]{:S(2)}) collective-permute-start(f32[2,2048]{1,0:T(2,128)S(1)} %pad_maximum_fusion.4), channel_id=1, source_target_pairs={{0,16},{16,0},{1,17},{17,1},{2,18},{18,2},{3,19},{19,3},{4,20},{20... | collective-permute-start | bytes 49160 | tf_op jit(solution)/shard_map/ppermute | solution.py:71
  75.6 0.8 collective-permute-done.1
  76.5 0.7 convert_reduce_fusion
  77.2 1.8 convolution_convert_fusion
  79.7 1.1 concatenate.27
  80.8 3.8 %all-to-all-start.2 = ((bf16[16,24,1152]{2,1,0:T(8,128)(2,1)}), bf16[16,24,1152]{2,1,0:T(8,128)(2,1)S(1)}, u32[]{:S(2)}, u32[]{:S(2)}) async-start(bf16[16,24,1152]{2,1,0:T(8,128)(2,1)} %concatenate.27), calls=%async_computation.2 | async-start | bytes 1769472 | tf_op jit(solution)/shard_map/all_to_all | solution.py:82
  84.9 22.1 %all-to-all-done.2 = bf16[16,24,1152]{2,1,0:T(8,128)(2,1)S(1)} async-done(((bf16[16,24,1152]{2,1,0:T(8,128)(2,1)}), bf16[16,24,1152]{2,1,0:T(8,128)(2,1)S(1)}, u32[]{:S(2)}, u32[]{:S(2)}) %all-to-all-start.2) | async-done | bytes 884768 | tf_op jit(solution)/shard_map/all_to_all | solution.py:82
  107.3 1.0 broadcast_in_dim.31
  108.3 10.3 %all-to-all-start.3 = ((bf16[16,24,1024]{2,1,0:T(8,128)(2,1)}), bf16[16,24,1024]{2,1,0:T(8,128)(2,1)S(1)}, u32[]{:S(2)}, u32[]{:S(2)}) async-start(bf16[16,24,1024]{2,1,0:T(8,128)(2,1)} %broadcast_in_dim.31), calls=%async_computation.3 | async-start | bytes 1572864 | tf_op jit(solution)/shard_map/all_to_all | solution.py:15
  118.6 2.7 %collective-permute-start.3 = (bf16[128,1024]{1,0:T(8,128)(2,1)S(1)}, bf16[128,1024]{1,0:T(8,128)(2,1)S(1)}, u32[]{:S(2)}, u32[]{:S(2)}) collective-permute-start(bf16[128,1024]{1,0:T(8,128)(2,1)S(1)} %copy-done.2), channel_id=1, source_target_pairs={{0,16},{16,0},{1,17},{17,1},{2,18},{18,2},{3,19},{19,3},{4,20},{20... | collective-permute-start | bytes 786440 | tf_op jit(solution)/shard_map/ppermute | solution.py:47
  121.3 1.1 collective-permute-done.3
  122.7 17.0 %all-to-all-done.3 = bf16[16,24,1024]{2,1,0:T(8,128)(2,1)S(1)} async-done(((bf16[16,24,1024]{2,1,0:T(8,128)(2,1)}), bf16[16,24,1024]{2,1,0:T(8,128)(2,1)S(1)}, u32[]{:S(2)}, u32[]{:S(2)}) %all-to-all-start.3) | async-done | bytes 786464 | tf_op jit(solution)/shard_map/all_to_all | solution.py:15
  139.7 0.5 fusion.33
  140.3 20.3 %all_to_all.36 = f32[16,3,384]{2,1,0:T(4,128)S(1)} all-to-all(f32[16,3,384]{2,1,0:T(4,128)S(1)} %broadcast_in_dim.35), channel_id=1, replica_groups=mesh['y_hi'=2,'z'=8,'core'=2,'y_lo'=4,'x'=4] {'y_hi','z'}, dimensions={0} | all-to-all | bytes 147456 | tf_op jit(solution)/shard_map/all_to_all | solution.py:15
  162.0 1.0 concatenate.31
  163.1 6.2 %all-to-all-start.5 = ((bf16[32,8,1152]{2,1,0:T(8,128)(2,1)}), bf16[32,8,1152]{2,1,0:T(8,128)(2,1)S(1)}, u32[]{:S(2)}, u32[]{:S(2)}) async-start(bf16[32,8,1152]{2,1,0:T(8,128)(2,1)} %concatenate.31), calls=%async_computation.5 | async-start | bytes 1179648 | tf_op jit(solution)/shard_map/all_to_all | solution.py:113
  169.2 2.1 %collective-permute-start.2 = (bf16[384,1024]{1,0:T(8,128)(2,1)S(1)}, bf16[384,1024]{1,0:T(8,128)(2,1)S(1)}, u32[]{:S(2)}, u32[]{:S(2)}) collective-permute-start(bf16[384,1024]{1,0:T(8,128)(2,1)S(1)} %bitcast.52), channel_id=1, source_target_pairs={{0,16},{16,0},{1,17},{17,1},{2,18},{18,2},{3,19},{19,3},{4,20},{20... | collective-permute-start | bytes 2359304 | tf_op jit(solution)/shard_map/ppermute | solution.py:86
  171.4 15.5 %all-to-all-done.5 = bf16[32,8,1152]{2,1,0:T(8,128)(2,1)S(1)} async-done(((bf16[32,8,1152]{2,1,0:T(8,128)(2,1)}), bf16[32,8,1152]{2,1,0:T(8,128)(2,1)S(1)}, u32[]{:S(2)}, u32[]{:S(2)}) %all-to-all-start.5) | async-done | bytes 589856 | tf_op jit(solution)/shard_map/all_to_all | solution.py:113
  187.3 0.7 broadcast_in_dim.37
  188.0 3.5 %all-to-all-start.6 = ((bf16[16,8,1024]{2,1,0:T(8,128)(2,1)}), bf16[16,8,1024]{2,1,0:T(8,128)(2,1)S(1)}, u32[]{:S(2)}, u32[]{:S(2)}) async-start(bf16[16,8,1024]{2,1,0:T(8,128)(2,1)} %broadcast_in_dim.37), calls=%async_computation.6 | async-start | bytes 524288 | tf_op jit(solution)/shard_map/all_to_all | solution.py:15
  191.7 1.3 pad_maximum_fusion
  193.0 7.8 %all-to-all-done.6 = bf16[16,8,1024]{2,1,0:T(8,128)(2,1)S(1)} async-done(((bf16[16,8,1024]{2,1,0:T(8,128)(2,1)}), bf16[16,8,1024]{2,1,0:T(8,128)(2,1)S(1)}, u32[]{:S(2)}, u32[]{:S(2)}) %all-to-all-start.6) | async-done | bytes 262176 | tf_op jit(solution)/shard_map/all_to_all | solution.py:15
  200.8 0.7 copy.100
  (55 shorter events, 5.0 us)
Async XLA Ops:
  0.6 21.2 %copy-start = (bf16[1024,1024]{1,0:T(8,128)(2,1)S(1)}, bf16[1024,1024]{1,0:T(8,128)(2,1)}, u32[]{:S(2)}) copy-start(bf16[1024,1024]{1,0:T(8,128)(2,1)} %param.3) | copy-start | bytes 6291460
  0.6 43.6 %collective-permute-start = (bf16[1024,1024]{1,0:T(8,128)(2,1)}, bf16[1024,1024]{1,0:T(8,128)(2,1)}, u32[]{:S(2)}, u32[]{:S(2)}) collective-permute-start(bf16[1024,1024]{1,0:T(8,128)(2,1)} %param.3), channel_id=1, source_target_pairs={{0,16},{16,0},{1,17},{17,1},{2,18},{18,2},{3,19},{19,3},{4,20},{20... | collective-permute-start | bytes 6291464 | tf_op jit(solution)/shard_map/ppermute | solution.py:46
  11.4 32.6 %all-to-all-start = ((bf16[32,32,384]{2,1,0:T(8,128)(2,1)}), bf16[32,32,384]{2,1,0:T(8,128)(2,1)S(1)}, u32[]{:S(2)}, u32[]{:S(2)}) async-start(bf16[32,32,384]{2,1,0:T(8,128)(2,1)} %bitcast.2), calls=%async_computation | async-start | bytes 1572864 | tf_op jit(solution)/shard_map/all_to_all | solution.py:59
  52.2 25.0 %copy-start.1 = (bf16[2048,1024]{1,0:T(8,128)(2,1)S(1)}, bf16[2048,1024]{1,0:T(8,128)(2,1)}, u32[]{:S(2)}) copy-start(bf16[2048,1024]{1,0:T(8,128)(2,1)} %constant_dynamic-update-slice_fusion) | copy-start | bytes 12582916
  70.6 5.8 %collective-permute-start.1 = (f32[2,2048]{1,0:T(2,128)S(1)}, f32[2,2048]{1,0:T(2,128)S(1)}, u32[]{:S(2)}, u32[]{:S(2)}) collective-permute-start(f32[2,2048]{1,0:T(2,128)S(1)} %pad_maximum_fusion.4), channel_id=1, source_target_pairs={{0,16},{16,0},{1,17},{17,1},{2,18},{18,2},{3,19},{19,3},{4,20},{20... | collective-permute-start | bytes 49160 | tf_op jit(solution)/shard_map/ppermute | solution.py:71
  80.8 37.8 %copy-start.2 = (bf16[128,1024]{1,0:T(8,128)(2,1)S(1)}, bf16[128,1024]{1,0:T(8,128)(2,1)}, u32[]{:S(2)}) copy-start(bf16[128,1024]{1,0:T(8,128)(2,1)} %param.5) | copy-start | bytes 786436
  80.8 26.1 %all-to-all-start.2 = ((bf16[16,24,1152]{2,1,0:T(8,128)(2,1)}), bf16[16,24,1152]{2,1,0:T(8,128)(2,1)S(1)}, u32[]{:S(2)}, u32[]{:S(2)}) async-start(bf16[16,24,1152]{2,1,0:T(8,128)(2,1)} %concatenate.27), calls=%async_computation.2 | async-start | bytes 1769472 | tf_op jit(solution)/shard_map/all_to_all | solution.py:82
  108.3 31.4 %all-to-all-start.3 = ((bf16[16,24,1024]{2,1,0:T(8,128)(2,1)}), bf16[16,24,1024]{2,1,0:T(8,128)(2,1)S(1)}, u32[]{:S(2)}, u32[]{:S(2)}) async-start(bf16[16,24,1024]{2,1,0:T(8,128)(2,1)} %broadcast_in_dim.31), calls=%async_computation.3 | async-start | bytes 1572864 | tf_op jit(solution)/shard_map/all_to_all | solution.py:15
  118.6 3.8 %collective-permute-start.3 = (bf16[128,1024]{1,0:T(8,128)(2,1)S(1)}, bf16[128,1024]{1,0:T(8,128)(2,1)S(1)}, u32[]{:S(2)}, u32[]{:S(2)}) collective-permute-start(bf16[128,1024]{1,0:T(8,128)(2,1)S(1)} %copy-done.2), channel_id=1, source_target_pairs={{0,16},{16,0},{1,17},{17,1},{2,18},{18,2},{3,19},{19,3},{4,20},{20... | collective-permute-start | bytes 786440 | tf_op jit(solution)/shard_map/ppermute | solution.py:47
  163.1 23.8 %all-to-all-start.5 = ((bf16[32,8,1152]{2,1,0:T(8,128)(2,1)}), bf16[32,8,1152]{2,1,0:T(8,128)(2,1)S(1)}, u32[]{:S(2)}, u32[]{:S(2)}) async-start(bf16[32,8,1152]{2,1,0:T(8,128)(2,1)} %concatenate.31), calls=%async_computation.5 | async-start | bytes 1179648 | tf_op jit(solution)/shard_map/all_to_all | solution.py:113
  169.2 22.3 %collective-permute-start.2 = (bf16[384,1024]{1,0:T(8,128)(2,1)S(1)}, bf16[384,1024]{1,0:T(8,128)(2,1)S(1)}, u32[]{:S(2)}, u32[]{:S(2)}) collective-permute-start(bf16[384,1024]{1,0:T(8,128)(2,1)S(1)} %bitcast.52), channel_id=1, source_target_pairs={{0,16},{16,0},{1,17},{17,1},{2,18},{18,2},{3,19},{19,3},{4,20},{20... | collective-permute-start | bytes 2359304 | tf_op jit(solution)/shard_map/ppermute | solution.py:86
  188.0 12.8 %all-to-all-start.6 = ((bf16[16,8,1024]{2,1,0:T(8,128)(2,1)}), bf16[16,8,1024]{2,1,0:T(8,128)(2,1)S(1)}, u32[]{:S(2)}, u32[]{:S(2)}) async-start(bf16[16,8,1024]{2,1,0:T(8,128)(2,1)} %broadcast_in_dim.37), calls=%async_computation.6 | async-start | bytes 524288 | tf_op jit(solution)/shard_map/all_to_all | solution.py:15

commit v2 on v0

v2 whole, which is shorter than its diff:
```python
import jax
import jax.numpy as jnp
from jax import lax
from jax.experimental import pallas as pl
from jax.experimental.pallas import tpu as pltpu
from jax.sharding import Mesh, PartitionSpec as P

temper = 20.0
f32, bf16 = jnp.float32, jnp.bfloat16
DP = ("y_hi", "z", "core")
CHIPS = ("y_hi", "z")
CENT = ("y_lo", "x")
SWAP = [(0, 1), (1, 0)]
D = 1024
WIDE = 1152
ROWS = 384
OWN = 24
VMEM = pl.BlockSpec(memory_space=pltpu.VMEM)
SMEM = pl.BlockSpec(memory_space=pltpu.SMEM)
NT = (((1,), (1,)), ((), ()))
NN = (((1,), (0,)), ((), ()))


def params():
    return pltpu.CompilerParams(vmem_limit_bytes=40 * 1024 * 1024)


def cost(flops, nbytes, exps=0):
    return pl.CostEstimate(flops=flops, bytes_accessed=nbytes, transcendentals=exps)


def count_lanes(count):
    n = count.shape[0]
    high = count.astype(bf16).astype(f32)
    mid = (count - high).astype(bf16).astype(f32)
    low = count - high - mid
    lane = lax.broadcasted_iota(jnp.int32, (n, 128), 1)
    wide = jnp.where(lane == 0, high, jnp.where(lane == 1, mid, jnp.where(lane == 2, low, 0.0)))
    return wide.astype(bf16)


def add_up(blocks_ref, n):
    total = blocks_ref[0].astype(f32)
    for i in range(1, n):
        total = total + blocks_ref[i].astype(f32)
    count = jnp.sum(total[:, D:], axis=1, keepdims=True)
    return total[:, :D], count


def scores_kernel(piece_t, points_a, points_b, piece, scores_a, scores_b, pairs, norm):
    @pl.when(pl.program_id(0) == 0)
    def _():
        rows = piece_t[...].T
        piece[...] = rows
        wide = rows.astype(f32)
        norm[...] = jnp.sum(wide * wide, axis=1, keepdims=True)

    found = []
    for points, scores in ((points_a, scores_a), (points_b, scores_b)):
        product = lax.dot_general(piece[...], points[...], NT, preferred_element_type=f32)
        s = (2.0 * product - norm[...]) / temper
        scores[...] = s
        peak = jnp.max(s, axis=0, keepdims=True)
        found += [peak, jnp.sum(jnp.exp(s - peak), axis=0, keepdims=True)]
    block = jnp.concatenate(found, axis=0)
    for i in range(16):
        pairs[i] = block


def level_one_scores(piece_t, points_a, points_b):
    step = 256
    points_spec = pl.BlockSpec((step, D), lambda i: (i, 0))
    scores_spec = pl.BlockSpec((ROWS, step), lambda i: (0, i))
    return pl.pallas_call(
        scores_kernel,
        grid=(1024 // step,),
        in_specs=[pl.BlockSpec((D, ROWS), lambda i: (0, 0)), points_spec, points_spec],
        out_specs=[
            pl.BlockSpec((ROWS, D), lambda i: (0, 0)),
            scores_spec,
            scores_spec,
            pl.BlockSpec((16, 4, step), lambda i: (0, 0, i)),
        ],
        out_shape=[
            jax.ShapeDtypeStruct((ROWS, D), bf16),
            jax.ShapeDtypeStruct((ROWS, 1024), f32),
            jax.ShapeDtypeStruct((ROWS, 1024), f32),
            jax.ShapeDtypeStruct((16, 4, 1024), f32),
        ],
        scratch_shapes=[pltpu.VMEM((ROWS, 1), f32)],
        compiler_params=params(),
        cost_estimate=cost(2 * ROWS * 2048 * D, 8 << 20, ROWS * 2048),
    )(piece_t, points_a, points_b)


def combine_kernel(pairs, out):
    for row in (0, 2):
        peaks, totals = pairs[:, row, :], pairs[:, row + 1, :]
        peak = jnp.max(peaks, axis=0, keepdims=True)
        out[row : row + 1, :] = peak
        out[row + 1 : row + 2, :] = jnp.sum(
            totals * jnp.exp(peaks - peak), axis=0, keepdims=True
        )


def combine(pairs):
    return pl.pallas_call(
        combine_kernel,
        in_specs=[VMEM],
        out_specs=VMEM,
        out_shape=jax.ShapeDtypeStruct((4, 1024), f32),
        compiler_params=params(),
        cost_estimate=cost(1 << 17, 1 << 18, 1 << 15),
    )(pairs)


def sums_kernel(mine, other, scores_a, scores_b, points_a, points_b, out, total, count):
    @pl.when(pl.program_id(0) == 0)
    def _():
        total[...] = jnp.zeros_like(total)
        count[...] = jnp.zeros_like(count)

    for at, points, scores in ((0, points_a, scores_a), (2, points_b, scores_b)):
        peak_m, total_m = mine[at : at + 1, :], mine[at + 1 : at + 2, :]
        peak_o, total_o = other[2 - at : 3 - at, :], other[3 - at : 4 - at, :]
        peak = jnp.maximum(peak_m, peak_o)
        whole = total_m * jnp.exp(peak_m - peak) + total_o * jnp.exp(peak_o - peak)
        resp = (jnp.exp(scores[...] - peak) * (1.0 / whole)).astype(bf16)
        total[...] += lax.dot_general(resp, points[...], NN, preferred_element_type=f32)
        count[...] += jnp.sum(resp.astype(f32), axis=1, keepdims=True)

    @pl.when(pl.program_id(0) == pl.num_programs(0) - 1)
    def _():
        out[:, :D] = total[...].astype(bf16)
        out[:, D:] = count_lanes(count[...])


def level_one_sums(mine, other, scores_a, scores_b, points_a, points_b):
    step = 512
    pair_spec = pl.BlockSpec((4, step), lambda i: (0, i))
    points_spec = pl.BlockSpec((step, D), lambda i: (i, 0))
    scores_spec = pl.BlockSpec((ROWS, step), lambda i: (0, i))
    return pl.pallas_call(
        sums_kernel,
        grid=(1024 // step,),
        in_specs=[pair_spec, pair_spec, scores_spec, scores_spec, points_spec, points_spec],
        out_specs=pl.BlockSpec((ROWS, WIDE), lambda i: (0, 0)),
        out_shape=jax.ShapeDtypeStruct((ROWS, WIDE), bf16),
        scratch_shapes=[pltpu.VMEM((ROWS, D), f32), pltpu.VMEM((ROWS, 1), f32)],
        compiler_params=params(),
        cost_estimate=cost(2 * ROWS * 2048 * D, 8 << 20, ROWS * 2048),
    )(mine, other, scores_a, scores_b, points_a, points_b)


def fresh_kernel(chip, blocks, rows, fresh, counts):
    sums, count = add_up(blocks, 16)
    new = ((sums + rows[...].astype(f32)) / (count + 1.0)).astype(bf16)
    for i in range(16):
        fresh[i] = new
    lane = lax.broadcasted_iota(jnp.int32, (OWN, ROWS), 1)
    row = lax.broadcasted_iota(jnp.int32, (OWN, ROWS), 0)
    placed = jnp.where(lane == row + chip[0] * OWN, count, 0.0)
    counts[...] = jnp.sum(placed, axis=0, keepdims=True)


def finish_rows(chip, blocks, rows):
    return pl.pallas_call(
        fresh_kernel,
        in_specs=[SMEM, VMEM, VMEM],
        out_specs=[VMEM, VMEM],
        out_shape=[
            jax.ShapeDtypeStruct((16, OWN, D), bf16),
            jax.ShapeDtypeStruct((1, ROWS), f32),
        ],
        compiler_params=params(),
        cost_estimate=cost(1 << 19, 1 << 20),
    )(chip, blocks, rows)


def group_scores_kernel(fresh, groups, counts, scores, trios):
    wide = groups[...].astype(f32)
    norm = jnp.sum(wide * wide, axis=1, keepdims=True)
    product = lax.dot_general(groups[...], fresh[...], NT, preferred_element_type=f32)
    s = (2.0 * product - norm) / temper
    scores[...] = s
    peak = jnp.max(s, axis=0, keepdims=True)
    total = jnp.sum(jnp.exp(s - peak), axis=0, keepdims=True)
    block = jnp.concatenate([peak, total, counts[...], jnp.zeros_like(peak)], axis=0)
    for i in range(16):
        trios[i] = block


def level_two_scores(fresh, groups, counts):
    return pl.pallas_call(
        group_scores_kernel,
        in_specs=[VMEM] * 3,
        out_specs=[VMEM] * 2,
        out_shape=[
            jax.ShapeDtypeStruct((256, ROWS), f32),
            jax.ShapeDtypeStruct((16, 4, ROWS), f32),
        ],
        compiler_params=params(),
        cost_estimate=cost(2 * ROWS * 256 * D, 2 << 20, ROWS * 256),
    )(fresh, groups, counts)


def group_sums_kernel(scores, trios, fresh, out):
    peaks, totals = trios[:, 0, :], trios[:, 1, :]
    peak = jnp.max(peaks, axis=0, keepdims=True)
    whole = jnp.sum(totals * jnp.exp(peaks - peak), axis=0, keepdims=True)
    counts = jnp.sum(trios[:, 2, :], axis=0, keepdims=True)
    resp = (jnp.exp(scores[...] - peak) * (1.0 / whole)).astype(bf16)
    weighted = (counts * resp.astype(f32)).astype(bf16)
    sums = lax.dot_general(weighted, fresh[...], NN, preferred_element_type=f32)
    out[:, :D] = sums.astype(bf16)
    out[:, D:] = count_lanes(jnp.sum(weighted.astype(f32), axis=1, keepdims=True))


def level_two_sums(scores, trios, fresh):
    return pl.pallas_call(
        group_sums_kernel,
        in_specs=[VMEM] * 3,
        out_specs=VMEM,
        out_shape=jax.ShapeDtypeStruct((256, WIDE), bf16),
        compiler_params=params(),
        cost_estimate=cost(2 * ROWS * 256 * D, 2 << 20, ROWS * 256),
    )(scores, trios, fresh)


def groups_kernel(blocks, rows, out):
    sums, count = add_up(blocks, 32)
    new = ((sums + rows[...].astype(f32)) / (count + 1.0)).astype(bf16)
    for i in range(16):
        out[i] = new


def finish_groups(blocks, rows):
    return pl.pallas_call(
        groups_kernel,
        in_specs=[VMEM] * 2,
        out_specs=VMEM,
        out_shape=jax.ShapeDtypeStruct((16, 8, D), bf16),
        compiler_params=params(),
        cost_estimate=cost(1 << 19, 1 << 20),
    )(blocks, rows)


def exchange(blocks, axes):
    return lax.all_to_all(blocks, axes, 0, 0)


def in_core_order(core, mine, other):
    first = jnp.where(core == 0, mine, other)
    second = jnp.where(core == 0, other, mine)
    return jnp.concatenate([first, second], axis=0)


def on_device(points, centroids, groups):
    core = lax.axis_index("core")
    chip = lax.axis_index(CHIPS)
    cent = lax.axis_index(CENT)

    columns = centroids.T
    target = lax.broadcasted_iota(jnp.int32, (32, 1, 1), 0) % 2
    to_send = jnp.where(target == 0, columns[None, :, :ROWS], columns[None, :, ROWS:])
    piece_t = exchange(to_send, DP).reshape(D, ROWS)
    points_other = lax.ppermute(points, "core", SWAP)
    groups_other = lax.ppermute(groups, "core", SWAP)
    groups_both = in_core_order(core, groups, groups_other)

    piece, scores_a, scores_b, pairs = level_one_scores(piece_t, points, points_other)
    mine = combine(exchange(pairs, CENT))
    other = lax.ppermute(mine, "core", SWAP)
    sums = level_one_sums(mine, other, scores_a, scores_b, points, points_other)
    blocks = exchange(sums.reshape(16, OWN, WIDE), CHIPS)
    rows = lax.dynamic_slice_in_dim(piece, chip * OWN, OWN, axis=0)
    fresh_rows, counts = finish_rows(chip.astype(jnp.int32)[None], blocks, rows)
    fresh = exchange(fresh_rows, CHIPS).reshape(ROWS, D)
    fresh_other = lax.ppermute(fresh, "core", SWAP)
    fresh_all = in_core_order(core, fresh, fresh_other)

    scores, trios = level_two_scores(fresh, groups_both, counts)
    sums = level_two_sums(scores, exchange(trios, CHIPS), fresh)
    blocks = exchange(sums.reshape(32, 8, WIDE), ("core", *CENT))
    rows = lax.dynamic_slice_in_dim(groups, cent * 8, 8, axis=0)
    new_groups = exchange(finish_groups(blocks, rows), CENT).reshape(128, D)
    return (fresh_all, new_groups)


def solution(mesh):
    split = Mesh(mesh.devices.reshape(2, 8, 2, 4, 4), ("y_hi", "z", "core", "y_lo", "x"))
    return jax.shard_map(
        on_device,
        mesh=split,
        in_specs=(P(DP, None), P(CENT, DP), P(DP, None)),
        out_specs=(P(CENT, None), P(DP, None)),
        check_vma=False,
    )
```

time: 900 us -> 193 us (0.21); the launches traced: 890 us -> 192 us
  waiting for transfers between devices: 473 us -> 64.8 us
  blocking collectives: 374 us -> 70.4 us
  starting transfers between devices: 0.12 us -> 42.2 us
  between operations: 13.8 us -> 0.82 us
  matrix products: 11.8 us -> 0 us
  other arithmetic: 12.7 us -> 1.65 us
  Pallas kernels: 0 us -> 11 us
    psum x2 -> x0, waiting for transfers between devices: 374 us -> none  [the longest x1 260 us: on_device(): sums_one, counts_one = lax.psum((sums_one, counts_one), 'dp')]
    psum x4 -> x0, blocking collectives: 255 us -> none  [the longest x1 98.2 us: on_device(): sums_one, counts_one = lax.psum((sums_one, counts_one), 'dp')]
    pmax x2 -> x0, blocking collectives: 120 us -> none  [the longest x1 84.3 us: on_device(): peak_two = lax.pmax(jnp.max(scores_two, axis=1), 'dp')]
    all_gather x1 -> x0, waiting for transfers between devices: 98 us -> none  [on_device(): piece = lax.all_gather(centroids, 'dp', axis=1, tiled=True)]
    all_to_all x0 -> x3, blocking collectives: none -> 70.4 us  [exchange(): return lax.all_to_all(blocks, axes, 0, 0)]
    all_to_all x0 -> x4, waiting for transfers between devices: none -> 62.8 us  [exchange(): return lax.all_to_all(blocks, axes, 0, 0)]
    all_to_all x0 -> x4, starting transfers between devices: none -> 23.5 us  [exchange(): return lax.all_to_all(blocks, axes, 0, 0)]
    ppermute x0 -> x4, starting transfers between devices: none -> 18.7 us  [the longest x1 8.92 us: on_device(): points_other = lax.ppermute(points, 'core', SWAP)]
  transfers between devices with their start and end apart: 3 -> 8, of which waited for: 3 -> 6; matrix products, arithmetic and copies ran while one was open for 0% -> 1% of each run, Pallas kernels for 0% -> 0%
where the time goes in v2:
time: 193 us; the launch traced here: 192 us
  blocking collectives  70.4 us (36%)
  waiting for transfers between devices  64.8 us (34%)
  starting transfers between devices  42.2 us (22%)
  Pallas kernels  11 us (6%)
    all_to_all x3, blocking collectives, exchange(): return lax.all_to_all(blocks, axes, 0, 0)  70.4 us
    all_to_all x4, waiting for transfers between devices, exchange(): return lax.all_to_all(blocks, axes, 0, 0)  62.8 us
    all_to_all x4, starting transfers between devices, exchange(): return lax.all_to_all(blocks, axes, 0, 0)  23.5 us
    ppermute x1, starting transfers between devices, on_device(): points_other = lax.ppermute(points, 'core', SWAP)  8.92 us
    ppermute x1, starting transfers between devices, on_device(): other = lax.ppermute(mine, 'core', SWAP)  4.97 us
  transfers between devices with their start and end apart: 8, of which 6 were waited for; matrix products, arithmetic and copies ran while one was open for 1% of the time, Pallas kernels for 0%

profile of v2, /device:TPU:1, one launch (start us, length us, event | category | flops | bytes accessed | tf_op | source)
XLA Modules:
  0.0 192.3 jit_solution(7045897921180338024)
XLA Ops:
  0.6 8.9 %collective-permute-start = (bf16[1024,1024]{1,0:T(8,128)(2,1)}, bf16[1024,1024]{1,0:T(8,128)(2,1)S(1)}, u32[]{:S(2)}, u32[]{:S(2)}) collective-permute-start(bf16[1024,1024]{1,0:T(8,128)(2,1)} %points_a.3), channel_id=1, source_target_pairs={{0,16},{16,0},{1,17},{17,1},{2,18},{18,2},{3,19},{19,3},{4,20},{20... | collective-permute-start | bytes 6291464 | tf_op jit(solution)/shard_map/ppermute | solution.py:267
  9.6 0.8 fusion.1
  10.3 0.2 broadcast_select_fusion
  10.5 32.4 %all_to_all.35 = bf16[32,32,384]{2,1,0:T(8,128)(2,1)S(1)} all-to-all(bf16[32,32,384]{2,1,0:T(8,128)(2,1)S(1)} %broadcast_select_fusion), channel_id=1, replica_groups=mesh['y_hi'=2,'z'=8,'core'=2,'y_lo'=4,'x'=4] {'y_hi','z','core'}, dimensions={0} | all-to-all | bytes 1572864 | tf_op jit(solution)/shard_map/all_to_all | solution.py:249
  42.9 0.0 collective-permute-done.points_b
  42.9 3.7 %shard_map.50 = (bf16[384,1024]{1,0:T(8,128)(2,1)S(1)}, f32[384,1024]{1,0:T(8,128)S(1)}, f32[384,1024]{1,0:T(8,128)S(1)}, f32[16,4,1024]{2,1,0:T(4,128)S(1)}) custom-call(bf16[1024,384]{1,0:T(8,128)(2,1)S(1)} %bitcast.12, bf16[1024,1024]{1,0:T(8,128)(2,1)S(1)} %copy-done, bf16[1024,1024]{1,0:T(8,128)(2,1)S(1)} %collective-permute-done.points_b), custom_call_target="tpu_custom_call" | custom-call | flops 1610612736 | bytes 8388608 | tf_op jit(solution)/shard_map/pallas_call | solution.py:74
  46.6 17.8 %all_to_all.36.pairs = f32[16,4,1024]{2,1,0:T(4,128)S(1)} all-to-all(f32[16,4,1024]{2,1,0:T(4,128)S(1)} %get-tuple-element.10), channel_id=1, replica_groups=mesh['y_hi'=2,'z'=8,'core'=2,'y_lo'=4,'x'=4] {'y_lo','x'}, dimensions={0} | all-to-all | bytes 524288 | tf_op jit(solution)/shard_map/all_to_all | solution.py:249
  64.4 0.1 shard_map.51.mine
  64.5 5.0 %collective-permute-start.1 = (f32[4,1024]{1,0:T(4,128)S(1)}, f32[4,1024]{1,0:T(4,128)S(1)}, u32[]{:S(2)}, u32[]{:S(2)}) collective-permute-start(f32[4,1024]{1,0:T(4,128)S(1)} %shard_map.51.mine), channel_id=1, source_target_pairs={{0,16},{16,0},{1,17},{17,1},{2,18},{18,2},{3,19},{19,3},{4,20},{20... | collective-permute-start | bytes 49160 | tf_op jit(solution)/shard_map/ppermute | solution.py:273
  69.5 0.8 collective-permute-done.1.other
  70.3 3.4 %shard_map.52 = bf16[384,1152]{1,0:T(8,128)(2,1)} custom-call(f32[4,1024]{1,0:T(4,128)S(1)} %shard_map.51.mine, f32[4,1024]{1,0:T(4,128)S(1)} %collective-permute-done.1.other, f32[384,1024]{1,0:T(8,128)S(1)} %get-tuple-element.11.scores_a, f32[384,1024]{1,0:T(8,128)S(1)} %get-tuple-element.12.scores_b, bf16[1024,1024]{1,0:T(8,128)(2,1)S(1)} %copy-done, ...), custom_call_target="tpu_custom_call" | custom-call | flops 1610612736 | bytes 8388608 | tf_op jit(solution)/shard_map/pallas_call | solution.py:143
  73.7 3.6 %all-to-all-start.2 = ((bf16[16,24,1152]{2,1,0:T(8,128)(2,1)}), bf16[16,24,1152]{2,1,0:T(8,128)(2,1)S(1)}, u32[]{:S(2)}, u32[]{:S(2)}) async-start(bf16[16,24,1152]{2,1,0:T(8,128)(2,1)} %bitcast.3), calls=%async_computation.2 | async-start | bytes 1769472 | tf_op jit(solution)/shard_map/all_to_all | solution.py:249
  77.3 0.0 copy-start.1
  77.4 22.3 %all-to-all-done.2.blocks = bf16[16,24,1152]{2,1,0:T(8,128)(2,1)S(1)} async-done(((bf16[16,24,1152]{2,1,0:T(8,128)(2,1)}), bf16[16,24,1152]{2,1,0:T(8,128)(2,1)S(1)}, u32[]{:S(2)}, u32[]{:S(2)}) %all-to-all-start.2) | async-done | bytes 884768 | tf_op jit(solution)/shard_map/all_to_all | solution.py:249
  99.6 1.1 shard_map.53
  100.7 10.3 %all-to-all-start.3 = ((bf16[16,24,1024]{2,1,0:T(8,128)(2,1)}), bf16[16,24,1024]{2,1,0:T(8,128)(2,1)S(1)}, u32[]{:S(2)}, u32[]{:S(2)}) async-start(bf16[16,24,1024]{2,1,0:T(8,128)(2,1)} %get-tuple-element.14), calls=%async_computation.3 | async-start | bytes 1572864 | tf_op jit(solution)/shard_map/all_to_all | solution.py:249
  111.0 2.7 %collective-permute-start.3 = (bf16[128,1024]{1,0:T(8,128)(2,1)S(1)}, bf16[128,1024]{1,0:T(8,128)(2,1)S(1)}, u32[]{:S(2)}, u32[]{:S(2)}) collective-permute-start(bf16[128,1024]{1,0:T(8,128)(2,1)S(1)} %copy-done.1), channel_id=1, source_target_pairs={{0,16},{16,0},{1,17},{17,1},{2,18},{18,2},{3,19},{19,3},{4,20},{20... | collective-permute-start | bytes 786440 | tf_op jit(solution)/shard_map/ppermute | solution.py:268
  113.7 1.1 collective-permute-done.3
  114.9 17.2 %all-to-all-done.3 = bf16[16,24,1024]{2,1,0:T(8,128)(2,1)S(1)} async-done(((bf16[16,24,1024]{2,1,0:T(8,128)(2,1)}), bf16[16,24,1024]{2,1,0:T(8,128)(2,1)S(1)}, u32[]{:S(2)}, u32[]{:S(2)}) %all-to-all-start.3) | async-done | bytes 786464 | tf_op jit(solution)/shard_map/all_to_all | solution.py:249
  132.2 0.6 shard_map.54
  132.7 20.3 %all_to_all.37.trios = f32[16,4,384]{2,1,0:T(4,128)S(1)} all-to-all(f32[16,4,384]{2,1,0:T(4,128)S(1)} %get-tuple-element.17), channel_id=1, replica_groups=mesh['y_hi'=2,'z'=8,'core'=2,'y_lo'=4,'x'=4] {'y_hi','z'}, dimensions={0} | all-to-all | bytes 196608 | tf_op jit(solution)/shard_map/all_to_all | solution.py:249
  153.0 1.3 shard_map.55
  154.3 6.0 %all-to-all-start.5 = ((bf16[32,8,1152]{2,1,0:T(8,128)(2,1)}), bf16[32,8,1152]{2,1,0:T(8,128)(2,1)S(1)}, u32[]{:S(2)}, u32[]{:S(2)}) async-start(bf16[32,8,1152]{2,1,0:T(8,128)(2,1)} %bitcast.5), calls=%async_computation.5 | async-start | bytes 1179648 | tf_op jit(solution)/shard_map/all_to_all | solution.py:249
  160.3 2.1 %collective-permute-start.2 = (bf16[384,1024]{1,0:T(8,128)(2,1)S(1)}, bf16[384,1024]{1,0:T(8,128)(2,1)S(1)}, u32[]{:S(2)}, u32[]{:S(2)}) collective-permute-start(bf16[384,1024]{1,0:T(8,128)(2,1)S(1)} %bitcast.11), channel_id=1, source_target_pairs={{0,16},{16,0},{1,17},{17,1},{2,18},{18,2},{3,19},{19,3},{4,20},{20... | collective-permute-start | bytes 2359304 | tf_op jit(solution)/shard_map/ppermute | solution.py:279
  162.5 15.5 %all-to-all-done.5.blocks = bf16[32,8,1152]{2,1,0:T(8,128)(2,1)S(1)} async-done(((bf16[32,8,1152]{2,1,0:T(8,128)(2,1)}), bf16[32,8,1152]{2,1,0:T(8,128)(2,1)S(1)}, u32[]{:S(2)}, u32[]{:S(2)}) %all-to-all-start.5) | async-done | bytes 589856 | tf_op jit(solution)/shard_map/all_to_all | solution.py:249
  178.0 0.8 shard_map.56
  178.8 3.5 %all-to-all-start.6 = ((bf16[16,8,1024]{2,1,0:T(8,128)(2,1)}), bf16[16,8,1024]{2,1,0:T(8,128)(2,1)S(1)}, u32[]{:S(2)}, u32[]{:S(2)}) async-start(bf16[16,8,1024]{2,1,0:T(8,128)(2,1)} %shard_map.56), calls=%async_computation.6 | async-start | bytes 524288 | tf_op jit(solution)/shard_map/all_to_all | solution.py:249
  182.4 0.0 collective-permute-done.2
  182.4 0.2 broadcast_select_fusion.2
  182.5 1.3 pad_maximum_fusion
  183.8 7.8 %all-to-all-done.6 = bf16[16,8,1024]{2,1,0:T(8,128)(2,1)S(1)} async-done(((bf16[16,8,1024]{2,1,0:T(8,128)(2,1)}), bf16[16,8,1024]{2,1,0:T(8,128)(2,1)S(1)}, u32[]{:S(2)}, u32[]{:S(2)}) %all-to-all-start.6) | async-done | bytes 262176 | tf_op jit(solution)/shard_map/all_to_all | solution.py:249
  191.6 0.7 copy.6
  (8 shorter events, 0.1 us)
Async XLA Ops:
  0.6 42.2 %copy-start = (bf16[1024,1024]{1,0:T(8,128)(2,1)S(1)}, bf16[1024,1024]{1,0:T(8,128)(2,1)}, u32[]{:S(2)}) copy-start(bf16[1024,1024]{1,0:T(8,128)(2,1)} %points_a.3) | copy-start | bytes 6291460
  0.6 42.2 %collective-permute-start = (bf16[1024,1024]{1,0:T(8,128)(2,1)}, bf16[1024,1024]{1,0:T(8,128)(2,1)S(1)}, u32[]{:S(2)}, u32[]{:S(2)}) collective-permute-start(bf16[1024,1024]{1,0:T(8,128)(2,1)} %points_a.3), channel_id=1, source_target_pairs={{0,16},{16,0},{1,17},{17,1},{2,18},{18,2},{3,19},{19,3},{4,20},{20... | collective-permute-start | bytes 6291464 | tf_op jit(solution)/shard_map/ppermute | solution.py:267
  64.5 5.8 %collective-permute-start.1 = (f32[4,1024]{1,0:T(4,128)S(1)}, f32[4,1024]{1,0:T(4,128)S(1)}, u32[]{:S(2)}, u32[]{:S(2)}) collective-permute-start(f32[4,1024]{1,0:T(4,128)S(1)} %shard_map.51.mine), channel_id=1, source_target_pairs={{0,16},{16,0},{1,17},{17,1},{2,18},{18,2},{3,19},{19,3},{4,20},{20... | collective-permute-start | bytes 49160 | tf_op jit(solution)/shard_map/ppermute | solution.py:273
  73.7 25.9 %all-to-all-start.2 = ((bf16[16,24,1152]{2,1,0:T(8,128)(2,1)}), bf16[16,24,1152]{2,1,0:T(8,128)(2,1)S(1)}, u32[]{:S(2)}, u32[]{:S(2)}) async-start(bf16[16,24,1152]{2,1,0:T(8,128)(2,1)} %bitcast.3), calls=%async_computation.2 | async-start | bytes 1769472 | tf_op jit(solution)/shard_map/all_to_all | solution.py:249
  77.3 33.7 %copy-start.1 = (bf16[128,1024]{1,0:T(8,128)(2,1)S(1)}, bf16[128,1024]{1,0:T(8,128)(2,1)}, u32[]{:S(2)}) copy-start(bf16[128,1024]{1,0:T(8,128)(2,1)} %param.5) | copy-start | bytes 786436
  100.7 31.5 %all-to-all-start.3 = ((bf16[16,24,1024]{2,1,0:T(8,128)(2,1)}), bf16[16,24,1024]{2,1,0:T(8,128)(2,1)S(1)}, u32[]{:S(2)}, u32[]{:S(2)}) async-start(bf16[16,24,1024]{2,1,0:T(8,128)(2,1)} %get-tuple-element.14), calls=%async_computation.3 | async-start | bytes 1572864 | tf_op jit(solution)/shard_map/all_to_all | solution.py:249
  111.0 3.8 %collective-permute-start.3 = (bf16[128,1024]{1,0:T(8,128)(2,1)S(1)}, bf16[128,1024]{1,0:T(8,128)(2,1)S(1)}, u32[]{:S(2)}, u32[]{:S(2)}) collective-permute-start(bf16[128,1024]{1,0:T(8,128)(2,1)S(1)} %copy-done.1), channel_id=1, source_target_pairs={{0,16},{16,0},{1,17},{17,1},{2,18},{18,2},{3,19},{19,3},{4,20},{20... | collective-permute-start | bytes 786440 | tf_op jit(solution)/shard_map/ppermute | solution.py:268
  154.3 23.7 %all-to-all-start.5 = ((bf16[32,8,1152]{2,1,0:T(8,128)(2,1)}), bf16[32,8,1152]{2,1,0:T(8,128)(2,1)S(1)}, u32[]{:S(2)}, u32[]{:S(2)}) async-start(bf16[32,8,1152]{2,1,0:T(8,128)(2,1)} %bitcast.5), calls=%async_computation.5 | async-start | bytes 1179648 | tf_op jit(solution)/shard_map/all_to_all | solution.py:249
  160.3 22.0 %collective-permute-start.2 = (bf16[384,1024]{1,0:T(8,128)(2,1)S(1)}, bf16[384,1024]{1,0:T(8,128)(2,1)S(1)}, u32[]{:S(2)}, u32[]{:S(2)}) collective-permute-start(bf16[384,1024]{1,0:T(8,128)(2,1)S(1)} %bitcast.11), channel_id=1, source_target_pairs={{0,16},{16,0},{1,17},{17,1},{2,18},{18,2},{3,19},{19,3},{4,20},{20... | collective-permute-start | bytes 2359304 | tf_op jit(solution)/shard_map/ppermute | solution.py:279
  178.8 12.8 %all-to-all-start.6 = ((bf16[16,8,1024]{2,1,0:T(8,128)(2,1)}), bf16[16,8,1024]{2,1,0:T(8,128)(2,1)S(1)}, u32[]{:S(2)}, u32[]{:S(2)}) async-start(bf16[16,8,1024]{2,1,0:T(8,128)(2,1)} %shard_map.56), calls=%async_computation.6 | async-start | bytes 524288 | tf_op jit(solution)/shard_map/all_to_all | solution.py:249

commit v3 on v2

--- a/solution.py
+++ b/solution.py
@@ -15,18 +15,33 @@
 WIDE = 1152
 ROWS = 384
 OWN = 24
+PACK = 200
+FAR = 144
+HALF = 192
 VMEM = pl.BlockSpec(memory_space=pltpu.VMEM)
 SMEM = pl.BlockSpec(memory_space=pltpu.SMEM)
 NT = (((1,), (1,)), ((), ()))
 NN = (((1,), (0,)), ((), ()))
 
 
-def params():
-    return pltpu.CompilerParams(vmem_limit_bytes=40 * 1024 * 1024)
+def params(mib=8):
+    return pltpu.CompilerParams(vmem_limit_bytes=mib * 1024 * 1024)
 
 
 def cost(flops, nbytes, exps=0):
     return pl.CostEstimate(flops=flops, bytes_accessed=nbytes, transcendentals=exps)
+
+
+def count_row(count):
+    high = count.astype(bf16).astype(f32)
+    mid = (count - high).astype(bf16).astype(f32)
+    low = count - high - mid
+    lane = lax.broadcasted_iota(jnp.int32, (OWN, 128), 1)
+    row = lax.broadcasted_iota(jnp.int32, (OWN, 128), 0)
+    placed = jnp.where(lane == row, high, 0.0)
+    placed = jnp.where(lane == row + OWN, mid, placed)
+    placed = jnp.where(lane == row + 2 * OWN, low, placed)
+    return jnp.sum(placed, axis=0, keepdims=True)
 
 
 def count_lanes(count):
@@ -88,7 +103,7 @@
             jax.ShapeDtypeStruct((16, 4, 1024), f32),
         ],
         scratch_shapes=[pltpu.VMEM((ROWS, 1), f32)],
-        compiler_params=params(),
+        compiler_params=params(24),
         cost_estimate=cost(2 * ROWS * 2048 * D, 8 << 20, ROWS * 2048),
     )(piece_t, points_a, points_b)
 
@@ -131,8 +146,11 @@
 
     @pl.when(pl.program_id(0) == pl.num_programs(0) - 1)
     def _():
-        out[:, :D] = total[...].astype(bf16)
-        out[:, D:] = count_lanes(count[...])
+        for b in range(16):
+            at = slice(b * OWN, (b + 1) * OWN)
+            parts = [total[at, j * 128 : (j + 1) * 128] for j in range(8)]
+            tail = jnp.zeros((7, 128), f32)
+            out[b] = jnp.concatenate([*parts, count_row(count[at, :]), tail], axis=0).astype(bf16)
 
 
 def level_one_sums(mine, other, scores_a, scores_b, points_a, points_b):
@@ -144,87 +162,130 @@
         sums_kernel,
         grid=(1024 // step,),
         in_specs=[pair_spec, pair_spec, scores_spec, scores_spec, points_spec, points_spec],
-        out_specs=pl.BlockSpec((ROWS, WIDE), lambda i: (0, 0)),
-        out_shape=jax.ShapeDtypeStruct((ROWS, WIDE), bf16),
+        out_specs=pl.BlockSpec((16, PACK, 128), lambda i: (0, 0, 0)),
+        out_shape=jax.ShapeDtypeStruct((16, PACK, 128), bf16),
         scratch_shapes=[pltpu.VMEM((ROWS, D), f32), pltpu.VMEM((ROWS, 1), f32)],
-        compiler_params=params(),
+        compiler_params=params(24),
         cost_estimate=cost(2 * ROWS * 2048 * D, 8 << 20, ROWS * 2048),
     )(mine, other, scores_a, scores_b, points_a, points_b)
 
 
-def fresh_kernel(chip, blocks, rows, fresh, counts):
-    sums, count = add_up(blocks, 16)
+def fresh_kernel(z, blocks, rows, fresh, counts):
+    total = blocks[0].astype(f32)
+    for i in range(1, 16):
+        total = total + blocks[i].astype(f32)
+    sums = jnp.concatenate([total[j * OWN : (j + 1) * OWN] for j in range(8)], axis=1)
+    lane = lax.broadcasted_iota(jnp.int32, (OWN, 128), 1)
+    row = lax.broadcasted_iota(jnp.int32, (OWN, 128), 0)
+    part = (lane == row) | (lane == row + OWN) | (lane == row + 2 * OWN)
+    count = jnp.sum(jnp.where(part, total[192:193], 0.0), axis=1, keepdims=True)
     new = ((sums + rows[...].astype(f32)) / (count + 1.0)).astype(bf16)
-    for i in range(16):
+    for i in range(8):
         fresh[i] = new
-    lane = lax.broadcasted_iota(jnp.int32, (OWN, ROWS), 1)
-    row = lax.broadcasted_iota(jnp.int32, (OWN, ROWS), 0)
-    placed = jnp.where(lane == row + chip[0] * OWN, count, 0.0)
+    lane = lax.broadcasted_iota(jnp.int32, (OWN, 256), 1)
+    row = lax.broadcasted_iota(jnp.int32, (OWN, 256), 0)
+    placed = jnp.where(lane == row + z[0] * OWN, count, 0.0)
     counts[...] = jnp.sum(placed, axis=0, keepdims=True)
 
 
-def finish_rows(chip, blocks, rows):
+def finish_rows(z, blocks, rows):
     return pl.pallas_call(
         fresh_kernel,
         in_specs=[SMEM, VMEM, VMEM],
         out_specs=[VMEM, VMEM],
         out_shape=[
-            jax.ShapeDtypeStruct((16, OWN, D), bf16),
-            jax.ShapeDtypeStruct((1, ROWS), f32),
+            jax.ShapeDtypeStruct((8, OWN, D), bf16),
+            jax.ShapeDtypeStruct((1, 256), f32),
         ],
         compiler_params=params(),
         cost_estimate=cost(1 << 19, 1 << 20),
-    )(chip, blocks, rows)
-
-
-def group_scores_kernel(fresh, groups, counts, scores, trios):
-    wide = groups[...].astype(f32)
+    )(z, blocks, rows)
+
+
+def group_scores_kernel(core, fresh, near, far, counts, scores, trios):
+    groups = jnp.concatenate([near[...], far[...]], axis=0)
+    wide = groups.astype(f32)
     norm = jnp.sum(wide * wide, axis=1, keepdims=True)
-    product = lax.dot_general(groups[...], fresh[...], NT, preferred_element_type=f32)
-    s = (2.0 * product - norm) / temper
-    scores[...] = s
-    peak = jnp.max(s, axis=0, keepdims=True)
-    total = jnp.sum(jnp.exp(s - peak), axis=0, keepdims=True)
-    block = jnp.concatenate([peak, total, counts[...], jnp.zeros_like(peak)], axis=0)
+    zero = jnp.zeros((1, HALF), f32)
+    blocks = []
+    for c in range(2):
+        product = lax.dot_general(groups, fresh[c], NT, preferred_element_type=f32)
+        s = (2.0 * product - norm) / temper
+        scores[c] = s
+        peak = jnp.max(s, axis=0, keepdims=True)
+        total = jnp.sum(jnp.exp(s - peak), axis=0, keepdims=True)
+        count = jnp.where(core[0] == c, counts[:, :HALF], zero)
+        blocks += [peak, total, count, zero]
+    block = jnp.concatenate(blocks, axis=0)
     for i in range(16):
-        trios[i] = block
-
-
-def level_two_scores(fresh, groups, counts):
+        trios[i, :, :HALF] = block
+        trios[i, :, HALF:] = jnp.zeros((8, 256 - HALF), f32)
+
+
+def level_two_scores(core, fresh, near, far, counts):
     return pl.pallas_call(
         group_scores_kernel,
-        in_specs=[VMEM] * 3,
+        in_specs=[SMEM] + [VMEM] * 4,
         out_specs=[VMEM] * 2,
         out_shape=[
-            jax.ShapeDtypeStruct((256, ROWS), f32),
-            jax.ShapeDtypeStruct((16, 4, ROWS), f32),
+            jax.ShapeDtypeStruct((2, 256, HALF), f32),
+            jax.ShapeDtypeStruct((16, 8, 256), f32),
         ],
         compiler_params=params(),
         cost_estimate=cost(2 * ROWS * 256 * D, 2 << 20, ROWS * 256),
-    )(fresh, groups, counts)
-
-
-def group_sums_kernel(scores, trios, fresh, out):
-    peaks, totals = trios[:, 0, :], trios[:, 1, :]
-    peak = jnp.max(peaks, axis=0, keepdims=True)
-    whole = jnp.sum(totals * jnp.exp(peaks - peak), axis=0, keepdims=True)
-    counts = jnp.sum(trios[:, 2, :], axis=0, keepdims=True)
-    resp = (jnp.exp(scores[...] - peak) * (1.0 / whole)).astype(bf16)
-    weighted = (counts * resp.astype(f32)).astype(bf16)
-    sums = lax.dot_general(weighted, fresh[...], NN, preferred_element_type=f32)
-    out[:, :D] = sums.astype(bf16)
-    out[:, D:] = count_lanes(jnp.sum(weighted.astype(f32), axis=1, keepdims=True))
-
-
-def level_two_sums(scores, trios, fresh):
+    )(core, fresh, near, far, counts)
+
+
+def exponents_kernel(scores, out, peaks):
+    for c in range(2):
+        s = scores[c]
+        peak = jnp.max(s, axis=0, keepdims=True)
+        out[c] = jnp.exp(s - peak)
+        peaks[c] = peak
+
+
+def level_two_exponents(scores):
+    return pl.pallas_call(
+        exponents_kernel,
+        in_specs=[VMEM],
+        out_specs=[VMEM] * 2,
+        out_shape=[
+            jax.ShapeDtypeStruct((2, 256, HALF), f32),
+            jax.ShapeDtypeStruct((2, 1, HALF), f32),
+        ],
+        compiler_params=params(),
+        cost_estimate=cost(ROWS * 512, 2 << 20, ROWS * 256),
+    )(scores)
+
+
+def group_sums_kernel(y_hi, expo, here, trios, fresh, out):
+    sums, count = jnp.zeros((256, D), f32), jnp.zeros((256, 1), f32)
+    for c in range(2):
+        at = 4 * c
+        peaks, totals = trios[:, at, :], trios[:, at + 1, :]
+        peak = jnp.max(peaks, axis=0, keepdims=True)
+        whole = jnp.sum(totals * jnp.exp(peaks - peak), axis=0, keepdims=True)
+        counts = jnp.sum(trios[:, at + 2, :], axis=0, keepdims=True)
+        peak, whole, counts = [v[:, :HALF] for v in (peak, whole, counts)]
+        resp = (expo[c] * (jnp.exp(here[c] - peak) / whole)).astype(bf16)
+        weighted = (counts * resp.astype(f32)).astype(bf16)
+        sums = sums + lax.dot_general(weighted, fresh[c], NN, preferred_element_type=f32)
+        count = count + jnp.sum(weighted.astype(f32), axis=1, keepdims=True)
+    lanes = count_lanes(count)
+    for place, at in ((y_hi[0], 0), (1 - y_hi[0], 128)):
+        out[place, :, :D] = sums[at : at + 128].astype(bf16)
+        out[place, :, D:] = lanes[at : at + 128]
+
+
+def level_two_sums(y_hi, expo, here, trios, fresh):
     return pl.pallas_call(
         group_sums_kernel,
-        in_specs=[VMEM] * 3,
+        in_specs=[SMEM] + [VMEM] * 4,
         out_specs=VMEM,
-        out_shape=jax.ShapeDtypeStruct((256, WIDE), bf16),
+        out_shape=jax.ShapeDtypeStruct((2, 128, WIDE), bf16),
         compiler_params=params(),
         cost_estimate=cost(2 * ROWS * 256 * D, 2 << 20, ROWS * 256),
-    )(scores, trios, fresh)
+    )(y_hi, expo, here, trios, fresh)
 
 
 def groups_kernel(blocks, rows, out):
@@ -249,42 +310,67 @@
     return lax.all_to_all(blocks, axes, 0, 0)
 
 
-def in_core_order(core, mine, other):
-    first = jnp.where(core == 0, mine, other)
-    second = jnp.where(core == 0, other, mine)
-    return jnp.concatenate([first, second], axis=0)
+def ordered(index, mine, other):
+    return jnp.where(index == 0, mine, other), jnp.where(index == 0, other, mine)
+
+
+MIRROR = [(h * 4 + y, (1 - h) * 4 + 3 - y) for h in range(2) for y in range(4)]
 
 
 def on_device(points, centroids, groups):
     core = lax.axis_index("core")
-    chip = lax.axis_index(CHIPS)
+    y_hi = lax.axis_index("y_hi")
+    z = lax.axis_index("z")
     cent = lax.axis_index(CENT)
+    core_scalar = core.astype(jnp.int32)[None]
+    y_scalar = y_hi.astype(jnp.int32)[None]
 
     columns = centroids.T
     target = lax.broadcasted_iota(jnp.int32, (32, 1, 1), 0) % 2
     to_send = jnp.where(target == 0, columns[None, :, :ROWS], columns[None, :, ROWS:])
+    to_send, points = lax.optimization_barrier((to_send, points))
     piece_t = exchange(to_send, DP).reshape(D, ROWS)
     points_other = lax.ppermute(points, "core", SWAP)
-    groups_other = lax.ppermute(groups, "core", SWAP)
-    groups_both = in_core_order(core, groups, groups_other)
 
     piece, scores_a, scores_b, pairs = level_one_scores(piece_t, points, points_other)
     mine = combine(exchange(pairs, CENT))
     other = lax.ppermute(mine, "core", SWAP)
-    sums = level_one_sums(mine, other, scores_a, scores_b, points, points_other)
-    blocks = exchange(sums.reshape(16, OWN, WIDE), CHIPS)
-    rows = lax.dynamic_slice_in_dim(piece, chip * OWN, OWN, axis=0)
-    fresh_rows, counts = finish_rows(chip.astype(jnp.int32)[None], blocks, rows)
-    fresh = exchange(fresh_rows, CHIPS).reshape(ROWS, D)
-    fresh_other = lax.ppermute(fresh, "core", SWAP)
-    fresh_all = in_core_order(core, fresh, fresh_other)
-
-    scores, trios = level_two_scores(fresh, groups_both, counts)
-    sums = level_two_sums(scores, exchange(trios, CHIPS), fresh)
-    blocks = exchange(sums.reshape(32, 8, WIDE), ("core", *CENT))
+    blocks = level_one_sums(mine, other, scores_a, scores_b, points, points_other)
+    blocks = exchange(blocks, CHIPS)
+    rows = lax.dynamic_slice_in_dim(piece, (y_hi * 8 + z) * OWN, OWN, axis=0)
+    fresh_rows, counts = finish_rows(z.astype(jnp.int32)[None], blocks, rows)
+
+    fresh_rows, groups_ready = lax.optimization_barrier((fresh_rows, groups))
+    mine = exchange(fresh_rows, "z").reshape(HALF, D)
+    groups_far = lax.ppermute(groups_ready, ("y_hi", "y_lo"), MIRROR)
+    fresh = lax.all_gather(mine, "core")
+
+    scores, trios = level_two_scores(core_scalar, fresh, groups, groups_far, counts)
+    expo, here = level_two_exponents(scores)
+    odd = z % 2
+    rest = HALF - FAR
+    expo, mine = lax.optimization_barrier((expo, mine))
+    part = lax.dynamic_slice_in_dim(mine, odd * rest, FAR, axis=0)
+    part = lax.ppermute(part, "y_hi", SWAP)
+    trios = exchange(trios, ("z", "core"))
+    sums = level_two_sums(y_scalar, expo, here, trios, fresh)
+    sums, part = lax.optimization_barrier((sums, part))
+    lacking = jnp.where(odd == 0, part[:rest], part[FAR - rest :])
+    lacking = lax.ppermute(lacking, "z", [(i, i ^ 1) for i in range(8)])
+    far_mine = jnp.where(
+        odd == 0,
+        jnp.concatenate([part, lacking], axis=0),
+        jnp.concatenate([lacking, part], axis=0),
+    )
+    blocks = exchange(sums.reshape(32, 8, WIDE), ("y_hi", *CENT))
     rows = lax.dynamic_slice_in_dim(groups, cent * 8, 8, axis=0)
-    new_groups = exchange(finish_groups(blocks, rows), CENT).reshape(128, D)
-    return (fresh_all, new_groups)
+    new_rows = finish_groups(blocks, rows)
+    far_other = lax.ppermute(far_mine, "core", SWAP)
+    new_groups = exchange(new_rows, CENT).reshape(128, D)
+
+    far = ordered(core, far_mine, far_other)
+    first, second = ordered(y_hi, fresh[0], far[0]), ordered(y_hi, fresh[1], far[1])
+    return (jnp.concatenate([*first, *second], axis=0), new_groups)
 
 
 def solution(mesh):

time: 193 us -> 185 us (0.959)
  waiting for transfers between devices: 64.8 us -> 47.1 us
  starting transfers between devices: 42.2 us -> 48.6 us
  blocking collectives: 70.4 us -> 73.2 us
    all_to_all x4, waiting for transfers between devices: 62.8 us -> 42.8 us  [exchange(): return lax.all_to_all(blocks, axes, 0, 0)]
    ppermute x2 -> x4, starting transfers between devices: 4.83 us -> 18.1 us  [the longest x1 7.43 us: on_device(): part = lax.ppermute(part, 'y_hi', SWAP)]
    all_gather x0 -> x1, blocking collectives: none -> 7.08 us  [on_device(): fresh = lax.all_gather(mine, 'core')]
    all_to_all x4, starting transfers between devices: 23.5 us -> 16.8 us  [exchange(): return lax.all_to_all(blocks, axes, 0, 0)]
    all_to_all x3, blocking collectives: 70.4 us -> 66.2 us  [exchange(): return lax.all_to_all(blocks, axes, 0, 0)]
    ppermute x2 -> x4, waiting for transfers between devices: 1.14 us -> 3.52 us  [the longest x1 3.51 us: on_device(): lacking = lax.ppermute(lacking, 'z', [(i, i ^ 1) for i in range(8)])]
  transfers between devices with their start and end apart: 8 -> 10, of which waited for: 6 -> 6; matrix products, arithmetic and copies ran while one was open for 1% -> 1% of each run, Pallas kernels for 0% -> 1%
where the time goes in v3:
time: 185 us; the launch traced here: 184 us
  blocking collectives  73.2 us (40%)
  starting transfers between devices  48.6 us (26%)
  waiting for transfers between devices  47.1 us (25%)
  Pallas kernels  10.9 us (6%)
    all_to_all x3, blocking collectives, exchange(): return lax.all_to_all(blocks, axes, 0, 0)  66.2 us
    all_to_all x4, waiting for transfers between devices, exchange(): return lax.all_to_all(blocks, axes, 0, 0)  42.8 us
    all_to_all x4, starting transfers between devices, exchange(): return lax.all_to_all(blocks, axes, 0, 0)  16.8 us
    ppermute x1, starting transfers between devices, on_device(): points_other = lax.ppermute(points, 'core', SWAP)  8.79 us
    ppermute x1, starting transfers between devices, on_device(): part = lax.ppermute(part, 'y_hi', SWAP)  7.43 us
    all_gather x1, blocking collectives, on_device(): fresh = lax.all_gather(mine, 'core')  7.08 us
    ppermute x1, starting transfers between devices, on_device(): groups_far = lax.ppermute(groups_ready, ('y_hi', 'y_lo'), MIRROR)  5.18 us
    ppermute x1, starting transfers between devices, on_device(): other = lax.ppermute(mine, 'core', SWAP)  4.95 us
  transfers between devices with their start and end apart: 10, of which 6 were waited for; matrix products, arithmetic and copies ran while one was open for 1% of the time, Pallas kernels for 1%

profile of v3, /device:TPU:1, one launch (start us, length us, event | category | flops | bytes accessed | tf_op | source)
XLA Modules:
  0.0 184.1 jit_solution(4523780933214725694)
XLA Ops:
  0.7 0.9 fusion.1
  1.6 0.2 broadcast_select_fusion
  1.7 8.8 %collective-permute-start = (bf16[1024,1024]{1,0:T(8,128)(2,1)}, bf16[1024,1024]{1,0:T(8,128)(2,1)S(1)}, u32[]{:S(2)}, u32[]{:S(2)}) collective-permute-start(bf16[1024,1024]{1,0:T(8,128)(2,1)} %points_a.1), channel_id=1, source_target_pairs={{0,16},{16,0},{1,17},{17,1},{2,18},{18,2},{3,19},{19,3},{4,20},{20... | collective-permute-start | bytes 6291464 | tf_op jit(solution)/shard_map/ppermute | solution.py:333
  10.5 32.4 %all_to_all.35 = bf16[32,32,384]{2,1,0:T(8,128)(2,1)S(1)} all-to-all(bf16[32,32,384]{2,1,0:T(8,128)(2,1)S(1)} %broadcast_select_fusion), channel_id=1, replica_groups=mesh['y_hi'=2,'z'=8,'core'=2,'y_lo'=4,'x'=4] {'y_hi','z','core'}, dimensions={0} | all-to-all | bytes 1572864 | tf_op jit(solution)/shard_map/all_to_all | solution.py:310
  42.9 3.7 %shard_map.50 = (bf16[384,1024]{1,0:T(8,128)(2,1)S(1)}, f32[384,1024]{1,0:T(8,128)S(1)}, f32[384,1024]{1,0:T(8,128)S(1)}, f32[16,4,1024]{2,1,0:T(4,128)S(1)}) custom-call(bf16[1024,384]{1,0:T(8,128)(2,1)S(1)} %bitcast.21, bf16[1024,1024]{1,0:T(8,128)(2,1)S(1)} %copy-done, bf16[1024,1024]{1,0:T(8,128)(2,1)S(1)} %collective-permute-done.points_b), custom_call_target="tpu_custom_call" | custom-call | flops 1610612736 | bytes 8388608 | tf_op jit(solution)/shard_map/pallas_call | solution.py:89
  46.6 17.8 %all_to_all.36.pairs = f32[16,4,1024]{2,1,0:T(4,128)S(1)} all-to-all(f32[16,4,1024]{2,1,0:T(4,128)S(1)} %get-tuple-element.22), channel_id=1, replica_groups=mesh['y_hi'=2,'z'=8,'core'=2,'y_lo'=4,'x'=4] {'y_lo','x'}, dimensions={0} | all-to-all | bytes 524288 | tf_op jit(solution)/shard_map/all_to_all | solution.py:310
  64.5 5.0 %collective-permute-start.1 = (f32[4,1024]{1,0:T(4,128)S(1)}, f32[4,1024]{1,0:T(4,128)S(1)}, u32[]{:S(2)}, u32[]{:S(2)}) collective-permute-start(f32[4,1024]{1,0:T(4,128)S(1)} %shard_map.51.mine), channel_id=1, source_target_pairs={{0,16},{16,0},{1,17},{17,1},{2,18},{18,2},{3,19},{19,3},{4,20},{20... | collective-permute-start | bytes 49160 | tf_op jit(solution)/shard_map/ppermute | solution.py:337
  69.5 0.8 collective-permute-done.1.other
  70.3 3.4 %shard_map.52 = bf16[16,200,128]{2,1,0:T(8,128)(2,1)} custom-call(f32[4,1024]{1,0:T(4,128)S(1)} %shard_map.51.mine, f32[4,1024]{1,0:T(4,128)S(1)} %collective-permute-done.1.other, f32[384,1024]{1,0:T(8,128)S(1)} %get-tuple-element.23.scores_a, f32[384,1024]{1,0:T(8,128)S(1)} %get-tuple-element.24.scores_b, bf16[1024,1024]{1,0:T(8,128)(2,1)S(1)} %copy-done, ...), custom_call_target="tpu_custom_call" | custom-call | flops 1610612736 | bytes 8388608 | tf_op jit(solution)/shard_map/pallas_call | solution.py:161
  73.7 3.8 %all-to-all-start.2 = ((bf16[16,200,128]{2,1,0:T(8,128)(2,1)}), bf16[16,200,128]{2,1,0:T(8,128)(2,1)S(1)}, u32[]{:S(2)}, u32[]{:S(2)}) async-start(bf16[16,200,128]{2,1,0:T(8,128)(2,1)} %shard_map.52), calls=%async_computation.2 | async-start | bytes 1638400 | tf_op jit(solution)/shard_map/all_to_all | solution.py:310
  77.5 21.4 %all-to-all-done.2.blocks = bf16[16,200,128]{2,1,0:T(8,128)(2,1)S(1)} async-done(((bf16[16,200,128]{2,1,0:T(8,128)(2,1)}), bf16[16,200,128]{2,1,0:T(8,128)(2,1)S(1)}, u32[]{:S(2)}, u32[]{:S(2)}) %all-to-all-start.2) | async-done | bytes 819232 | tf_op jit(solution)/shard_map/all_to_all | solution.py:310
  98.9 0.9 shard_map.53
  99.8 4.4 %all-to-all-start.3 = ((bf16[8,24,1024]{2,1,0:T(8,128)(2,1)}), bf16[8,24,1024]{2,1,0:T(8,128)(2,1)S(1)}, u32[]{:S(2)}, u32[]{:S(2)}) async-start(bf16[8,24,1024]{2,1,0:T(8,128)(2,1)} %get-tuple-element.27), calls=%async_computation.3 | async-start | bytes 786432 | tf_op jit(solution)/shard_map/all_to_all | solution.py:310
  104.2 5.2 %collective-permute-start.2 = (bf16[128,1024]{1,0:T(8,128)(2,1)S(1)}, bf16[128,1024]{1,0:T(8,128)(2,1)S(1)}, u32[]{:S(2)}, u32[]{:S(2)}) collective-permute-start(bf16[128,1024]{1,0:T(8,128)(2,1)S(1)} %copy-done.1), channel_id=1, source_target_pairs={{0,268},{4,264},{8,260},{12,256},{256,12},{260,8},{264,4},{268,0},... | collective-permute-start | bytes 786440 | tf_op jit(solution)/shard_map/ppermute | solution.py:345
  109.4 5.3 %all-to-all-done.3 = bf16[8,24,1024]{2,1,0:T(8,128)(2,1)S(1)} async-done(((bf16[8,24,1024]{2,1,0:T(8,128)(2,1)}), bf16[8,24,1024]{2,1,0:T(8,128)(2,1)S(1)}, u32[]{:S(2)}, u32[]{:S(2)}) %all-to-all-start.3) | async-done | bytes 393248 | tf_op jit(solution)/shard_map/all_to_all | solution.py:310
  114.7 7.1 %all_gather.3.fresh = bf16[2,192,1024]{2,1,0:T(8,128)(2,1)S(1)} all-gather(bf16[1,192,1024]{2,1,0:T(8,128)(2,1)S(1)} %bitcast.22), channel_id=1, replica_groups=mesh['y_hi'=2,'z'=8,'core'=2,'y_lo'=4,'x'=4] {'core'}, dimensions={0}, use_global_device_ids=true | all-gather | bytes 1179648 | tf_op jit(solution)/shard_map/all_gather | solution.py:346
  121.8 0.6 shard_map.54
  122.4 0.1 shard_map.55
  122.5 7.4 %collective-permute-start.3 = (bf16[144,1024]{1,0:T(8,128)(2,1)S(1)}, bf16[144,1024]{1,0:T(8,128)(2,1)S(1)}, u32[]{:S(2)}, u32[]{:S(2)}) collective-permute-start(bf16[144,1024]{1,0:T(8,128)(2,1)S(1)} %constant_dynamic-slice_fusion.1), channel_id=1, source_target_pairs={{0,256},{256,0},{1,257},{257,1},{2,258},{258,2},{3,259},{259,3},{4... | collective-permute-start | bytes 884744 | tf_op jit(solution)/shard_map/ppermute | solution.py:354
  130.0 16.0 %all_to_all.37.trios = f32[16,8,256]{2,1,0:T(8,128)S(1)} all-to-all(f32[16,8,256]{2,1,0:T(8,128)S(1)} %get-tuple-element.34), channel_id=1, replica_groups=mesh['y_hi'=2,'z'=8,'core'=2,'y_lo'=4,'x'=4] {'z','core'}, dimensions={0} | all-to-all | bytes 262144 | tf_op jit(solution)/shard_map/all_to_all | solution.py:310
  146.0 1.3 shard_map.56
  147.3 3.9 %all-to-all-start.5 = ((bf16[32,8,1152]{2,1,0:T(8,128)(2,1)}), bf16[32,8,1152]{2,1,0:T(8,128)(2,1)S(1)}, u32[]{:S(2)}, u32[]{:S(2)}) async-start(bf16[32,8,1152]{2,1,0:T(8,128)(2,1)} %bitcast.9), calls=%async_computation.5 | async-start | bytes 1179648 | tf_op jit(solution)/shard_map/all_to_all | solution.py:310
  151.2 2.0 %collective-permute-start.4 = (bf16[48,1024]{1,0:T(8,128)(2,1)S(1)}, bf16[48,1024]{1,0:T(8,128)(2,1)S(1)}, u32[]{:S(2)}, u32[]{:S(2)}) collective-permute-start(bf16[48,1024]{1,0:T(8,128)(2,1)S(1)} %slice_select_fusion), channel_id=1, source_target_pairs={{0,32},{32,0},{64,96},{96,64},{128,160},{160,128},{192,224},{224,1... | collective-permute-start | bytes 294920 | tf_op jit(solution)/shard_map/ppermute | solution.py:359
  153.2 3.5 %collective-permute-done.4 = bf16[48,1024]{1,0:T(8,128)(2,1)S(1)} collective-permute-done((bf16[48,1024]{1,0:T(8,128)(2,1)S(1)}, bf16[48,1024]{1,0:T(8,128)(2,1)S(1)}, u32[]{:S(2)}, u32[]{:S(2)}) %collective-permute-start.4) | collective-permute-done | bytes 98336 | tf_op jit(solution)/shard_map/ppermute | solution.py:359
  156.8 3.5 %collective-permute-start.5 = (bf16[192,1024]{1,0:T(8,128)(2,1)S(1)}, bf16[192,1024]{1,0:T(8,128)(2,1)S(1)}, u32[]{:S(2)}, u32[]{:S(2)}) collective-permute-start(bf16[192,1024]{1,0:T(8,128)(2,1)S(1)} %maximum_select_fusion), channel_id=1, source_target_pairs={{0,16},{16,0},{1,17},{17,1},{2,18},{18,2},{3,19},{19,3},{4,20},{20... | collective-permute-start | bytes 1179656 | tf_op jit(solution)/shard_map/ppermute | solution.py:368
  160.3 8.5 %all-to-all-done.5.blocks = bf16[32,8,1152]{2,1,0:T(8,128)(2,1)S(1)} async-done(((bf16[32,8,1152]{2,1,0:T(8,128)(2,1)}), bf16[32,8,1152]{2,1,0:T(8,128)(2,1)S(1)}, u32[]{:S(2)}, u32[]{:S(2)}) %all-to-all-start.5) | async-done | bytes 589856 | tf_op jit(solution)/shard_map/all_to_all | solution.py:310
  168.8 0.8 shard_map.57
  169.7 4.8 %all-to-all-start.6 = ((bf16[16,8,1024]{2,1,0:T(8,128)(2,1)}), bf16[16,8,1024]{2,1,0:T(8,128)(2,1)S(1)}, u32[]{:S(2)}, u32[]{:S(2)}) async-start(bf16[16,8,1024]{2,1,0:T(8,128)(2,1)} %shard_map.57), calls=%async_computation.6 | async-start | bytes 524288 | tf_op jit(solution)/shard_map/all_to_all | solution.py:310
  174.5 0.1 broadcast_select_fusion.6
  174.6 1.3 pad_maximum_fusion
  175.8 7.5 %all-to-all-done.6 = bf16[16,8,1024]{2,1,0:T(8,128)(2,1)S(1)} async-done(((bf16[16,8,1024]{2,1,0:T(8,128)(2,1)}), bf16[16,8,1024]{2,1,0:T(8,128)(2,1)S(1)}, u32[]{:S(2)}, u32[]{:S(2)}) %all-to-all-start.6) | async-done | bytes 262176 | tf_op jit(solution)/shard_map/all_to_all | solution.py:310
  183.4 0.7 copy.6
  (15 shorter events, 0.3 us)
Async XLA Ops:
  0.6 42.2 %copy-start = (bf16[1024,1024]{1,0:T(8,128)(2,1)S(1)}, bf16[1024,1024]{1,0:T(8,128)(2,1)}, u32[]{:S(2)}) copy-start(bf16[1024,1024]{1,0:T(8,128)(2,1)} %points_a.1) | copy-start | bytes 6291460
  1.7 41.2 %collective-permute-start = (bf16[1024,1024]{1,0:T(8,128)(2,1)}, bf16[1024,1024]{1,0:T(8,128)(2,1)S(1)}, u32[]{:S(2)}, u32[]{:S(2)}) collective-permute-start(bf16[1024,1024]{1,0:T(8,128)(2,1)} %points_a.1), channel_id=1, source_target_pairs={{0,16},{16,0},{1,17},{17,1},{2,18},{18,2},{3,19},{19,3},{4,20},{20... | collective-permute-start | bytes 6291464 | tf_op jit(solution)/shard_map/ppermute | solution.py:333
  64.5 5.8 %collective-permute-start.1 = (f32[4,1024]{1,0:T(4,128)S(1)}, f32[4,1024]{1,0:T(4,128)S(1)}, u32[]{:S(2)}, u32[]{:S(2)}) collective-permute-start(f32[4,1024]{1,0:T(4,128)S(1)} %shard_map.51.mine), channel_id=1, source_target_pairs={{0,16},{16,0},{1,17},{17,1},{2,18},{18,2},{3,19},{19,3},{4,20},{20... | collective-permute-start | bytes 49160 | tf_op jit(solution)/shard_map/ppermute | solution.py:337
  73.7 30.5 %copy-start.1 = (bf16[128,1024]{1,0:T(8,128)(2,1)S(1)}, bf16[128,1024]{1,0:T(8,128)(2,1)}, u32[]{:S(2)}) copy-start(bf16[128,1024]{1,0:T(8,128)(2,1)} %near.1) | copy-start | bytes 786436
  73.7 25.2 %all-to-all-start.2 = ((bf16[16,200,128]{2,1,0:T(8,128)(2,1)}), bf16[16,200,128]{2,1,0:T(8,128)(2,1)S(1)}, u32[]{:S(2)}, u32[]{:S(2)}) async-start(bf16[16,200,128]{2,1,0:T(8,128)(2,1)} %shard_map.52), calls=%async_computation.2 | async-start | bytes 1638400 | tf_op jit(solution)/shard_map/all_to_all | solution.py:310
  99.8 14.9 %all-to-all-start.3 = ((bf16[8,24,1024]{2,1,0:T(8,128)(2,1)}), bf16[8,24,1024]{2,1,0:T(8,128)(2,1)S(1)}, u32[]{:S(2)}, u32[]{:S(2)}) async-start(bf16[8,24,1024]{2,1,0:T(8,128)(2,1)} %get-tuple-element.27), calls=%async_computation.3 | async-start | bytes 786432 | tf_op jit(solution)/shard_map/all_to_all | solution.py:310
  104.2 17.6 %collective-permute-start.2 = (bf16[128,1024]{1,0:T(8,128)(2,1)S(1)}, bf16[128,1024]{1,0:T(8,128)(2,1)S(1)}, u32[]{:S(2)}, u32[]{:S(2)}) collective-permute-start(bf16[128,1024]{1,0:T(8,128)(2,1)S(1)} %copy-done.1), channel_id=1, source_target_pairs={{0,268},{4,264},{8,260},{12,256},{256,12},{260,8},{264,4},{268,0},... | collective-permute-start | bytes 786440 | tf_op jit(solution)/shard_map/ppermute | solution.py:345
  122.5 24.7 %collective-permute-start.3 = (bf16[144,1024]{1,0:T(8,128)(2,1)S(1)}, bf16[144,1024]{1,0:T(8,128)(2,1)S(1)}, u32[]{:S(2)}, u32[]{:S(2)}) collective-permute-start(bf16[144,1024]{1,0:T(8,128)(2,1)S(1)} %constant_dynamic-slice_fusion.1), channel_id=1, source_target_pairs={{0,256},{256,0},{1,257},{257,1},{2,258},{258,2},{3,259},{259,3},{4... | collective-permute-start | bytes 884744 | tf_op jit(solution)/shard_map/ppermute | solution.py:354
  147.3 21.6 %all-to-all-start.5 = ((bf16[32,8,1152]{2,1,0:T(8,128)(2,1)}), bf16[32,8,1152]{2,1,0:T(8,128)(2,1)S(1)}, u32[]{:S(2)}, u32[]{:S(2)}) async-start(bf16[32,8,1152]{2,1,0:T(8,128)(2,1)} %bitcast.9), calls=%async_computation.5 | async-start | bytes 1179648 | tf_op jit(solution)/shard_map/all_to_all | solution.py:310
  151.2 5.5 %collective-permute-start.4 = (bf16[48,1024]{1,0:T(8,128)(2,1)S(1)}, bf16[48,1024]{1,0:T(8,128)(2,1)S(1)}, u32[]{:S(2)}, u32[]{:S(2)}) collective-permute-start(bf16[48,1024]{1,0:T(8,128)(2,1)S(1)} %slice_select_fusion), channel_id=1, source_target_pairs={{0,32},{32,0},{64,96},{96,64},{128,160},{160,128},{192,224},{224,1... | collective-permute-start | bytes 294920 | tf_op jit(solution)/shard_map/ppermute | solution.py:359
  156.8 17.7 %collective-permute-start.5 = (bf16[192,1024]{1,0:T(8,128)(2,1)S(1)}, bf16[192,1024]{1,0:T(8,128)(2,1)S(1)}, u32[]{:S(2)}, u32[]{:S(2)}) collective-permute-start(bf16[192,1024]{1,0:T(8,128)(2,1)S(1)} %maximum_select_fusion), channel_id=1, source_target_pairs={{0,16},{16,0},{1,17},{17,1},{2,18},{18,2},{3,19},{19,3},{4,20},{20... | collective-permute-start | bytes 1179656 | tf_op jit(solution)/shard_map/ppermute | solution.py:368
  169.7 13.7 %all-to-all-start.6 = ((bf16[16,8,1024]{2,1,0:T(8,128)(2,1)}), bf16[16,8,1024]{2,1,0:T(8,128)(2,1)S(1)}, u32[]{:S(2)}, u32[]{:S(2)}) async-start(bf16[16,8,1024]{2,1,0:T(8,128)(2,1)} %shard_map.57), calls=%async_computation.6 | async-start | bytes 524288 | tf_op jit(solution)/shard_map/all_to_all | solution.py:310

commit v4 on v3

--- a/solution.py
+++ b/solution.py
@@ -13,6 +13,7 @@
 SWAP = [(0, 1), (1, 0)]
 D = 1024
 WIDE = 1152
+STEP = 256
 ROWS = 384
 OWN = 24
 PACK = 200
@@ -62,48 +63,53 @@
     return total[:, :D], count
 
 
-def scores_kernel(piece_t, points_a, points_b, piece, scores_a, scores_b, pairs, norm):
-    @pl.when(pl.program_id(0) == 0)
-    def _():
-        rows = piece_t[...].T
-        piece[...] = rows
-        wide = rows.astype(f32)
-        norm[...] = jnp.sum(wide * wide, axis=1, keepdims=True)
-
-    found = []
-    for points, scores in ((points_a, scores_a), (points_b, scores_b)):
-        product = lax.dot_general(piece[...], points[...], NT, preferred_element_type=f32)
-        s = (2.0 * product - norm[...]) / temper
-        scores[...] = s
-        peak = jnp.max(s, axis=0, keepdims=True)
-        found += [peak, jnp.sum(jnp.exp(s - peak), axis=0, keepdims=True)]
-    block = jnp.concatenate(found, axis=0)
-    for i in range(16):
-        pairs[i] = block
+def spread_kernel(columns, out):
+    for i in range(32):
+        out[i] = columns[:, (i % 2) * ROWS : (i % 2 + 1) * ROWS]
+
+
+def spread_halves(columns):
+    return pl.pallas_call(
+        spread_kernel,
+        in_specs=[VMEM],
+        out_specs=VMEM,
+        out_shape=jax.ShapeDtypeStruct((32, 32, ROWS), bf16),
+        compiler_params=params(),
+        cost_estimate=cost(0, 1 << 20),
+    )(columns)
+
+
+def scores_kernel(piece_t, points_a, points_b, piece, scores_a, scores_b, pairs):
+    rows = piece_t[...].T
+    piece[...] = rows
+    wide = rows.astype(f32)
+    norm = jnp.sum(wide * wide, axis=1, keepdims=True)
+    for i in range(1024 // STEP):
+        at = slice(i * STEP, (i + 1) * STEP)
+        found = []
+        for points, scores in ((points_a, scores_a), (points_b, scores_b)):
+            product = lax.dot_general(piece[...], points[at, :], NT, preferred_element_type=f32)
+            s = (2.0 * product - norm) * (1.0 / temper)
+            scores[:, at] = s
+            peak = jnp.max(s, axis=0, keepdims=True)
+            found += [peak, jnp.sum(jnp.exp(s - peak), axis=0, keepdims=True)]
+        block = jnp.concatenate(found, axis=0)
+        for j in range(16):
+            pairs[j, :, at] = block
 
 
 def level_one_scores(piece_t, points_a, points_b):
-    step = 256
-    points_spec = pl.BlockSpec((step, D), lambda i: (i, 0))
-    scores_spec = pl.BlockSpec((ROWS, step), lambda i: (0, i))
     return pl.pallas_call(
         scores_kernel,
-        grid=(1024 // step,),
-        in_specs=[pl.BlockSpec((D, ROWS), lambda i: (0, 0)), points_spec, points_spec],
-        out_specs=[
-            pl.BlockSpec((ROWS, D), lambda i: (0, 0)),
-            scores_spec,
-            scores_spec,
-            pl.BlockSpec((16, 4, step), lambda i: (0, 0, i)),
-        ],
+        in_specs=[VMEM] * 3,
+        out_specs=[VMEM] * 4,
         out_shape=[
             jax.ShapeDtypeStruct((ROWS, D), bf16),
             jax.ShapeDtypeStruct((ROWS, 1024), f32),
             jax.ShapeDtypeStruct((ROWS, 1024), f32),
             jax.ShapeDtypeStruct((16, 4, 1024), f32),
         ],
-        scratch_shapes=[pltpu.VMEM((ROWS, 1), f32)],
-        compiler_params=params(24),
+        compiler_params=params(16),
         cost_estimate=cost(2 * ROWS * 2048 * D, 8 << 20, ROWS * 2048),
     )(piece_t, points_a, points_b)
 
@@ -129,42 +135,35 @@
     )(pairs)
 
 
-def sums_kernel(mine, other, scores_a, scores_b, points_a, points_b, out, total, count):
-    @pl.when(pl.program_id(0) == 0)
-    def _():
-        total[...] = jnp.zeros_like(total)
-        count[...] = jnp.zeros_like(count)
-
-    for at, points, scores in ((0, points_a, scores_a), (2, points_b, scores_b)):
+def sums_kernel(mine, other, scores_a, scores_b, points_a, points_b, out, resp, total):
+    count = jnp.zeros((ROWS, 1), f32)
+    for at, scores in ((0, scores_a), (2, scores_b)):
         peak_m, total_m = mine[at : at + 1, :], mine[at + 1 : at + 2, :]
         peak_o, total_o = other[2 - at : 3 - at, :], other[3 - at : 4 - at, :]
         peak = jnp.maximum(peak_m, peak_o)
         whole = total_m * jnp.exp(peak_m - peak) + total_o * jnp.exp(peak_o - peak)
-        resp = (jnp.exp(scores[...] - peak) * (1.0 / whole)).astype(bf16)
-        total[...] += lax.dot_general(resp, points[...], NN, preferred_element_type=f32)
-        count[...] += jnp.sum(resp.astype(f32), axis=1, keepdims=True)
-
-    @pl.when(pl.program_id(0) == pl.num_programs(0) - 1)
-    def _():
-        for b in range(16):
-            at = slice(b * OWN, (b + 1) * OWN)
-            parts = [total[at, j * 128 : (j + 1) * 128] for j in range(8)]
-            tail = jnp.zeros((7, 128), f32)
-            out[b] = jnp.concatenate([*parts, count_row(count[at, :]), tail], axis=0).astype(bf16)
+        part = (jnp.exp(scores[...] - peak) * (1.0 / whole)).astype(bf16)
+        resp[at // 2] = part
+        count = count + jnp.sum(part.astype(f32), axis=1, keepdims=True)
+    for j in range(1024 // STEP):
+        at = slice(j * STEP, (j + 1) * STEP)
+        total[:, at] = lax.dot_general(
+            resp[0], points_a[:, at], NN, preferred_element_type=f32
+        ) + lax.dot_general(resp[1], points_b[:, at], NN, preferred_element_type=f32)
+    for b in range(16):
+        at = slice(b * OWN, (b + 1) * OWN)
+        parts = [total[at, j * 128 : (j + 1) * 128] for j in range(8)]
+        tail = jnp.zeros((7, 128), f32)
+        out[b] = jnp.concatenate([*parts, count_row(count[at, :]), tail], axis=0).astype(bf16)
 
 
 def level_one_sums(mine, other, scores_a, scores_b, points_a, points_b):
-    step = 512
-    pair_spec = pl.BlockSpec((4, step), lambda i: (0, i))
-    points_spec = pl.BlockSpec((step, D), lambda i: (i, 0))
-    scores_spec = pl.BlockSpec((ROWS, step), lambda i: (0, i))
     return pl.pallas_call(
         sums_kernel,
-        grid=(1024 // step,),
-        in_specs=[pair_spec, pair_spec, scores_spec, scores_spec, points_spec, points_spec],
-        out_specs=pl.BlockSpec((16, PACK, 128), lambda i: (0, 0, 0)),
+        in_specs=[VMEM] * 6,
+        out_specs=VMEM,
         out_shape=jax.ShapeDtypeStruct((16, PACK, 128), bf16),
-        scratch_shapes=[pltpu.VMEM((ROWS, D), f32), pltpu.VMEM((ROWS, 1), f32)],
+        scratch_shapes=[pltpu.VMEM((2, ROWS, 1024), bf16), pltpu.VMEM((ROWS, D), f32)],
         compiler_params=params(24),
         cost_estimate=cost(2 * ROWS * 2048 * D, 8 << 20, ROWS * 2048),
     )(mine, other, scores_a, scores_b, points_a, points_b)
@@ -325,9 +324,7 @@
     core_scalar = core.astype(jnp.int32)[None]
     y_scalar = y_hi.astype(jnp.int32)[None]
 
-    columns = centroids.T
-    target = lax.broadcasted_iota(jnp.int32, (32, 1, 1), 0) % 2
-    to_send = jnp.where(target == 0, columns[None, :, :ROWS], columns[None, :, ROWS:])
+    to_send = spread_halves(centroids.T)
     to_send, points = lax.optimization_barrier((to_send, points))
     piece_t = exchange(to_send, DP).reshape(D, ROWS)
     points_other = lax.ppermute(points, "core", SWAP)

time: 185 us -> 183 us (0.989)
  Pallas kernels: 10.9 us -> 8.86 us
    pallas_call x2 -> x3, Pallas kernels: 7.09 us -> 5.03 us  [the longest x1 2.68 us: level_one_sums(): pl.pallas_call(sums_kernel, in_specs=[VMEM] * 6, out_specs=VMEM, out_shap...]
where the time goes in v4:
time: 183 us; the launch traced here: 182 us
  blocking collectives  73.2 us (40%)
  starting transfers between devices  48.4 us (26%)
  waiting for transfers between devices  47.4 us (26%)
  Pallas kernels  8.86 us (5%)
    all_to_all x3, blocking collectives, exchange(): return lax.all_to_all(blocks, axes, 0, 0)  66.2 us
    all_to_all x4, waiting for transfers between devices, exchange(): return lax.all_to_all(blocks, axes, 0, 0)  42.8 us
    all_to_all x4, starting transfers between devices, exchange(): return lax.all_to_all(blocks, axes, 0, 0)  16.7 us
    ppermute x1, starting transfers between devices, on_device(): points_other = lax.ppermute(points, 'core', SWAP)  8.79 us
    ppermute x1, starting transfers between devices, on_device(): part = lax.ppermute(part, 'y_hi', SWAP)  7.45 us
    all_gather x1, blocking collectives, on_device(): fresh = lax.all_gather(mine, 'core')  7.08 us
    ppermute x1, starting transfers between devices, on_device(): groups_far = lax.ppermute(groups_ready, ('y_hi', 'y_lo'), MIRROR)  5.2 us
    ppermute x1, starting transfers between devices, on_device(): other = lax.ppermute(mine, 'core', SWAP)  4.95 us
  transfers between devices with their start and end apart: 10, of which 6 were waited for; matrix products, arithmetic and copies ran while one was open for 1% of the time, Pallas kernels for 1%

profile of v4, /device:TPU:1, one launch (start us, length us, event | category | flops | bytes accessed | tf_op | source)
XLA Modules:
  0.0 181.9 jit_solution(9366952549343463246)
XLA Ops:
  0.7 0.9 copy-done.2
  1.7 8.8 %collective-permute-start = (bf16[1024,1024]{1,0:T(8,128)(2,1)}, bf16[1024,1024]{1,0:T(8,128)(2,1)S(1)}, u32[]{:S(2)}, u32[]{:S(2)}) collective-permute-start(bf16[1024,1024]{1,0:T(8,128)(2,1)} %points_a.1), channel_id=1, source_target_pairs={{0,16},{16,0},{1,17},{17,1},{2,18},{18,2},{3,19},{19,3},{4,20},{20... | collective-permute-start | bytes 6291464 | tf_op jit(solution)/shard_map/ppermute | solution.py:330
  10.5 32.4 %all_to_all.35 = bf16[32,32,384]{2,1,0:T(8,128)(2,1)S(1)} all-to-all(bf16[32,32,384]{2,1,0:T(8,128)(2,1)S(1)} %shard_map.50), channel_id=1, replica_groups=mesh['y_hi'=2,'z'=8,'core'=2,'y_lo'=4,'x'=4] {'y_hi','z','core'}, dimensions={0} | all-to-all | bytes 1572864 | tf_op jit(solution)/shard_map/all_to_all | solution.py:309
  42.8 2.3 %shard_map.51 = (bf16[384,1024]{1,0:T(8,128)(2,1)S(1)}, f32[384,1024]{1,0:T(8,128)S(1)}, f32[384,1024]{1,0:T(8,128)S(1)}, f32[16,4,1024]{2,1,0:T(4,128)S(1)}) custom-call(bf16[1024,384]{1,0:T(8,128)(2,1)S(1)} %bitcast.21, bf16[1024,1024]{1,0:T(8,128)(2,1)S(1)} %copy-done, bf16[1024,1024]{1,0:T(8,128)(2,1)S(1)} %collective-permute-done.points_b), custom_call_target="tpu_custom_call" | custom-call | flops 1610612736 | bytes 8388608 | tf_op jit(solution)/shard_map/pallas_call | solution.py:102
  45.1 17.8 %all_to_all.36.pairs = f32[16,4,1024]{2,1,0:T(4,128)S(1)} all-to-all(f32[16,4,1024]{2,1,0:T(4,128)S(1)} %get-tuple-element.22), channel_id=1, replica_groups=mesh['y_hi'=2,'z'=8,'core'=2,'y_lo'=4,'x'=4] {'y_lo','x'}, dimensions={0} | all-to-all | bytes 524288 | tf_op jit(solution)/shard_map/all_to_all | solution.py:309
  62.9 0.1 shard_map.52.mine
  63.0 4.9 %collective-permute-start.1 = (f32[4,1024]{1,0:T(4,128)S(1)}, f32[4,1024]{1,0:T(4,128)S(1)}, u32[]{:S(2)}, u32[]{:S(2)}) collective-permute-start(f32[4,1024]{1,0:T(4,128)S(1)} %shard_map.52.mine), channel_id=1, source_target_pairs={{0,16},{16,0},{1,17},{17,1},{2,18},{18,2},{3,19},{19,3},{4,20},{20... | collective-permute-start | bytes 49160 | tf_op jit(solution)/shard_map/ppermute | solution.py:334
  68.0 0.8 collective-permute-done.1.other
  68.8 2.7 %shard_map.53 = bf16[16,200,128]{2,1,0:T(8,128)(2,1)} custom-call(f32[4,1024]{1,0:T(4,128)S(1)} %shard_map.52.mine, f32[4,1024]{1,0:T(4,128)S(1)} %collective-permute-done.1.other, f32[384,1024]{1,0:T(8,128)S(1)} %get-tuple-element.23.scores_a, f32[384,1024]{1,0:T(8,128)S(1)} %get-tuple-element.24.scores_b, bf16[1024,1024]{1,0:T(8,128)(2,1)S(1)} %copy-done, ...), custom_call_target="tpu_custom_call" | custom-call | flops 1610612736 | bytes 8388608 | tf_op jit(solution)/shard_map/pallas_call | solution.py:161
  71.5 3.8 %all-to-all-start.2 = ((bf16[16,200,128]{2,1,0:T(8,128)(2,1)}), bf16[16,200,128]{2,1,0:T(8,128)(2,1)S(1)}, u32[]{:S(2)}, u32[]{:S(2)}) async-start(bf16[16,200,128]{2,1,0:T(8,128)(2,1)} %shard_map.53), calls=%async_computation.2 | async-start | bytes 1638400 | tf_op jit(solution)/shard_map/all_to_all | solution.py:309
  75.3 21.4 %all-to-all-done.2.blocks = bf16[16,200,128]{2,1,0:T(8,128)(2,1)S(1)} async-done(((bf16[16,200,128]{2,1,0:T(8,128)(2,1)}), bf16[16,200,128]{2,1,0:T(8,128)(2,1)S(1)}, u32[]{:S(2)}, u32[]{:S(2)}) %all-to-all-start.2) | async-done | bytes 819232 | tf_op jit(solution)/shard_map/all_to_all | solution.py:309
  96.7 0.9 shard_map.54
  97.6 4.4 %all-to-all-start.3 = ((bf16[8,24,1024]{2,1,0:T(8,128)(2,1)}), bf16[8,24,1024]{2,1,0:T(8,128)(2,1)S(1)}, u32[]{:S(2)}, u32[]{:S(2)}) async-start(bf16[8,24,1024]{2,1,0:T(8,128)(2,1)} %get-tuple-element.27), calls=%async_computation.3 | async-start | bytes 786432 | tf_op jit(solution)/shard_map/all_to_all | solution.py:309
  101.9 5.2 %collective-permute-start.2 = (bf16[128,1024]{1,0:T(8,128)(2,1)S(1)}, bf16[128,1024]{1,0:T(8,128)(2,1)S(1)}, u32[]{:S(2)}, u32[]{:S(2)}) collective-permute-start(bf16[128,1024]{1,0:T(8,128)(2,1)S(1)} %copy-done.1), channel_id=1, source_target_pairs={{0,268},{4,264},{8,260},{12,256},{256,12},{260,8},{264,4},{268,0},... | collective-permute-start | bytes 786440 | tf_op jit(solution)/shard_map/ppermute | solution.py:342
  107.2 5.3 %all-to-all-done.3 = bf16[8,24,1024]{2,1,0:T(8,128)(2,1)S(1)} async-done(((bf16[8,24,1024]{2,1,0:T(8,128)(2,1)}), bf16[8,24,1024]{2,1,0:T(8,128)(2,1)S(1)}, u32[]{:S(2)}, u32[]{:S(2)}) %all-to-all-start.3) | async-done | bytes 393248 | tf_op jit(solution)/shard_map/all_to_all | solution.py:309
  112.5 7.1 %all_gather.3.fresh = bf16[2,192,1024]{2,1,0:T(8,128)(2,1)S(1)} all-gather(bf16[1,192,1024]{2,1,0:T(8,128)(2,1)S(1)} %bitcast.23), channel_id=1, replica_groups=mesh['y_hi'=2,'z'=8,'core'=2,'y_lo'=4,'x'=4] {'core'}, dimensions={0}, use_global_device_ids=true | all-gather | bytes 1179648 | tf_op jit(solution)/shard_map/all_gather | solution.py:343
  119.6 0.6 shard_map.55
  120.2 0.1 shard_map.56
  120.3 7.5 %collective-permute-start.3 = (bf16[144,1024]{1,0:T(8,128)(2,1)S(1)}, bf16[144,1024]{1,0:T(8,128)(2,1)S(1)}, u32[]{:S(2)}, u32[]{:S(2)}) collective-permute-start(bf16[144,1024]{1,0:T(8,128)(2,1)S(1)} %constant_dynamic-slice_fusion.1), channel_id=1, source_target_pairs={{0,256},{256,0},{1,257},{257,1},{2,258},{258,2},{3,259},{259,3},{4... | collective-permute-start | bytes 884744 | tf_op jit(solution)/shard_map/ppermute | solution.py:351
  127.8 16.0 %all_to_all.37.trios = f32[16,8,256]{2,1,0:T(8,128)S(1)} all-to-all(f32[16,8,256]{2,1,0:T(8,128)S(1)} %get-tuple-element.34), channel_id=1, replica_groups=mesh['y_hi'=2,'z'=8,'core'=2,'y_lo'=4,'x'=4] {'z','core'}, dimensions={0} | all-to-all | bytes 262144 | tf_op jit(solution)/shard_map/all_to_all | solution.py:309
  143.8 1.3 shard_map.57
  145.1 3.9 %all-to-all-start.5 = ((bf16[32,8,1152]{2,1,0:T(8,128)(2,1)}), bf16[32,8,1152]{2,1,0:T(8,128)(2,1)S(1)}, u32[]{:S(2)}, u32[]{:S(2)}) async-start(bf16[32,8,1152]{2,1,0:T(8,128)(2,1)} %bitcast.9), calls=%async_computation.5 | async-start | bytes 1179648 | tf_op jit(solution)/shard_map/all_to_all | solution.py:309
  149.0 2.0 %collective-permute-start.4 = (bf16[48,1024]{1,0:T(8,128)(2,1)S(1)}, bf16[48,1024]{1,0:T(8,128)(2,1)S(1)}, u32[]{:S(2)}, u32[]{:S(2)}) collective-permute-start(bf16[48,1024]{1,0:T(8,128)(2,1)S(1)} %slice_select_fusion), channel_id=1, source_target_pairs={{0,32},{32,0},{64,96},{96,64},{128,160},{160,128},{192,224},{224,1... | collective-permute-start | bytes 294920 | tf_op jit(solution)/shard_map/ppermute | solution.py:356
  151.0 3.7 %collective-permute-done.4 = bf16[48,1024]{1,0:T(8,128)(2,1)S(1)} collective-permute-done((bf16[48,1024]{1,0:T(8,128)(2,1)S(1)}, bf16[48,1024]{1,0:T(8,128)(2,1)S(1)}, u32[]{:S(2)}, u32[]{:S(2)}) %collective-permute-start.4) | collective-permute-done | bytes 98336 | tf_op jit(solution)/shard_map/ppermute | solution.py:356
  154.8 3.3 %collective-permute-start.5 = (bf16[192,1024]{1,0:T(8,128)(2,1)S(1)}, bf16[192,1024]{1,0:T(8,128)(2,1)S(1)}, u32[]{:S(2)}, u32[]{:S(2)}) collective-permute-start(bf16[192,1024]{1,0:T(8,128)(2,1)S(1)} %maximum_select_fusion), channel_id=1, source_target_pairs={{0,16},{16,0},{1,17},{17,1},{2,18},{18,2},{3,19},{19,3},{4,20},{20... | collective-permute-start | bytes 1179656 | tf_op jit(solution)/shard_map/ppermute | solution.py:365
  158.1 8.6 %all-to-all-done.5.blocks = bf16[32,8,1152]{2,1,0:T(8,128)(2,1)S(1)} async-done(((bf16[32,8,1152]{2,1,0:T(8,128)(2,1)}), bf16[32,8,1152]{2,1,0:T(8,128)(2,1)S(1)}, u32[]{:S(2)}, u32[]{:S(2)}) %all-to-all-start.5) | async-done | bytes 589856 | tf_op jit(solution)/shard_map/all_to_all | solution.py:309
  166.7 0.8 shard_map.58
  167.5 4.7 %all-to-all-start.6 = ((bf16[16,8,1024]{2,1,0:T(8,128)(2,1)}), bf16[16,8,1024]{2,1,0:T(8,128)(2,1)S(1)}, u32[]{:S(2)}, u32[]{:S(2)}) async-start(bf16[16,8,1024]{2,1,0:T(8,128)(2,1)} %shard_map.58), calls=%async_computation.6 | async-start | bytes 524288 | tf_op jit(solution)/shard_map/all_to_all | solution.py:309
  172.3 0.1 broadcast_select_fusion.5
  172.4 1.3 pad_maximum_fusion
  173.6 7.5 %all-to-all-done.6 = bf16[16,8,1024]{2,1,0:T(8,128)(2,1)S(1)} async-done(((bf16[16,8,1024]{2,1,0:T(8,128)(2,1)}), bf16[16,8,1024]{2,1,0:T(8,128)(2,1)S(1)}, u32[]{:S(2)}, u32[]{:S(2)}) %all-to-all-start.6) | async-done | bytes 262176 | tf_op jit(solution)/shard_map/all_to_all | solution.py:309
  181.2 0.7 copy.6
  (15 shorter events, 0.2 us)
Async XLA Ops:
  0.6 42.2 %copy-start = (bf16[1024,1024]{1,0:T(8,128)(2,1)S(1)}, bf16[1024,1024]{1,0:T(8,128)(2,1)}, u32[]{:S(2)}) copy-start(bf16[1024,1024]{1,0:T(8,128)(2,1)} %points_a.1) | copy-start | bytes 6291460
  0.6 0.9 copy-start.2
  1.7 41.2 %collective-permute-start = (bf16[1024,1024]{1,0:T(8,128)(2,1)}, bf16[1024,1024]{1,0:T(8,128)(2,1)S(1)}, u32[]{:S(2)}, u32[]{:S(2)}) collective-permute-start(bf16[1024,1024]{1,0:T(8,128)(2,1)} %points_a.1), channel_id=1, source_target_pairs={{0,16},{16,0},{1,17},{17,1},{2,18},{18,2},{3,19},{19,3},{4,20},{20... | collective-permute-start | bytes 6291464 | tf_op jit(solution)/shard_map/ppermute | solution.py:330
  63.0 5.8 %collective-permute-start.1 = (f32[4,1024]{1,0:T(4,128)S(1)}, f32[4,1024]{1,0:T(4,128)S(1)}, u32[]{:S(2)}, u32[]{:S(2)}) collective-permute-start(f32[4,1024]{1,0:T(4,128)S(1)} %shard_map.52.mine), channel_id=1, source_target_pairs={{0,16},{16,0},{1,17},{17,1},{2,18},{18,2},{3,19},{19,3},{4,20},{20... | collective-permute-start | bytes 49160 | tf_op jit(solution)/shard_map/ppermute | solution.py:334
  71.5 30.5 %copy-start.1 = (bf16[128,1024]{1,0:T(8,128)(2,1)S(1)}, bf16[128,1024]{1,0:T(8,128)(2,1)}, u32[]{:S(2)}) copy-start(bf16[128,1024]{1,0:T(8,128)(2,1)} %near.1) | copy-start | bytes 786436
  71.5 25.2 %all-to-all-start.2 = ((bf16[16,200,128]{2,1,0:T(8,128)(2,1)}), bf16[16,200,128]{2,1,0:T(8,128)(2,1)S(1)}, u32[]{:S(2)}, u32[]{:S(2)}) async-start(bf16[16,200,128]{2,1,0:T(8,128)(2,1)} %shard_map.53), calls=%async_computation.2 | async-start | bytes 1638400 | tf_op jit(solution)/shard_map/all_to_all | solution.py:309
  97.6 14.9 %all-to-all-start.3 = ((bf16[8,24,1024]{2,1,0:T(8,128)(2,1)}), bf16[8,24,1024]{2,1,0:T(8,128)(2,1)S(1)}, u32[]{:S(2)}, u32[]{:S(2)}) async-start(bf16[8,24,1024]{2,1,0:T(8,128)(2,1)} %get-tuple-element.27), calls=%async_computation.3 | async-start | bytes 786432 | tf_op jit(solution)/shard_map/all_to_all | solution.py:309
  101.9 17.6 %collective-permute-start.2 = (bf16[128,1024]{1,0:T(8,128)(2,1)S(1)}, bf16[128,1024]{1,0:T(8,128)(2,1)S(1)}, u32[]{:S(2)}, u32[]{:S(2)}) collective-permute-start(bf16[128,1024]{1,0:T(8,128)(2,1)S(1)} %copy-done.1), channel_id=1, source_target_pairs={{0,268},{4,264},{8,260},{12,256},{256,12},{260,8},{264,4},{268,0},... | collective-permute-start | bytes 786440 | tf_op jit(solution)/shard_map/ppermute | solution.py:342
  120.3 24.7 %collective-permute-start.3 = (bf16[144,1024]{1,0:T(8,128)(2,1)S(1)}, bf16[144,1024]{1,0:T(8,128)(2,1)S(1)}, u32[]{:S(2)}, u32[]{:S(2)}) collective-permute-start(bf16[144,1024]{1,0:T(8,128)(2,1)S(1)} %constant_dynamic-slice_fusion.1), channel_id=1, source_target_pairs={{0,256},{256,0},{1,257},{257,1},{2,258},{258,2},{3,259},{259,3},{4... | collective-permute-start | bytes 884744 | tf_op jit(solution)/shard_map/ppermute | solution.py:351
  145.1 21.6 %all-to-all-start.5 = ((bf16[32,8,1152]{2,1,0:T(8,128)(2,1)}), bf16[32,8,1152]{2,1,0:T(8,128)(2,1)S(1)}, u32[]{:S(2)}, u32[]{:S(2)}) async-start(bf16[32,8,1152]{2,1,0:T(8,128)(2,1)} %bitcast.9), calls=%async_computation.5 | async-start | bytes 1179648 | tf_op jit(solution)/shard_map/all_to_all | solution.py:309
  149.0 5.7 %collective-permute-start.4 = (bf16[48,1024]{1,0:T(8,128)(2,1)S(1)}, bf16[48,1024]{1,0:T(8,128)(2,1)S(1)}, u32[]{:S(2)}, u32[]{:S(2)}) collective-permute-start(bf16[48,1024]{1,0:T(8,128)(2,1)S(1)} %slice_select_fusion), channel_id=1, source_target_pairs={{0,32},{32,0},{64,96},{96,64},{128,160},{160,128},{192,224},{224,1... | collective-permute-start | bytes 294920 | tf_op jit(solution)/shard_map/ppermute | solution.py:356
  154.8 17.5 %collective-permute-start.5 = (bf16[192,1024]{1,0:T(8,128)(2,1)S(1)}, bf16[192,1024]{1,0:T(8,128)(2,1)S(1)}, u32[]{:S(2)}, u32[]{:S(2)}) collective-permute-start(bf16[192,1024]{1,0:T(8,128)(2,1)S(1)} %maximum_select_fusion), channel_id=1, source_target_pairs={{0,16},{16,0},{1,17},{17,1},{2,18},{18,2},{3,19},{19,3},{4,20},{20... | collective-permute-start | bytes 1179656 | tf_op jit(solution)/shard_map/ppermute | solution.py:365
  167.5 13.7 %all-to-all-start.6 = ((bf16[16,8,1024]{2,1,0:T(8,128)(2,1)}), bf16[16,8,1024]{2,1,0:T(8,128)(2,1)S(1)}, u32[]{:S(2)}, u32[]{:S(2)}) async-start(bf16[16,8,1024]{2,1,0:T(8,128)(2,1)} %shard_map.58), calls=%async_computation.6 | async-start | bytes 524288 | tf_op jit(solution)/shard_map/all_to_all | solution.py:309

commit v5 on v4

--- a/solution.py
+++ b/solution.py
@@ -10,6 +10,7 @@
 DP = ("y_hi", "z", "core")
 CHIPS = ("y_hi", "z")
 CENT = ("y_lo", "x")
+NEAR = ("x", "y_lo")
 SWAP = [(0, 1), (1, 0)]
 D = 1024
 WIDE = 1152
@@ -272,8 +273,10 @@
         count = count + jnp.sum(weighted.astype(f32), axis=1, keepdims=True)
     lanes = count_lanes(count)
     for place, at in ((y_hi[0], 0), (1 - y_hi[0], 128)):
-        out[place, :, :D] = sums[at : at + 128].astype(bf16)
-        out[place, :, D:] = lanes[at : at + 128]
+        for i in range(16):
+            block = slice(at + i * 8, at + i * 8 + 8)
+            out[i, place, :, :D] = sums[block].astype(bf16)
+            out[i, place, :, D:] = lanes[block]
 
 
 def level_two_sums(y_hi, expo, here, trios, fresh):
@@ -281,7 +284,7 @@
         group_sums_kernel,
         in_specs=[SMEM] + [VMEM] * 4,
         out_specs=VMEM,
-        out_shape=jax.ShapeDtypeStruct((2, 128, WIDE), bf16),
+        out_shape=jax.ShapeDtypeStruct((16, 2, 8, WIDE), bf16),
         compiler_params=params(),
         cost_estimate=cost(2 * ROWS * 256 * D, 2 << 20, ROWS * 256),
     )(y_hi, expo, here, trios, fresh)
@@ -320,7 +323,7 @@
     core = lax.axis_index("core")
     y_hi = lax.axis_index("y_hi")
     z = lax.axis_index("z")
-    cent = lax.axis_index(CENT)
+    cent = lax.axis_index(NEAR)
     core_scalar = core.astype(jnp.int32)[None]
     y_scalar = y_hi.astype(jnp.int32)[None]
 
@@ -330,7 +333,7 @@
     points_other = lax.ppermute(points, "core", SWAP)
 
     piece, scores_a, scores_b, pairs = level_one_scores(piece_t, points, points_other)
-    mine = combine(exchange(pairs, CENT))
+    mine = combine(exchange(pairs, NEAR))
     other = lax.ppermute(mine, "core", SWAP)
     blocks = level_one_sums(mine, other, scores_a, scores_b, points, points_other)
     blocks = exchange(blocks, CHIPS)
@@ -349,7 +352,7 @@
     expo, mine = lax.optimization_barrier((expo, mine))
     part = lax.dynamic_slice_in_dim(mine, odd * rest, FAR, axis=0)
     part = lax.ppermute(part, "y_hi", SWAP)
-    trios = exchange(trios, ("z", "core"))
+    trios = exchange(trios, ("core", "z"))
     sums = level_two_sums(y_scalar, expo, here, trios, fresh)
     sums, part = lax.optimization_barrier((sums, part))
     lacking = jnp.where(odd == 0, part[:rest], part[FAR - rest :])
@@ -359,11 +362,11 @@
         jnp.concatenate([part, lacking], axis=0),
         jnp.concatenate([lacking, part], axis=0),
     )
-    blocks = exchange(sums.reshape(32, 8, WIDE), ("y_hi", *CENT))
+    blocks = exchange(sums.reshape(32, 8, WIDE), (*NEAR, "y_hi"))
     rows = lax.dynamic_slice_in_dim(groups, cent * 8, 8, axis=0)
     new_rows = finish_groups(blocks, rows)
     far_other = lax.ppermute(far_mine, "core", SWAP)
-    new_groups = exchange(new_rows, CENT).reshape(128, D)
+    new_groups = exchange(new_rows, NEAR).reshape(128, D)
 
     far = ordered(core, far_mine, far_other)
     first, second = ordered(y_hi, fresh[0], far[0]), ordered(y_hi, fresh[1], far[1])

time: 183 us -> 181 us (0.989)
  blocking collectives: 73.2 us -> 69.4 us
    all_to_all x3, blocking collectives: 66.2 us -> 64 us  [exchange(): return lax.all_to_all(blocks, axes, 0, 0)]
    ppermute x1, starting transfers between devices: 5.2 us -> 3.01 us  [on_device(): groups_far = lax.ppermute(groups_ready, ('y_hi', 'y_lo'), MIRROR)]
    ppermute x1, starting transfers between devices: 7.45 us -> 5.28 us  [on_device(): part = lax.ppermute(part, 'y_hi', SWAP)]
    all_to_all x4, starting transfers between devices: 16.7 us -> 18.6 us  [exchange(): return lax.all_to_all(blocks, axes, 0, 0)]
where the time goes in v5:
time: 181 us; the launch traced here: 178 us
  blocking collectives  69.4 us (38%)
  starting transfers between devices  48.3 us (27%)
  waiting for transfers between devices  47.8 us (26%)
  Pallas kernels  8.86 us (5%)
    all_to_all x3, blocking collectives, exchange(): return lax.all_to_all(blocks, axes, 0, 0)  64 us
    all_to_all x4, waiting for transfers between devices, exchange(): return lax.all_to_all(blocks, axes, 0, 0)  44 us
    all_to_all x4, starting transfers between devices, exchange(): return lax.all_to_all(blocks, axes, 0, 0)  18.6 us
    ppermute x1, starting transfers between devices, on_device(): points_other = lax.ppermute(points, 'core', SWAP)  8.79 us
    all_gather x1, blocking collectives, on_device(): fresh = lax.all_gather(mine, 'core')  5.46 us
    ppermute x1, starting transfers between devices, on_device(): part = lax.ppermute(part, 'y_hi', SWAP)  5.28 us
    ppermute x1, starting transfers between devices, on_device(): other = lax.ppermute(mine, 'core', SWAP)  5.25 us
    ppermute x1, starting transfers between devices, on_device(): far_other = lax.ppermute(far_mine, 'core', SWAP)  4.99 us
  transfers between devices with their start and end apart: 10, of which 6 were waited for; matrix products, arithmetic and copies ran while one was open for 1% of the time, Pallas kernels for 1%

profile of v5, /device:TPU:1, one launch (start us, length us, event | category | flops | bytes accessed | tf_op | source)
XLA Modules:
  0.0 178.4 jit_solution(3379896092736685782)
XLA Ops:
  0.7 0.9 copy-done.2
  1.7 8.8 %collective-permute-start = (bf16[1024,1024]{1,0:T(8,128)(2,1)}, bf16[1024,1024]{1,0:T(8,128)(2,1)S(1)}, u32[]{:S(2)}, u32[]{:S(2)}) collective-permute-start(bf16[1024,1024]{1,0:T(8,128)(2,1)} %points_a.1), channel_id=1, source_target_pairs={{0,16},{16,0},{1,17},{17,1},{2,18},{18,2},{3,19},{19,3},{4,20},{20... | collective-permute-start | bytes 6291464 | tf_op jit(solution)/shard_map/ppermute | solution.py:333
  10.5 32.4 %all_to_all.35 = bf16[32,32,384]{2,1,0:T(8,128)(2,1)S(1)} all-to-all(bf16[32,32,384]{2,1,0:T(8,128)(2,1)S(1)} %shard_map.50), channel_id=1, replica_groups=mesh['y_hi'=2,'z'=8,'core'=2,'y_lo'=4,'x'=4] {'y_hi','z','core'}, dimensions={0} | all-to-all | bytes 1572864 | tf_op jit(solution)/shard_map/all_to_all | solution.py:312
  42.8 2.3 %shard_map.51 = (bf16[384,1024]{1,0:T(8,128)(2,1)S(1)}, f32[384,1024]{1,0:T(8,128)S(1)}, f32[384,1024]{1,0:T(8,128)S(1)}, f32[16,4,1024]{2,1,0:T(4,128)S(1)}) custom-call(bf16[1024,384]{1,0:T(8,128)(2,1)S(1)} %bitcast.21, bf16[1024,1024]{1,0:T(8,128)(2,1)S(1)} %copy-done, bf16[1024,1024]{1,0:T(8,128)(2,1)S(1)} %collective-permute-done.points_b), custom_call_target="tpu_custom_call" | custom-call | flops 1610612736 | bytes 8388608 | tf_op jit(solution)/shard_map/pallas_call | solution.py:103
  45.1 17.5 %all_to_all.36.pairs = f32[16,4,1024]{2,1,0:T(4,128)S(1)} all-to-all(f32[16,4,1024]{2,1,0:T(4,128)S(1)} %get-tuple-element.22), channel_id=1, replica_groups=mesh['y_hi'=2,'z'=8,'core'=2,'y_lo'=4,'x'=4] {'x','y_lo'}, dimensions={0} | all-to-all | bytes 524288 | tf_op jit(solution)/shard_map/all_to_all | solution.py:312
  62.6 0.1 shard_map.52.mine
  62.7 5.2 %collective-permute-start.1 = (f32[4,1024]{1,0:T(4,128)S(1)}, f32[4,1024]{1,0:T(4,128)S(1)}, u32[]{:S(2)}, u32[]{:S(2)}) collective-permute-start(f32[4,1024]{1,0:T(4,128)S(1)} %shard_map.52.mine), channel_id=1, source_target_pairs={{0,16},{16,0},{1,17},{17,1},{2,18},{18,2},{3,19},{19,3},{4,20},{20... | collective-permute-start | bytes 49160 | tf_op jit(solution)/shard_map/ppermute | solution.py:337
  67.9 0.8 collective-permute-done.1.other
  68.8 2.7 %shard_map.53 = bf16[16,200,128]{2,1,0:T(8,128)(2,1)} custom-call(f32[4,1024]{1,0:T(4,128)S(1)} %shard_map.52.mine, f32[4,1024]{1,0:T(4,128)S(1)} %collective-permute-done.1.other, f32[384,1024]{1,0:T(8,128)S(1)} %get-tuple-element.23.scores_a, f32[384,1024]{1,0:T(8,128)S(1)} %get-tuple-element.24.scores_b, bf16[1024,1024]{1,0:T(8,128)(2,1)S(1)} %copy-done, ...), custom_call_target="tpu_custom_call" | custom-call | flops 1610612736 | bytes 8388608 | tf_op jit(solution)/shard_map/pallas_call | solution.py:162
  71.4 3.8 %all-to-all-start.2 = ((bf16[16,200,128]{2,1,0:T(8,128)(2,1)}), bf16[16,200,128]{2,1,0:T(8,128)(2,1)S(1)}, u32[]{:S(2)}, u32[]{:S(2)}) async-start(bf16[16,200,128]{2,1,0:T(8,128)(2,1)} %shard_map.53), calls=%async_computation.2 | async-start | bytes 1638400 | tf_op jit(solution)/shard_map/all_to_all | solution.py:312
  75.2 22.0 %all-to-all-done.2.blocks = bf16[16,200,128]{2,1,0:T(8,128)(2,1)S(1)} async-done(((bf16[16,200,128]{2,1,0:T(8,128)(2,1)}), bf16[16,200,128]{2,1,0:T(8,128)(2,1)S(1)}, u32[]{:S(2)}, u32[]{:S(2)}) %all-to-all-start.2) | async-done | bytes 819232 | tf_op jit(solution)/shard_map/all_to_all | solution.py:312
  97.3 0.9 shard_map.54
  98.2 5.5 %all-to-all-start.3 = ((bf16[8,24,1024]{2,1,0:T(8,128)(2,1)}), bf16[8,24,1024]{2,1,0:T(8,128)(2,1)S(1)}, u32[]{:S(2)}, u32[]{:S(2)}) async-start(bf16[8,24,1024]{2,1,0:T(8,128)(2,1)} %get-tuple-element.27), calls=%async_computation.3 | async-start | bytes 786432 | tf_op jit(solution)/shard_map/all_to_all | solution.py:312
  103.7 3.0 %collective-permute-start.2 = (bf16[128,1024]{1,0:T(8,128)(2,1)S(1)}, bf16[128,1024]{1,0:T(8,128)(2,1)S(1)}, u32[]{:S(2)}, u32[]{:S(2)}) collective-permute-start(bf16[128,1024]{1,0:T(8,128)(2,1)S(1)} %copy-done.1), channel_id=1, source_target_pairs={{0,268},{4,264},{8,260},{12,256},{256,12},{260,8},{264,4},{268,0},... | collective-permute-start | bytes 786440 | tf_op jit(solution)/shard_map/ppermute | solution.py:345
  106.7 9.1 %all-to-all-done.3 = bf16[8,24,1024]{2,1,0:T(8,128)(2,1)S(1)} async-done(((bf16[8,24,1024]{2,1,0:T(8,128)(2,1)}), bf16[8,24,1024]{2,1,0:T(8,128)(2,1)S(1)}, u32[]{:S(2)}, u32[]{:S(2)}) %all-to-all-start.3) | async-done | bytes 393248 | tf_op jit(solution)/shard_map/all_to_all | solution.py:312
  115.9 5.5 %all_gather.3.fresh = bf16[2,192,1024]{2,1,0:T(8,128)(2,1)S(1)} all-gather(bf16[1,192,1024]{2,1,0:T(8,128)(2,1)S(1)} %bitcast.23), channel_id=1, replica_groups=mesh['y_hi'=2,'z'=8,'core'=2,'y_lo'=4,'x'=4] {'core'}, dimensions={0}, use_global_device_ids=true | all-gather | bytes 1179648 | tf_op jit(solution)/shard_map/all_gather | solution.py:346
  121.3 0.6 shard_map.55
  121.9 0.1 shard_map.56
  122.1 5.3 %collective-permute-start.3 = (bf16[144,1024]{1,0:T(8,128)(2,1)S(1)}, bf16[144,1024]{1,0:T(8,128)(2,1)S(1)}, u32[]{:S(2)}, u32[]{:S(2)}) collective-permute-start(bf16[144,1024]{1,0:T(8,128)(2,1)S(1)} %constant_dynamic-slice_fusion.1), channel_id=1, source_target_pairs={{0,256},{256,0},{1,257},{257,1},{2,258},{258,2},{3,259},{259,3},{4... | collective-permute-start | bytes 884744 | tf_op jit(solution)/shard_map/ppermute | solution.py:354
  127.4 14.1 %all_to_all.37.trios = f32[16,8,256]{2,1,0:T(8,128)S(1)} all-to-all(f32[16,8,256]{2,1,0:T(8,128)S(1)} %get-tuple-element.34), channel_id=1, replica_groups=mesh['y_hi'=2,'z'=8,'core'=2,'y_lo'=4,'x'=4] {'core','z'}, dimensions={0} | all-to-all | bytes 262144 | tf_op jit(solution)/shard_map/all_to_all | solution.py:312
  141.5 1.3 shard_map.57
  142.8 4.9 %all-to-all-start.5 = ((bf16[32,8,1152]{2,1,0:T(8,128)(2,1)}), bf16[32,8,1152]{2,1,0:T(8,128)(2,1)S(1)}, u32[]{:S(2)}, u32[]{:S(2)}) async-start(bf16[32,8,1152]{2,1,0:T(8,128)(2,1)} %bitcast.9), calls=%async_computation.5 | async-start | bytes 1179648 | tf_op jit(solution)/shard_map/all_to_all | solution.py:312
  147.8 2.4 %collective-permute-start.4 = (bf16[48,1024]{1,0:T(8,128)(2,1)S(1)}, bf16[48,1024]{1,0:T(8,128)(2,1)S(1)}, u32[]{:S(2)}, u32[]{:S(2)}) collective-permute-start(bf16[48,1024]{1,0:T(8,128)(2,1)S(1)} %slice_select_fusion), channel_id=1, source_target_pairs={{0,32},{32,0},{64,96},{96,64},{128,160},{160,128},{192,224},{224,1... | collective-permute-start | bytes 294920 | tf_op jit(solution)/shard_map/ppermute | solution.py:359
  150.1 3.0 %collective-permute-done.4 = bf16[48,1024]{1,0:T(8,128)(2,1)S(1)} collective-permute-done((bf16[48,1024]{1,0:T(8,128)(2,1)S(1)}, bf16[48,1024]{1,0:T(8,128)(2,1)S(1)}, u32[]{:S(2)}, u32[]{:S(2)}) %collective-permute-start.4) | collective-permute-done | bytes 98336 | tf_op jit(solution)/shard_map/ppermute | solution.py:359
  153.2 5.0 %collective-permute-start.5 = (bf16[192,1024]{1,0:T(8,128)(2,1)S(1)}, bf16[192,1024]{1,0:T(8,128)(2,1)S(1)}, u32[]{:S(2)}, u32[]{:S(2)}) collective-permute-start(bf16[192,1024]{1,0:T(8,128)(2,1)S(1)} %maximum_select_fusion), channel_id=1, source_target_pairs={{0,16},{16,0},{1,17},{17,1},{2,18},{18,2},{3,19},{19,3},{4,20},{20... | collective-permute-start | bytes 1179656 | tf_op jit(solution)/shard_map/ppermute | solution.py:368
  158.2 6.2 %all-to-all-done.5.blocks = bf16[32,8,1152]{2,1,0:T(8,128)(2,1)S(1)} async-done(((bf16[32,8,1152]{2,1,0:T(8,128)(2,1)}), bf16[32,8,1152]{2,1,0:T(8,128)(2,1)S(1)}, u32[]{:S(2)}, u32[]{:S(2)}) %all-to-all-start.5) | async-done | bytes 589856 | tf_op jit(solution)/shard_map/all_to_all | solution.py:312
  164.5 0.8 shard_map.58
  165.3 4.4 %all-to-all-start.6 = ((bf16[16,8,1024]{2,1,0:T(8,128)(2,1)}), bf16[16,8,1024]{2,1,0:T(8,128)(2,1)S(1)}, u32[]{:S(2)}, u32[]{:S(2)}) async-start(bf16[16,8,1024]{2,1,0:T(8,128)(2,1)} %shard_map.58), calls=%async_computation.6 | async-start | bytes 524288 | tf_op jit(solution)/shard_map/all_to_all | solution.py:312
  169.7 0.1 broadcast_select_fusion.5
  169.8 1.3 pad_maximum_fusion
  171.1 6.6 %all-to-all-done.6 = bf16[16,8,1024]{2,1,0:T(8,128)(2,1)S(1)} async-done(((bf16[16,8,1024]{2,1,0:T(8,128)(2,1)}), bf16[16,8,1024]{2,1,0:T(8,128)(2,1)S(1)}, u32[]{:S(2)}, u32[]{:S(2)}) %all-to-all-start.6) | async-done | bytes 262176 | tf_op jit(solution)/shard_map/all_to_all | solution.py:312
  177.7 0.7 copy.6
  (15 shorter events, 0.2 us)
Async XLA Ops:
  0.6 42.2 %copy-start = (bf16[1024,1024]{1,0:T(8,128)(2,1)S(1)}, bf16[1024,1024]{1,0:T(8,128)(2,1)}, u32[]{:S(2)}) copy-start(bf16[1024,1024]{1,0:T(8,128)(2,1)} %points_a.1) | copy-start | bytes 6291460
  0.6 0.9 copy-start.2
  1.7 41.2 %collective-permute-start = (bf16[1024,1024]{1,0:T(8,128)(2,1)}, bf16[1024,1024]{1,0:T(8,128)(2,1)S(1)}, u32[]{:S(2)}, u32[]{:S(2)}) collective-permute-start(bf16[1024,1024]{1,0:T(8,128)(2,1)} %points_a.1), channel_id=1, source_target_pairs={{0,16},{16,0},{1,17},{17,1},{2,18},{18,2},{3,19},{19,3},{4,20},{20... | collective-permute-start | bytes 6291464 | tf_op jit(solution)/shard_map/ppermute | solution.py:333
  62.7 6.1 %collective-permute-start.1 = (f32[4,1024]{1,0:T(4,128)S(1)}, f32[4,1024]{1,0:T(4,128)S(1)}, u32[]{:S(2)}, u32[]{:S(2)}) collective-permute-start(f32[4,1024]{1,0:T(4,128)S(1)} %shard_map.52.mine), channel_id=1, source_target_pairs={{0,16},{16,0},{1,17},{17,1},{2,18},{18,2},{3,19},{19,3},{4,20},{20... | collective-permute-start | bytes 49160 | tf_op jit(solution)/shard_map/ppermute | solution.py:337
  71.4 32.3 %copy-start.1 = (bf16[128,1024]{1,0:T(8,128)(2,1)S(1)}, bf16[128,1024]{1,0:T(8,128)(2,1)}, u32[]{:S(2)}) copy-start(bf16[128,1024]{1,0:T(8,128)(2,1)} %near.1) | copy-start | bytes 786436
  71.4 25.8 %all-to-all-start.2 = ((bf16[16,200,128]{2,1,0:T(8,128)(2,1)}), bf16[16,200,128]{2,1,0:T(8,128)(2,1)S(1)}, u32[]{:S(2)}, u32[]{:S(2)}) async-start(bf16[16,200,128]{2,1,0:T(8,128)(2,1)} %shard_map.53), calls=%async_computation.2 | async-start | bytes 1638400 | tf_op jit(solution)/shard_map/all_to_all | solution.py:312
  98.2 17.7 %all-to-all-start.3 = ((bf16[8,24,1024]{2,1,0:T(8,128)(2,1)}), bf16[8,24,1024]{2,1,0:T(8,128)(2,1)S(1)}, u32[]{:S(2)}, u32[]{:S(2)}) async-start(bf16[8,24,1024]{2,1,0:T(8,128)(2,1)} %get-tuple-element.27), calls=%async_computation.3 | async-start | bytes 786432 | tf_op jit(solution)/shard_map/all_to_all | solution.py:312
  103.7 17.6 %collective-permute-start.2 = (bf16[128,1024]{1,0:T(8,128)(2,1)S(1)}, bf16[128,1024]{1,0:T(8,128)(2,1)S(1)}, u32[]{:S(2)}, u32[]{:S(2)}) collective-permute-start(bf16[128,1024]{1,0:T(8,128)(2,1)S(1)} %copy-done.1), channel_id=1, source_target_pairs={{0,268},{4,264},{8,260},{12,256},{256,12},{260,8},{264,4},{268,0},... | collective-permute-start | bytes 786440 | tf_op jit(solution)/shard_map/ppermute | solution.py:345
  122.1 20.7 %collective-permute-start.3 = (bf16[144,1024]{1,0:T(8,128)(2,1)S(1)}, bf16[144,1024]{1,0:T(8,128)(2,1)S(1)}, u32[]{:S(2)}, u32[]{:S(2)}) collective-permute-start(bf16[144,1024]{1,0:T(8,128)(2,1)S(1)} %constant_dynamic-slice_fusion.1), channel_id=1, source_target_pairs={{0,256},{256,0},{1,257},{257,1},{2,258},{258,2},{3,259},{259,3},{4... | collective-permute-start | bytes 884744 | tf_op jit(solution)/shard_map/ppermute | solution.py:354
  142.8 21.7 %all-to-all-start.5 = ((bf16[32,8,1152]{2,1,0:T(8,128)(2,1)}), bf16[32,8,1152]{2,1,0:T(8,128)(2,1)S(1)}, u32[]{:S(2)}, u32[]{:S(2)}) async-start(bf16[32,8,1152]{2,1,0:T(8,128)(2,1)} %bitcast.9), calls=%async_computation.5 | async-start | bytes 1179648 | tf_op jit(solution)/shard_map/all_to_all | solution.py:312
  147.8 5.4 %collective-permute-start.4 = (bf16[48,1024]{1,0:T(8,128)(2,1)S(1)}, bf16[48,1024]{1,0:T(8,128)(2,1)S(1)}, u32[]{:S(2)}, u32[]{:S(2)}) collective-permute-start(bf16[48,1024]{1,0:T(8,128)(2,1)S(1)} %slice_select_fusion), channel_id=1, source_target_pairs={{0,32},{32,0},{64,96},{96,64},{128,160},{160,128},{192,224},{224,1... | collective-permute-start | bytes 294920 | tf_op jit(solution)/shard_map/ppermute | solution.py:359
  153.2 16.5 %collective-permute-start.5 = (bf16[192,1024]{1,0:T(8,128)(2,1)S(1)}, bf16[192,1024]{1,0:T(8,128)(2,1)S(1)}, u32[]{:S(2)}, u32[]{:S(2)}) collective-permute-start(bf16[192,1024]{1,0:T(8,128)(2,1)S(1)} %maximum_select_fusion), channel_id=1, source_target_pairs={{0,16},{16,0},{1,17},{17,1},{2,18},{18,2},{3,19},{19,3},{4,20},{20... | collective-permute-start | bytes 1179656 | tf_op jit(solution)/shard_map/ppermute | solution.py:368
  165.3 12.4 %all-to-all-start.6 = ((bf16[16,8,1024]{2,1,0:T(8,128)(2,1)}), bf16[16,8,1024]{2,1,0:T(8,128)(2,1)S(1)}, u32[]{:S(2)}, u32[]{:S(2)}) async-start(bf16[16,8,1024]{2,1,0:T(8,128)(2,1)} %shard_map.58), calls=%async_computation.6 | async-start | bytes 524288 | tf_op jit(solution)/shard_map/all_to_all | solution.py:312

commit v6 on v5

--- a/solution.py
+++ b/solution.py
@@ -138,19 +138,21 @@
 
 def sums_kernel(mine, other, scores_a, scores_b, points_a, points_b, out, resp, total):
     count = jnp.zeros((ROWS, 1), f32)
-    for at, scores in ((0, scores_a), (2, scores_b)):
+    for place, scores, points in ((0, scores_a, points_a), (1, scores_b, points_b)):
+        at = 2 * place
         peak_m, total_m = mine[at : at + 1, :], mine[at + 1 : at + 2, :]
         peak_o, total_o = other[2 - at : 3 - at, :], other[3 - at : 4 - at, :]
         peak = jnp.maximum(peak_m, peak_o)
         whole = total_m * jnp.exp(peak_m - peak) + total_o * jnp.exp(peak_o - peak)
         part = (jnp.exp(scores[...] - peak) * (1.0 / whole)).astype(bf16)
-        resp[at // 2] = part
+        resp[place] = part
         count = count + jnp.sum(part.astype(f32), axis=1, keepdims=True)
-    for j in range(1024 // STEP):
-        at = slice(j * STEP, (j + 1) * STEP)
-        total[:, at] = lax.dot_general(
-            resp[0], points_a[:, at], NN, preferred_element_type=f32
-        ) + lax.dot_general(resp[1], points_b[:, at], NN, preferred_element_type=f32)
+        for j in range(1024 // STEP):
+            cols = slice(j * STEP, (j + 1) * STEP)
+            sums = lax.dot_general(
+                resp[place], points[:, cols], NN, preferred_element_type=f32
+            )
+            total[:, cols] = total[:, cols] + sums if place else sums
     for b in range(16):
         at = slice(b * OWN, (b + 1) * OWN)
         parts = [total[at, j * 128 : (j + 1) * 128] for j in range(8)]
@@ -202,7 +204,7 @@
     )(z, blocks, rows)
 
 
-def group_scores_kernel(core, fresh, near, far, counts, scores, trios):
+def group_scores_kernel(core, fresh, near, far, counts, expo, peaks, trios):
     groups = jnp.concatenate([near[...], far[...]], axis=0)
     wide = groups.astype(f32)
     norm = jnp.sum(wide * wide, axis=1, keepdims=True)
@@ -211,9 +213,10 @@
     for c in range(2):
         product = lax.dot_general(groups, fresh[c], NT, preferred_element_type=f32)
         s = (2.0 * product - norm) / temper
-        scores[c] = s
         peak = jnp.max(s, axis=0, keepdims=True)
-        total = jnp.sum(jnp.exp(s - peak), axis=0, keepdims=True)
+        part = jnp.exp(s - peak)
+        expo[c], peaks[c] = part, peak
+        total = jnp.sum(part, axis=0, keepdims=True)
         count = jnp.where(core[0] == c, counts[:, :HALF], zero)
         blocks += [peak, total, count, zero]
     block = jnp.concatenate(blocks, axis=0)
@@ -226,36 +229,15 @@
     return pl.pallas_call(
         group_scores_kernel,
         in_specs=[SMEM] + [VMEM] * 4,
-        out_specs=[VMEM] * 2,
-        out_shape=[
-            jax.ShapeDtypeStruct((2, 256, HALF), f32),
-            jax.ShapeDtypeStruct((16, 8, 256), f32),
-        ],
-        compiler_params=params(),
-        cost_estimate=cost(2 * ROWS * 256 * D, 2 << 20, ROWS * 256),
-    )(core, fresh, near, far, counts)
-
-
-def exponents_kernel(scores, out, peaks):
-    for c in range(2):
-        s = scores[c]
-        peak = jnp.max(s, axis=0, keepdims=True)
-        out[c] = jnp.exp(s - peak)
-        peaks[c] = peak
-
-
-def level_two_exponents(scores):
-    return pl.pallas_call(
-        exponents_kernel,
-        in_specs=[VMEM],
-        out_specs=[VMEM] * 2,
+        out_specs=[VMEM] * 3,
         out_shape=[
             jax.ShapeDtypeStruct((2, 256, HALF), f32),
             jax.ShapeDtypeStruct((2, 1, HALF), f32),
+            jax.ShapeDtypeStruct((16, 8, 256), f32),
         ],
         compiler_params=params(),
-        cost_estimate=cost(ROWS * 512, 2 << 20, ROWS * 256),
-    )(scores)
+        cost_estimate=cost(2 * ROWS * 256 * D, 2 << 20, ROWS * 256),
+    )(core, fresh, near, far, counts)
 
 
 def group_sums_kernel(y_hi, expo, here, trios, fresh, out):
@@ -312,23 +294,38 @@
     return lax.all_to_all(blocks, axes, 0, 0)
 
 
-def ordered(index, mine, other):
-    return jnp.where(index == 0, mine, other), jnp.where(index == 0, other, mine)
+def ordered(first, mine, other):
+    return jnp.where(first, mine, other), jnp.where(first, other, mine)
+
+
+def cut(rows, at, n):
+    return lax.dynamic_slice(rows, (at, 0), (n, rows.shape[1]), allow_negative_indices=False)
 
 
 MIRROR = [(h * 4 + y, (1 - h) * 4 + 3 - y) for h in range(2) for y in range(4)]
 
 
 def on_device(points, centroids, groups):
-    core = lax.axis_index("core")
-    y_hi = lax.axis_index("y_hi")
-    z = lax.axis_index("z")
-    cent = lax.axis_index(NEAR)
-    core_scalar = core.astype(jnp.int32)[None]
-    y_scalar = y_hi.astype(jnp.int32)[None]
+    core = lax.axis_index("core").astype(jnp.int32)
+    y_hi = lax.axis_index("y_hi").astype(jnp.int32)
+    z = lax.axis_index("z").astype(jnp.int32)
+    cent = lax.axis_index(NEAR).astype(jnp.int32)
+    odd = z % 2
 
     to_send = spread_halves(centroids.T)
-    to_send, points = lax.optimization_barrier((to_send, points))
+    indices = (
+        core[None],
+        y_hi[None],
+        z[None],
+        (y_hi * 8 + z) * OWN,
+        odd * (HALF - FAR),
+        cent * 8,
+        core == 0,
+        y_hi == 0,
+        odd == 0,
+    )
+    to_send, points, indices = lax.optimization_barrier((to_send, points, indices))
+    core, y_hi, z, own_at, far_at, cent_at, first_core, first_y, even = indices
     piece_t = exchange(to_send, DP).reshape(D, ROWS)
     points_other = lax.ppermute(points, "core", SWAP)
 
@@ -336,41 +333,41 @@
     mine = combine(exchange(pairs, NEAR))
     other = lax.ppermute(mine, "core", SWAP)
     blocks = level_one_sums(mine, other, scores_a, scores_b, points, points_other)
+    rows = cut(piece, own_at, OWN)
+    blocks, rows = lax.optimization_barrier((blocks, rows))
     blocks = exchange(blocks, CHIPS)
-    rows = lax.dynamic_slice_in_dim(piece, (y_hi * 8 + z) * OWN, OWN, axis=0)
-    fresh_rows, counts = finish_rows(z.astype(jnp.int32)[None], blocks, rows)
+    fresh_rows, counts = finish_rows(z, blocks, rows)
 
     fresh_rows, groups_ready = lax.optimization_barrier((fresh_rows, groups))
     mine = exchange(fresh_rows, "z").reshape(HALF, D)
     groups_far = lax.ppermute(groups_ready, ("y_hi", "y_lo"), MIRROR)
     fresh = lax.all_gather(mine, "core")
 
-    scores, trios = level_two_scores(core_scalar, fresh, groups, groups_far, counts)
-    expo, here = level_two_exponents(scores)
-    odd = z % 2
+    expo, here, trios = level_two_scores(core, fresh, groups, groups_far, counts)
     rest = HALF - FAR
     expo, mine = lax.optimization_barrier((expo, mine))
-    part = lax.dynamic_slice_in_dim(mine, odd * rest, FAR, axis=0)
+    part = cut(mine, far_at, FAR)
     part = lax.ppermute(part, "y_hi", SWAP)
     trios = exchange(trios, ("core", "z"))
-    sums = level_two_sums(y_scalar, expo, here, trios, fresh)
+    sums = level_two_sums(y_hi, expo, here, trios, fresh)
     sums, part = lax.optimization_barrier((sums, part))
-    lacking = jnp.where(odd == 0, part[:rest], part[FAR - rest :])
+    lacking = jnp.where(even, part[:rest], part[FAR - rest :])
     lacking = lax.ppermute(lacking, "z", [(i, i ^ 1) for i in range(8)])
     far_mine = jnp.where(
-        odd == 0,
+        even,
         jnp.concatenate([part, lacking], axis=0),
         jnp.concatenate([lacking, part], axis=0),
     )
     blocks = exchange(sums.reshape(32, 8, WIDE), (*NEAR, "y_hi"))
-    rows = lax.dynamic_slice_in_dim(groups, cent * 8, 8, axis=0)
+    rows = cut(groups, cent_at, 8)
+    far_other = lax.ppermute(far_mine, "core", SWAP)
+    far = ordered(first_core, far_mine, far_other)
+    first, second = ordered(first_y, fresh[0], far[0]), ordered(first_y, fresh[1], far[1])
+    fresh_all = jnp.concatenate([*first, *second], axis=0)
+    blocks, fresh_all = lax.optimization_barrier((blocks, fresh_all))
     new_rows = finish_groups(blocks, rows)
-    far_other = lax.ppermute(far_mine, "core", SWAP)
     new_groups = exchange(new_rows, NEAR).reshape(128, D)
-
-    far = ordered(core, far_mine, far_other)
-    first, second = ordered(y_hi, fresh[0], far[0]), ordered(y_hi, fresh[1], far[1])
-    return (jnp.concatenate([*first, *second], axis=0), new_groups)
+    return (fresh_all, new_groups)
 
 
 def solution(mesh):

time: 181 us -> 178 us (0.983)
  blocking collectives: 69.4 us -> 107 us
  waiting for transfers between devices: 47.8 us -> 15.2 us
  starting transfers between devices: 48.3 us -> 41.7 us
    all_to_all x3 -> x5, blocking collectives: 64 us -> 101 us  [exchange(): return lax.all_to_all(blocks, axes, 0, 0)]
    all_to_all x4 -> x2, waiting for transfers between devices: 44 us -> 10.6 us  [exchange(): return lax.all_to_all(blocks, axes, 0, 0)]
    all_to_all x4 -> x2, starting transfers between devices: 18.6 us -> 8.32 us  [exchange(): return lax.all_to_all(blocks, axes, 0, 0)]
    ppermute x1, starting transfers between devices: 5.28 us -> 7.27 us  [on_device(): part = lax.ppermute(part, 'y_hi', SWAP)]
  transfers between devices with their start and end apart: 10 -> 8, of which waited for: 6 -> 5; matrix products, arithmetic and copies ran while one was open for 1% -> 1% of each run, Pallas kernels for 1% -> 1%
where the time goes in v6:
time: 178 us; the launch traced here: 175 us
  blocking collectives  107 us (60%)
  starting transfers between devices  41.7 us (23%)
  waiting for transfers between devices  15.2 us (9%)
  Pallas kernels  7.15 us (4%)
  local copies, waits for them, and re-layouts  1.78 us (1%)
    all_to_all x5, blocking collectives, exchange(): return lax.all_to_all(blocks, axes, 0, 0)  101 us
    all_to_all x2, waiting for transfers between devices, exchange(): return lax.all_to_all(blocks, axes, 0, 0)  10.6 us
    ppermute x1, starting transfers between devices, on_device(): points_other = lax.ppermute(points, 'core', SWAP)  8.79 us
    all_to_all x2, starting transfers between devices, exchange(): return lax.all_to_all(blocks, axes, 0, 0)  8.32 us
    ppermute x1, starting transfers between devices, on_device(): part = lax.ppermute(part, 'y_hi', SWAP)  7.27 us
    all_gather x1, blocking collectives, on_device(): fresh = lax.all_gather(mine, 'core')  6.29 us
    ppermute x1, starting transfers between devices, on_device(): other = lax.ppermute(mine, 'core', SWAP)  5.24 us
    ppermute x1, starting transfers between devices, on_device(): far_other = lax.ppermute(far_mine, 'core', SWAP)  5.11 us
  transfers between devices with their start and end apart: 8, of which 5 were waited for; matrix products, arithmetic and copies ran while one was open for 1% of the time, Pallas kernels for 1%

profile of v6, /device:TPU:1, one launch (start us, length us, event | category | flops | bytes accessed | tf_op | source)
XLA Modules:
  0.0 175.4 jit_solution(5308535573630431181)
XLA Ops:
  0.7 0.9 copy-done.2
  1.7 8.8 %collective-permute-start = (bf16[1024,1024]{1,0:T(8,128)(2,1)}, bf16[1024,1024]{1,0:T(8,128)(2,1)S(1)}, u32[]{:S(2)}, u32[]{:S(2)}) collective-permute-start(bf16[1024,1024]{1,0:T(8,128)(2,1)} %points_a.1), channel_id=1, source_target_pairs={{0,16},{16,0},{1,17},{17,1},{2,18},{18,2},{3,19},{19,3},{4,20},{20... | collective-permute-start | bytes 6291464 | tf_op jit(solution)/shard_map/ppermute | solution.py:330
  10.5 32.4 %all_to_all.35 = bf16[32,32,384]{2,1,0:T(8,128)(2,1)S(1)} all-to-all(bf16[32,32,384]{2,1,0:T(8,128)(2,1)S(1)} %shard_map.50), channel_id=1, replica_groups=mesh['y_hi'=2,'z'=8,'core'=2,'y_lo'=4,'x'=4] {'y_hi','z','core'}, dimensions={0} | all-to-all | bytes 1572864 | tf_op jit(solution)/shard_map/all_to_all | solution.py:294
  42.8 2.3 %shard_map.51 = (bf16[384,1024]{1,0:T(8,128)(2,1)S(1)}, f32[384,1024]{1,0:T(8,128)S(1)}, f32[384,1024]{1,0:T(8,128)S(1)}, f32[16,4,1024]{2,1,0:T(4,128)S(1)}) custom-call(bf16[1024,384]{1,0:T(8,128)(2,1)S(1)} %bitcast.21, bf16[1024,1024]{1,0:T(8,128)(2,1)S(1)} %copy-done, bf16[1024,1024]{1,0:T(8,128)(2,1)S(1)} %collective-permute-done.points_b), custom_call_target="tpu_custom_call" | custom-call | flops 1610612736 | bytes 8388608 | tf_op jit(solution)/shard_map/pallas_call | solution.py:103
  45.1 17.5 %all_to_all.36.pairs = f32[16,4,1024]{2,1,0:T(4,128)S(1)} all-to-all(f32[16,4,1024]{2,1,0:T(4,128)S(1)} %get-tuple-element.37), channel_id=1, replica_groups=mesh['y_hi'=2,'z'=8,'core'=2,'y_lo'=4,'x'=4] {'x','y_lo'}, dimensions={0} | all-to-all | bytes 524288 | tf_op jit(solution)/shard_map/all_to_all | solution.py:294
  62.6 0.1 shard_map.52.mine
  62.7 5.2 %collective-permute-start.1 = (f32[4,1024]{1,0:T(4,128)S(1)}, f32[4,1024]{1,0:T(4,128)S(1)}, u32[]{:S(2)}, u32[]{:S(2)}) collective-permute-start(f32[4,1024]{1,0:T(4,128)S(1)} %shard_map.52.mine), channel_id=1, source_target_pairs={{0,16},{16,0},{1,17},{17,1},{2,18},{18,2},{3,19},{19,3},{4,20},{20... | collective-permute-start | bytes 49160 | tf_op jit(solution)/shard_map/ppermute | solution.py:334
  68.0 0.8 collective-permute-done.1.other
  68.8 1.8 %shard_map.53 = bf16[16,200,128]{2,1,0:T(8,128)(2,1)S(1)} custom-call(f32[4,1024]{1,0:T(4,128)S(1)} %shard_map.52.mine, f32[4,1024]{1,0:T(4,128)S(1)} %collective-permute-done.1.other, f32[384,1024]{1,0:T(8,128)S(1)} %get-tuple-element.38.scores_a, f32[384,1024]{1,0:T(8,128)S(1)} %get-tuple-element.39.scores_b, bf16[1024,1024]{1,0:T(8,128)(2,1)S(1)} %copy-done, ...), custom_call_target="tpu_custom_call" | custom-call | flops 1610612736 | bytes 8388608 | tf_op jit(solution)/shard_map/pallas_call | solution.py:164
  70.6 24.9 %all_to_all.37.blocks = bf16[16,200,128]{2,1,0:T(8,128)(2,1)S(1)} all-to-all(bf16[16,200,128]{2,1,0:T(8,128)(2,1)S(1)} %shard_map.53), channel_id=1, replica_groups=mesh['y_hi'=2,'z'=8,'core'=2,'y_lo'=4,'x'=4] {'y_hi','z'}, dimensions={0} | all-to-all | bytes 1638400 | tf_op jit(solution)/shard_map/all_to_all | solution.py:294
  95.4 0.9 shard_map.54
  96.3 3.9 %all-to-all-start.3 = ((bf16[8,24,1024]{2,1,0:T(8,128)(2,1)}), bf16[8,24,1024]{2,1,0:T(8,128)(2,1)S(1)}, u32[]{:S(2)}, u32[]{:S(2)}) async-start(bf16[8,24,1024]{2,1,0:T(8,128)(2,1)} %get-tuple-element.45), calls=%async_computation.3 | async-start | bytes 786432 | tf_op jit(solution)/shard_map/all_to_all | solution.py:294
  100.2 4.1 %collective-permute-start.2 = (bf16[128,1024]{1,0:T(8,128)(2,1)S(1)}, bf16[128,1024]{1,0:T(8,128)(2,1)S(1)}, u32[]{:S(2)}, u32[]{:S(2)}) collective-permute-start(bf16[128,1024]{1,0:T(8,128)(2,1)S(1)} %copy-done.1), channel_id=1, source_target_pairs={{0,268},{4,264},{8,260},{12,256},{256,12},{260,8},{264,4},{268,0},... | collective-permute-start | bytes 786440 | tf_op jit(solution)/shard_map/ppermute | solution.py:343
  104.3 7.2 %all-to-all-done.3 = bf16[8,24,1024]{2,1,0:T(8,128)(2,1)S(1)} async-done(((bf16[8,24,1024]{2,1,0:T(8,128)(2,1)}), bf16[8,24,1024]{2,1,0:T(8,128)(2,1)S(1)}, u32[]{:S(2)}, u32[]{:S(2)}) %all-to-all-start.3) | async-done | bytes 393248 | tf_op jit(solution)/shard_map/all_to_all | solution.py:294
  111.5 6.3 %all_gather.3.fresh = bf16[2,192,1024]{2,1,0:T(8,128)(2,1)S(1)} all-gather(bf16[1,192,1024]{2,1,0:T(8,128)(2,1)S(1)} %bitcast.23), channel_id=1, replica_groups=mesh['y_hi'=2,'z'=8,'core'=2,'y_lo'=4,'x'=4] {'core'}, dimensions={0}, use_global_device_ids=true | all-gather | bytes 1179648 | tf_op jit(solution)/shard_map/all_gather | solution.py:344
  117.8 0.6 shard_map.55
  118.4 0.1 constant_dynamic-slice_fusion.1
  118.5 7.3 %collective-permute-start.3 = (bf16[144,1024]{1,0:T(8,128)(2,1)S(1)}, bf16[144,1024]{1,0:T(8,128)(2,1)S(1)}, u32[]{:S(2)}, u32[]{:S(2)}) collective-permute-start(bf16[144,1024]{1,0:T(8,128)(2,1)S(1)} %constant_dynamic-slice_fusion.1), channel_id=1, source_target_pairs={{0,256},{256,0},{1,257},{257,1},{2,258},{258,2},{3,259},{259,3},{4... | collective-permute-start | bytes 884744 | tf_op jit(solution)/shard_map/ppermute | solution.py:350
  125.8 14.1 %all_to_all.38.trios = f32[16,8,256]{2,1,0:T(8,128)S(1)} all-to-all(f32[16,8,256]{2,1,0:T(8,128)S(1)} %get-tuple-element.51), channel_id=1, replica_groups=mesh['y_hi'=2,'z'=8,'core'=2,'y_lo'=4,'x'=4] {'core','z'}, dimensions={0} | all-to-all | bytes 262144 | tf_op jit(solution)/shard_map/all_to_all | solution.py:294
  139.9 1.3 shard_map.56
  141.2 4.4 %all-to-all-start.5 = ((bf16[32,8,1152]{2,1,0:T(8,128)(2,1)}), bf16[32,8,1152]{2,1,0:T(8,128)(2,1)S(1)}, u32[]{:S(2)}, u32[]{:S(2)}) async-start(bf16[32,8,1152]{2,1,0:T(8,128)(2,1)} %bitcast.7), calls=%async_computation.5 | async-start | bytes 1179648 | tf_op jit(solution)/shard_map/all_to_all | solution.py:294
  145.7 2.9 %collective-permute-start.4 = (bf16[48,1024]{1,0:T(8,128)(2,1)S(1)}, bf16[48,1024]{1,0:T(8,128)(2,1)S(1)}, u32[]{:S(2)}, u32[]{:S(2)}) collective-permute-start(bf16[48,1024]{1,0:T(8,128)(2,1)S(1)} %slice_select_fusion), channel_id=1, source_target_pairs={{0,32},{32,0},{64,96},{96,64},{128,160},{160,128},{192,224},{224,1... | collective-permute-start | bytes 294920 | tf_op jit(solution)/shard_map/ppermute | solution.py:355
  148.6 2.5 %collective-permute-done.4 = bf16[48,1024]{1,0:T(8,128)(2,1)S(1)} collective-permute-done((bf16[48,1024]{1,0:T(8,128)(2,1)S(1)}, bf16[48,1024]{1,0:T(8,128)(2,1)S(1)}, u32[]{:S(2)}, u32[]{:S(2)}) %collective-permute-start.4) | collective-permute-done | bytes 98336 | tf_op jit(solution)/shard_map/ppermute | solution.py:355
  151.1 0.1 maximum_select_fusion
  151.2 5.1 %collective-permute-start.5 = (bf16[192,1024]{1,0:T(8,128)(2,1)S(1)}, bf16[192,1024]{1,0:T(8,128)(2,1)S(1)}, u32[]{:S(2)}, u32[]{:S(2)}) collective-permute-start(bf16[192,1024]{1,0:T(8,128)(2,1)S(1)} %maximum_select_fusion), channel_id=1, source_target_pairs={{0,16},{16,0},{1,17},{17,1},{2,18},{18,2},{3,19},{19,3},{4,20},{20... | collective-permute-start | bytes 1179656 | tf_op jit(solution)/shard_map/ppermute | solution.py:363
  156.3 1.3 collective-permute-done.5
  157.6 0.1 broadcast_select_fusion.5
  157.7 1.3 pad_maximum_fusion
  159.0 3.4 %all-to-all-done.5.blocks = bf16[32,8,1152]{2,1,0:T(8,128)(2,1)S(1)} async-done(((bf16[32,8,1152]{2,1,0:T(8,128)(2,1)}), bf16[32,8,1152]{2,1,0:T(8,128)(2,1)S(1)}, u32[]{:S(2)}, u32[]{:S(2)}) %all-to-all-start.5) | async-done | bytes 589856 | tf_op jit(solution)/shard_map/all_to_all | solution.py:294
  162.4 0.1 shard_map.57
  162.5 12.2 %all_to_all.39 = bf16[16,8,1024]{2,1,0:T(8,128)(2,1)S(1)} all-to-all(bf16[16,8,1024]{2,1,0:T(8,128)(2,1)S(1)} %shard_map.57), channel_id=1, replica_groups=mesh['y_hi'=2,'z'=8,'core'=2,'y_lo'=4,'x'=4] {'x','y_lo'}, dimensions={0} | all-to-all | bytes 524288 | tf_op jit(solution)/shard_map/all_to_all | solution.py:294
  174.7 0.7 copy.6
  (12 shorter events, 0.2 us)
Async XLA Ops:
  0.6 42.2 %copy-start = (bf16[1024,1024]{1,0:T(8,128)(2,1)S(1)}, bf16[1024,1024]{1,0:T(8,128)(2,1)}, u32[]{:S(2)}) copy-start(bf16[1024,1024]{1,0:T(8,128)(2,1)} %points_a.1) | copy-start | bytes 6291460
  0.7 0.9 copy-start.2
  1.7 41.2 %collective-permute-start = (bf16[1024,1024]{1,0:T(8,128)(2,1)}, bf16[1024,1024]{1,0:T(8,128)(2,1)S(1)}, u32[]{:S(2)}, u32[]{:S(2)}) collective-permute-start(bf16[1024,1024]{1,0:T(8,128)(2,1)} %points_a.1), channel_id=1, source_target_pairs={{0,16},{16,0},{1,17},{17,1},{2,18},{18,2},{3,19},{19,3},{4,20},{20... | collective-permute-start | bytes 6291464 | tf_op jit(solution)/shard_map/ppermute | solution.py:330
  62.7 6.1 %collective-permute-start.1 = (f32[4,1024]{1,0:T(4,128)S(1)}, f32[4,1024]{1,0:T(4,128)S(1)}, u32[]{:S(2)}, u32[]{:S(2)}) collective-permute-start(f32[4,1024]{1,0:T(4,128)S(1)} %shard_map.52.mine), channel_id=1, source_target_pairs={{0,16},{16,0},{1,17},{17,1},{2,18},{18,2},{3,19},{19,3},{4,20},{20... | collective-permute-start | bytes 49160 | tf_op jit(solution)/shard_map/ppermute | solution.py:334
  70.6 29.6 %copy-start.1 = (bf16[128,1024]{1,0:T(8,128)(2,1)S(1)}, bf16[128,1024]{1,0:T(8,128)(2,1)}, u32[]{:S(2)}) copy-start(bf16[128,1024]{1,0:T(8,128)(2,1)} %near.1) | copy-start | bytes 786436
  96.3 15.2 %all-to-all-start.3 = ((bf16[8,24,1024]{2,1,0:T(8,128)(2,1)}), bf16[8,24,1024]{2,1,0:T(8,128)(2,1)S(1)}, u32[]{:S(2)}, u32[]{:S(2)}) async-start(bf16[8,24,1024]{2,1,0:T(8,128)(2,1)} %get-tuple-element.45), calls=%async_computation.3 | async-start | bytes 786432 | tf_op jit(solution)/shard_map/all_to_all | solution.py:294
  100.2 17.6 %collective-permute-start.2 = (bf16[128,1024]{1,0:T(8,128)(2,1)S(1)}, bf16[128,1024]{1,0:T(8,128)(2,1)S(1)}, u32[]{:S(2)}, u32[]{:S(2)}) collective-permute-start(bf16[128,1024]{1,0:T(8,128)(2,1)S(1)} %copy-done.1), channel_id=1, source_target_pairs={{0,268},{4,264},{8,260},{12,256},{256,12},{260,8},{264,4},{268,0},... | collective-permute-start | bytes 786440 | tf_op jit(solution)/shard_map/ppermute | solution.py:343
  118.5 22.7 %collective-permute-start.3 = (bf16[144,1024]{1,0:T(8,128)(2,1)S(1)}, bf16[144,1024]{1,0:T(8,128)(2,1)S(1)}, u32[]{:S(2)}, u32[]{:S(2)}) collective-permute-start(bf16[144,1024]{1,0:T(8,128)(2,1)S(1)} %constant_dynamic-slice_fusion.1), channel_id=1, source_target_pairs={{0,256},{256,0},{1,257},{257,1},{2,258},{258,2},{3,259},{259,3},{4... | collective-permute-start | bytes 884744 | tf_op jit(solution)/shard_map/ppermute | solution.py:350
  141.2 21.2 %all-to-all-start.5 = ((bf16[32,8,1152]{2,1,0:T(8,128)(2,1)}), bf16[32,8,1152]{2,1,0:T(8,128)(2,1)S(1)}, u32[]{:S(2)}, u32[]{:S(2)}) async-start(bf16[32,8,1152]{2,1,0:T(8,128)(2,1)} %bitcast.7), calls=%async_computation.5 | async-start | bytes 1179648 | tf_op jit(solution)/shard_map/all_to_all | solution.py:294
  145.7 5.4 %collective-permute-start.4 = (bf16[48,1024]{1,0:T(8,128)(2,1)S(1)}, bf16[48,1024]{1,0:T(8,128)(2,1)S(1)}, u32[]{:S(2)}, u32[]{:S(2)}) collective-permute-start(bf16[48,1024]{1,0:T(8,128)(2,1)S(1)} %slice_select_fusion), channel_id=1, source_target_pairs={{0,32},{32,0},{64,96},{96,64},{128,160},{160,128},{192,224},{224,1... | collective-permute-start | bytes 294920 | tf_op jit(solution)/shard_map/ppermute | solution.py:355
  151.2 6.4 %collective-permute-start.5 = (bf16[192,1024]{1,0:T(8,128)(2,1)S(1)}, bf16[192,1024]{1,0:T(8,128)(2,1)S(1)}, u32[]{:S(2)}, u32[]{:S(2)}) collective-permute-start(bf16[192,1024]{1,0:T(8,128)(2,1)S(1)} %maximum_select_fusion), channel_id=1, source_target_pairs={{0,16},{16,0},{1,17},{17,1},{2,18},{18,2},{3,19},{19,3},{4,20},{20... | collective-permute-start | bytes 1179656 | tf_op jit(solution)/shard_map/ppermute | solution.py:363

commit v7 on v6

--- a/solution.py
+++ b/solution.py
@@ -14,7 +14,7 @@
 SWAP = [(0, 1), (1, 0)]
 D = 1024
 WIDE = 1152
-STEP = 256
+STEP = 512
 ROWS = 384
 OWN = 24
 PACK = 200
@@ -345,7 +345,6 @@
 
     expo, here, trios = level_two_scores(core, fresh, groups, groups_far, counts)
     rest = HALF - FAR
-    expo, mine = lax.optimization_barrier((expo, mine))
     part = cut(mine, far_at, FAR)
     part = lax.ppermute(part, "y_hi", SWAP)
     trios = exchange(trios, ("core", "z"))

time: 178 us -> 186 us (1.045)
  starting transfers between devices: 41.7 us -> 55.7 us
  blocking collectives: 107 us -> 101 us
    all_to_all x2, starting transfers between devices: 8.32 us -> 19.8 us  [exchange(): return lax.all_to_all(blocks, axes, 0, 0)]
    all_to_all x5, blocking collectives: 101 us -> 97.4 us  [exchange(): return lax.all_to_all(blocks, axes, 0, 0)]
    ppermute x1, starting transfers between devices: 7.27 us -> 10.1 us  [on_device(): part = lax.ppermute(part, 'y_hi', SWAP)]
    all_gather x1, blocking collectives: 6.29 us -> 3.72 us  [on_device(): fresh = lax.all_gather(mine, 'core')]
where the time goes in v7:
time: 186 us; the launch traced here: 184 us
  blocking collectives  101 us (54%)
  starting transfers between devices  55.7 us (30%)
  waiting for transfers between devices  15.6 us (8%)
  Pallas kernels  7.11 us (4%)
    all_to_all x5, blocking collectives, exchange(): return lax.all_to_all(blocks, axes, 0, 0)  97.4 us
    all_to_all x2, starting transfers between devices, exchange(): return lax.all_to_all(blocks, axes, 0, 0)  19.8 us
    all_to_all x2, waiting for transfers between devices, exchange(): return lax.all_to_all(blocks, axes, 0, 0)  11.2 us
    ppermute x1, starting transfers between devices, on_device(): part = lax.ppermute(part, 'y_hi', SWAP)  10.1 us
    ppermute x1, starting transfers between devices, on_device(): points_other = lax.ppermute(points, 'core', SWAP)  8.79 us
    ppermute x1, starting transfers between devices, on_device(): other = lax.ppermute(mine, 'core', SWAP)  5.25 us
    ppermute x1, starting transfers between devices, on_device(): far_other = lax.ppermute(far_mine, 'core', SWAP)  4.26 us
    ppermute x1, starting transfers between devices, on_device(): groups_far = lax.ppermute(groups_ready, ('y_hi', 'y_lo'), MIRROR)  4.07 us
  transfers between devices with their start and end apart: 8, of which 5 were waited for; matrix products, arithmetic and copies ran while one was open for 1% of the time, Pallas kernels for 1%

profile of v7, /device:TPU:1, one launch (start us, length us, event | category | flops | bytes accessed | tf_op | source)
XLA Modules:
  0.0 183.5 jit_solution(13522361596863336126)
XLA Ops:
  0.7 0.9 copy-done.2
  1.7 8.8 %collective-permute-start = (bf16[1024,1024]{1,0:T(8,128)(2,1)}, bf16[1024,1024]{1,0:T(8,128)(2,1)S(1)}, u32[]{:S(2)}, u32[]{:S(2)}) collective-permute-start(bf16[1024,1024]{1,0:T(8,128)(2,1)} %points_a.1), channel_id=1, source_target_pairs={{0,16},{16,0},{1,17},{17,1},{2,18},{18,2},{3,19},{19,3},{4,20},{20... | collective-permute-start | bytes 6291464 | tf_op jit(solution)/shard_map/ppermute | solution.py:330
  10.5 32.4 %all_to_all.35 = bf16[32,32,384]{2,1,0:T(8,128)(2,1)S(1)} all-to-all(bf16[32,32,384]{2,1,0:T(8,128)(2,1)S(1)} %shard_map.50), channel_id=1, replica_groups=mesh['y_hi'=2,'z'=8,'core'=2,'y_lo'=4,'x'=4] {'y_hi','z','core'}, dimensions={0} | all-to-all | bytes 1572864 | tf_op jit(solution)/shard_map/all_to_all | solution.py:294
  42.8 2.2 %shard_map.51 = (bf16[384,1024]{1,0:T(8,128)(2,1)S(1)}, f32[384,1024]{1,0:T(8,128)S(1)}, f32[384,1024]{1,0:T(8,128)S(1)}, f32[16,4,1024]{2,1,0:T(4,128)S(1)}) custom-call(bf16[1024,384]{1,0:T(8,128)(2,1)S(1)} %bitcast.21, bf16[1024,1024]{1,0:T(8,128)(2,1)S(1)} %copy-done, bf16[1024,1024]{1,0:T(8,128)(2,1)S(1)} %collective-permute-done.points_b), custom_call_target="tpu_custom_call" | custom-call | flops 1610612736 | bytes 8388608 | tf_op jit(solution)/shard_map/pallas_call | solution.py:103
  45.1 17.5 %all_to_all.36.pairs = f32[16,4,1024]{2,1,0:T(4,128)S(1)} all-to-all(f32[16,4,1024]{2,1,0:T(4,128)S(1)} %get-tuple-element.35), channel_id=1, replica_groups=mesh['y_hi'=2,'z'=8,'core'=2,'y_lo'=4,'x'=4] {'x','y_lo'}, dimensions={0} | all-to-all | bytes 524288 | tf_op jit(solution)/shard_map/all_to_all | solution.py:294
  62.5 0.1 shard_map.52.mine
  62.6 5.3 %collective-permute-start.1 = (f32[4,1024]{1,0:T(4,128)S(1)}, f32[4,1024]{1,0:T(4,128)S(1)}, u32[]{:S(2)}, u32[]{:S(2)}) collective-permute-start(f32[4,1024]{1,0:T(4,128)S(1)} %shard_map.52.mine), channel_id=1, source_target_pairs={{0,16},{16,0},{1,17},{17,1},{2,18},{18,2},{3,19},{19,3},{4,20},{20... | collective-permute-start | bytes 49160 | tf_op jit(solution)/shard_map/ppermute | solution.py:334
  67.9 0.8 collective-permute-done.1.other
  68.7 1.8 shard_map.53
  70.5 24.9 %all_to_all.37.blocks = bf16[16,200,128]{2,1,0:T(8,128)(2,1)S(1)} all-to-all(bf16[16,200,128]{2,1,0:T(8,128)(2,1)S(1)} %shard_map.53), channel_id=1, replica_groups=mesh['y_hi'=2,'z'=8,'core'=2,'y_lo'=4,'x'=4] {'y_hi','z'}, dimensions={0} | all-to-all | bytes 1638400 | tf_op jit(solution)/shard_map/all_to_all | solution.py:294
  95.4 0.9 shard_map.54
  96.3 3.9 %all-to-all-start.3 = ((bf16[8,24,1024]{2,1,0:T(8,128)(2,1)}), bf16[8,24,1024]{2,1,0:T(8,128)(2,1)S(1)}, u32[]{:S(2)}, u32[]{:S(2)}) async-start(bf16[8,24,1024]{2,1,0:T(8,128)(2,1)} %get-tuple-element.43), calls=%async_computation.3 | async-start | bytes 786432 | tf_op jit(solution)/shard_map/all_to_all | solution.py:294
  100.2 4.1 %collective-permute-start.2 = (bf16[128,1024]{1,0:T(8,128)(2,1)S(1)}, bf16[128,1024]{1,0:T(8,128)(2,1)S(1)}, u32[]{:S(2)}, u32[]{:S(2)}) collective-permute-start(bf16[128,1024]{1,0:T(8,128)(2,1)S(1)} %copy-done.1), channel_id=1, source_target_pairs={{0,268},{4,264},{8,260},{12,256},{256,12},{260,8},{264,4},{268,0},... | collective-permute-start | bytes 786440 | tf_op jit(solution)/shard_map/ppermute | solution.py:343
  104.3 7.3 %all-to-all-done.3 = bf16[8,24,1024]{2,1,0:T(8,128)(2,1)S(1)} async-done(((bf16[8,24,1024]{2,1,0:T(8,128)(2,1)}), bf16[8,24,1024]{2,1,0:T(8,128)(2,1)S(1)}, u32[]{:S(2)}, u32[]{:S(2)}) %all-to-all-start.3) | async-done | bytes 393248 | tf_op jit(solution)/shard_map/all_to_all | solution.py:294
  111.6 0.1 constant_dynamic-slice_fusion.1
  111.6 10.1 %collective-permute-start.3 = (bf16[144,1024]{1,0:T(8,128)(2,1)S(1)}, bf16[144,1024]{1,0:T(8,128)(2,1)S(1)}, u32[]{:S(2)}, u32[]{:S(2)}) collective-permute-start(bf16[144,1024]{1,0:T(8,128)(2,1)S(1)} %constant_dynamic-slice_fusion.1), channel_id=1, source_target_pairs={{0,256},{256,0},{1,257},{257,1},{2,258},{258,2},{3,259},{259,3},{4... | collective-permute-start | bytes 884744 | tf_op jit(solution)/shard_map/ppermute | solution.py:349
  121.7 3.7 %all_gather.3.fresh = bf16[2,192,1024]{2,1,0:T(8,128)(2,1)S(1)} all-gather(bf16[1,192,1024]{2,1,0:T(8,128)(2,1)S(1)} %bitcast.24), channel_id=1, replica_groups=mesh['y_hi'=2,'z'=8,'core'=2,'y_lo'=4,'x'=4] {'core'}, dimensions={0}, use_global_device_ids=true | all-gather | bytes 1179648 | tf_op jit(solution)/shard_map/all_gather | solution.py:344
  125.4 0.6 shard_map.55
  126.0 10.2 %all_to_all.38.trios = f32[16,8,256]{2,1,0:T(8,128)S(1)} all-to-all(f32[16,8,256]{2,1,0:T(8,128)S(1)} %get-tuple-element.48), channel_id=1, replica_groups=mesh['y_hi'=2,'z'=8,'core'=2,'y_lo'=4,'x'=4] {'core','z'}, dimensions={0} | all-to-all | bytes 262144 | tf_op jit(solution)/shard_map/all_to_all | solution.py:294
  136.2 1.3 shard_map.56
  137.5 15.9 %all-to-all-start.5 = ((bf16[32,8,1152]{2,1,0:T(8,128)(2,1)}), bf16[32,8,1152]{2,1,0:T(8,128)(2,1)S(1)}, u32[]{:S(2)}, u32[]{:S(2)}) async-start(bf16[32,8,1152]{2,1,0:T(8,128)(2,1)} %bitcast.7), calls=%async_computation.5 | async-start | bytes 1179648 | tf_op jit(solution)/shard_map/all_to_all | solution.py:294
  153.5 3.4 %collective-permute-start.4 = (bf16[48,1024]{1,0:T(8,128)(2,1)S(1)}, bf16[48,1024]{1,0:T(8,128)(2,1)S(1)}, u32[]{:S(2)}, u32[]{:S(2)}) collective-permute-start(bf16[48,1024]{1,0:T(8,128)(2,1)S(1)} %slice_select_fusion), channel_id=1, source_target_pairs={{0,32},{32,0},{64,96},{96,64},{128,160},{160,128},{192,224},{224,1... | collective-permute-start | bytes 294920 | tf_op jit(solution)/shard_map/ppermute | solution.py:354
  156.9 2.3 %collective-permute-done.4 = bf16[48,1024]{1,0:T(8,128)(2,1)S(1)} collective-permute-done((bf16[48,1024]{1,0:T(8,128)(2,1)S(1)}, bf16[48,1024]{1,0:T(8,128)(2,1)S(1)}, u32[]{:S(2)}, u32[]{:S(2)}) %collective-permute-start.4) | collective-permute-done | bytes 98336 | tf_op jit(solution)/shard_map/ppermute | solution.py:354
  159.2 0.1 maximum_select_fusion
  159.3 4.3 %collective-permute-start.5 = (bf16[192,1024]{1,0:T(8,128)(2,1)S(1)}, bf16[192,1024]{1,0:T(8,128)(2,1)S(1)}, u32[]{:S(2)}, u32[]{:S(2)}) collective-permute-start(bf16[192,1024]{1,0:T(8,128)(2,1)S(1)} %maximum_select_fusion), channel_id=1, source_target_pairs={{0,16},{16,0},{1,17},{17,1},{2,18},{18,2},{3,19},{19,3},{4,20},{20... | collective-permute-start | bytes 1179656 | tf_op jit(solution)/shard_map/ppermute | solution.py:362
  163.6 1.3 collective-permute-done.5
  164.9 0.1 broadcast_select_fusion.5
  165.0 1.3 pad_maximum_fusion
  166.2 4.0 %all-to-all-done.5.blocks = bf16[32,8,1152]{2,1,0:T(8,128)(2,1)S(1)} async-done(((bf16[32,8,1152]{2,1,0:T(8,128)(2,1)}), bf16[32,8,1152]{2,1,0:T(8,128)(2,1)S(1)}, u32[]{:S(2)}, u32[]{:S(2)}) %all-to-all-start.5) | async-done | bytes 589856 | tf_op jit(solution)/shard_map/all_to_all | solution.py:294
  170.2 0.1 shard_map.57
  170.3 12.5 %all_to_all.39 = bf16[16,8,1024]{2,1,0:T(8,128)(2,1)S(1)} all-to-all(bf16[16,8,1024]{2,1,0:T(8,128)(2,1)S(1)} %shard_map.57), channel_id=1, replica_groups=mesh['y_hi'=2,'z'=8,'core'=2,'y_lo'=4,'x'=4] {'x','y_lo'}, dimensions={0} | all-to-all | bytes 524288 | tf_op jit(solution)/shard_map/all_to_all | solution.py:294
  182.8 0.7 copy.6
  (12 shorter events, 0.2 us)
Async XLA Ops:
  0.6 42.2 %copy-start = (bf16[1024,1024]{1,0:T(8,128)(2,1)S(1)}, bf16[1024,1024]{1,0:T(8,128)(2,1)}, u32[]{:S(2)}) copy-start(bf16[1024,1024]{1,0:T(8,128)(2,1)} %points_a.1) | copy-start | bytes 6291460
  0.7 0.9 copy-start.2
  1.7 41.2 %collective-permute-start = (bf16[1024,1024]{1,0:T(8,128)(2,1)}, bf16[1024,1024]{1,0:T(8,128)(2,1)S(1)}, u32[]{:S(2)}, u32[]{:S(2)}) collective-permute-start(bf16[1024,1024]{1,0:T(8,128)(2,1)} %points_a.1), channel_id=1, source_target_pairs={{0,16},{16,0},{1,17},{17,1},{2,18},{18,2},{3,19},{19,3},{4,20},{20... | collective-permute-start | bytes 6291464 | tf_op jit(solution)/shard_map/ppermute | solution.py:330
  62.6 6.1 %collective-permute-start.1 = (f32[4,1024]{1,0:T(4,128)S(1)}, f32[4,1024]{1,0:T(4,128)S(1)}, u32[]{:S(2)}, u32[]{:S(2)}) collective-permute-start(f32[4,1024]{1,0:T(4,128)S(1)} %shard_map.52.mine), channel_id=1, source_target_pairs={{0,16},{16,0},{1,17},{17,1},{2,18},{18,2},{3,19},{19,3},{4,20},{20... | collective-permute-start | bytes 49160 | tf_op jit(solution)/shard_map/ppermute | solution.py:334
  70.5 29.7 %copy-start.1 = (bf16[128,1024]{1,0:T(8,128)(2,1)S(1)}, bf16[128,1024]{1,0:T(8,128)(2,1)}, u32[]{:S(2)}) copy-start(bf16[128,1024]{1,0:T(8,128)(2,1)} %near.1) | copy-start | bytes 786436
  96.3 15.3 %all-to-all-start.3 = ((bf16[8,24,1024]{2,1,0:T(8,128)(2,1)}), bf16[8,24,1024]{2,1,0:T(8,128)(2,1)S(1)}, u32[]{:S(2)}, u32[]{:S(2)}) async-start(bf16[8,24,1024]{2,1,0:T(8,128)(2,1)} %get-tuple-element.43), calls=%async_computation.3 | async-start | bytes 786432 | tf_op jit(solution)/shard_map/all_to_all | solution.py:294
  100.2 25.2 %collective-permute-start.2 = (bf16[128,1024]{1,0:T(8,128)(2,1)S(1)}, bf16[128,1024]{1,0:T(8,128)(2,1)S(1)}, u32[]{:S(2)}, u32[]{:S(2)}) collective-permute-start(bf16[128,1024]{1,0:T(8,128)(2,1)S(1)} %copy-done.1), channel_id=1, source_target_pairs={{0,268},{4,264},{8,260},{12,256},{256,12},{260,8},{264,4},{268,0},... | collective-permute-start | bytes 786440 | tf_op jit(solution)/shard_map/ppermute | solution.py:343
  111.6 25.9 %collective-permute-start.3 = (bf16[144,1024]{1,0:T(8,128)(2,1)S(1)}, bf16[144,1024]{1,0:T(8,128)(2,1)S(1)}, u32[]{:S(2)}, u32[]{:S(2)}) collective-permute-start(bf16[144,1024]{1,0:T(8,128)(2,1)S(1)} %constant_dynamic-slice_fusion.1), channel_id=1, source_target_pairs={{0,256},{256,0},{1,257},{257,1},{2,258},{258,2},{3,259},{259,3},{4... | collective-permute-start | bytes 884744 | tf_op jit(solution)/shard_map/ppermute | solution.py:349
  137.5 32.6 %all-to-all-start.5 = ((bf16[32,8,1152]{2,1,0:T(8,128)(2,1)}), bf16[32,8,1152]{2,1,0:T(8,128)(2,1)S(1)}, u32[]{:S(2)}, u32[]{:S(2)}) async-start(bf16[32,8,1152]{2,1,0:T(8,128)(2,1)} %bitcast.7), calls=%async_computation.5 | async-start | bytes 1179648 | tf_op jit(solution)/shard_map/all_to_all | solution.py:294
  153.5 5.7 %collective-permute-start.4 = (bf16[48,1024]{1,0:T(8,128)(2,1)S(1)}, bf16[48,1024]{1,0:T(8,128)(2,1)S(1)}, u32[]{:S(2)}, u32[]{:S(2)}) collective-permute-start(bf16[48,1024]{1,0:T(8,128)(2,1)S(1)} %slice_select_fusion), channel_id=1, source_target_pairs={{0,32},{32,0},{64,96},{96,64},{128,160},{160,128},{192,224},{224,1... | collective-permute-start | bytes 294920 | tf_op jit(solution)/shard_map/ppermute | solution.py:354
  159.3 5.6 %collective-permute-start.5 = (bf16[192,1024]{1,0:T(8,128)(2,1)S(1)}, bf16[192,1024]{1,0:T(8,128)(2,1)S(1)}, u32[]{:S(2)}, u32[]{:S(2)}) collective-permute-start(bf16[192,1024]{1,0:T(8,128)(2,1)S(1)} %maximum_select_fusion), channel_id=1, source_target_pairs={{0,16},{16,0},{1,17},{17,1},{2,18},{18,2},{3,19},{19,3},{4,20},{20... | collective-permute-start | bytes 1179656 | tf_op jit(solution)/shard_map/ppermute | solution.py:362

commit v8 on v7

--- a/solution.py
+++ b/solution.py
@@ -345,6 +345,7 @@
 
     expo, here, trios = level_two_scores(core, fresh, groups, groups_far, counts)
     rest = HALF - FAR
+    expo, mine = lax.optimization_barrier((expo, mine))
     part = cut(mine, far_at, FAR)
     part = lax.ppermute(part, "y_hi", SWAP)
     trios = exchange(trios, ("core", "z"))

time: 186 us -> 178 us (0.957)
  starting transfers between devices: 55.7 us -> 41.7 us
  blocking collectives: 101 us -> 107 us
    all_to_all x2, starting transfers between devices: 19.8 us -> 8.35 us  [exchange(): return lax.all_to_all(blocks, axes, 0, 0)]
    all_to_all x5, blocking collectives: 97.4 us -> 101 us  [exchange(): return lax.all_to_all(blocks, axes, 0, 0)]
    ppermute x1, starting transfers between devices: 10.1 us -> 7.24 us  [on_device(): part = lax.ppermute(part, 'y_hi', SWAP)]
    all_gather x1, blocking collectives: 3.72 us -> 6.25 us  [on_device(): fresh = lax.all_gather(mine, 'core')]
where the time goes in v8:
time: 178 us; the launch traced here: 175 us
  blocking collectives  107 us (60%)
  starting transfers between devices  41.7 us (23%)
  waiting for transfers between devices  15.3 us (9%)
  Pallas kernels  7.1 us (4%)
  local copies, waits for them, and re-layouts  1.78 us (1%)
    all_to_all x5, blocking collectives, exchange(): return lax.all_to_all(blocks, axes, 0, 0)  101 us
    all_to_all x2, waiting for transfers between devices, exchange(): return lax.all_to_all(blocks, axes, 0, 0)  10.7 us
    ppermute x1, starting transfers between devices, on_device(): points_other = lax.ppermute(points, 'core', SWAP)  8.79 us
    all_to_all x2, starting transfers between devices, exchange(): return lax.all_to_all(blocks, axes, 0, 0)  8.35 us
    ppermute x1, starting transfers between devices, on_device(): part = lax.ppermute(part, 'y_hi', SWAP)  7.24 us
    all_gather x1, blocking collectives, on_device(): fresh = lax.all_gather(mine, 'core')  6.25 us
    ppermute x1, starting transfers between devices, on_device(): other = lax.ppermute(mine, 'core', SWAP)  5.25 us
    ppermute x1, starting transfers between devices, on_device(): far_other = lax.ppermute(far_mine, 'core', SWAP)  5.1 us
  transfers between devices with their start and end apart: 8, of which 5 were waited for; matrix products, arithmetic and copies ran while one was open for 1% of the time, Pallas kernels for 1%

profile of v8, /device:TPU:1, one launch (start us, length us, event | category | flops | bytes accessed | tf_op | source)
XLA Modules:
  0.0 175.4 jit_solution(7782785496141655884)
XLA Ops:
  0.7 0.9 copy-done.2
  1.7 8.8 %collective-permute-start = (bf16[1024,1024]{1,0:T(8,128)(2,1)}, bf16[1024,1024]{1,0:T(8,128)(2,1)S(1)}, u32[]{:S(2)}, u32[]{:S(2)}) collective-permute-start(bf16[1024,1024]{1,0:T(8,128)(2,1)} %points_a.1), channel_id=1, source_target_pairs={{0,16},{16,0},{1,17},{17,1},{2,18},{18,2},{3,19},{19,3},{4,20},{20... | collective-permute-start | bytes 6291464 | tf_op jit(solution)/shard_map/ppermute | solution.py:330
  10.5 32.4 %all_to_all.35 = bf16[32,32,384]{2,1,0:T(8,128)(2,1)S(1)} all-to-all(bf16[32,32,384]{2,1,0:T(8,128)(2,1)S(1)} %shard_map.50), channel_id=1, replica_groups=mesh['y_hi'=2,'z'=8,'core'=2,'y_lo'=4,'x'=4] {'y_hi','z','core'}, dimensions={0} | all-to-all | bytes 1572864 | tf_op jit(solution)/shard_map/all_to_all | solution.py:294
  42.8 2.2 %shard_map.51 = (bf16[384,1024]{1,0:T(8,128)(2,1)S(1)}, f32[384,1024]{1,0:T(8,128)S(1)}, f32[384,1024]{1,0:T(8,128)S(1)}, f32[16,4,1024]{2,1,0:T(4,128)S(1)}) custom-call(bf16[1024,384]{1,0:T(8,128)(2,1)S(1)} %bitcast.21, bf16[1024,1024]{1,0:T(8,128)(2,1)S(1)} %copy-done, bf16[1024,1024]{1,0:T(8,128)(2,1)S(1)} %collective-permute-done.points_b), custom_call_target="tpu_custom_call" | custom-call | flops 1610612736 | bytes 8388608 | tf_op jit(solution)/shard_map/pallas_call | solution.py:103
  45.1 17.5 %all_to_all.36.pairs = f32[16,4,1024]{2,1,0:T(4,128)S(1)} all-to-all(f32[16,4,1024]{2,1,0:T(4,128)S(1)} %get-tuple-element.37), channel_id=1, replica_groups=mesh['y_hi'=2,'z'=8,'core'=2,'y_lo'=4,'x'=4] {'x','y_lo'}, dimensions={0} | all-to-all | bytes 524288 | tf_op jit(solution)/shard_map/all_to_all | solution.py:294
  62.5 0.1 shard_map.52.mine
  62.6 5.3 %collective-permute-start.1 = (f32[4,1024]{1,0:T(4,128)S(1)}, f32[4,1024]{1,0:T(4,128)S(1)}, u32[]{:S(2)}, u32[]{:S(2)}) collective-permute-start(f32[4,1024]{1,0:T(4,128)S(1)} %shard_map.52.mine), channel_id=1, source_target_pairs={{0,16},{16,0},{1,17},{17,1},{2,18},{18,2},{3,19},{19,3},{4,20},{20... | collective-permute-start | bytes 49160 | tf_op jit(solution)/shard_map/ppermute | solution.py:334
  67.9 0.8 collective-permute-done.1.other
  68.7 1.8 %shard_map.53 = bf16[16,200,128]{2,1,0:T(8,128)(2,1)S(1)} custom-call(f32[4,1024]{1,0:T(4,128)S(1)} %shard_map.52.mine, f32[4,1024]{1,0:T(4,128)S(1)} %collective-permute-done.1.other, f32[384,1024]{1,0:T(8,128)S(1)} %get-tuple-element.38.scores_a, f32[384,1024]{1,0:T(8,128)S(1)} %get-tuple-element.39.scores_b, bf16[1024,1024]{1,0:T(8,128)(2,1)S(1)} %copy-done, ...), custom_call_target="tpu_custom_call" | custom-call | flops 1610612736 | bytes 8388608 | tf_op jit(solution)/shard_map/pallas_call | solution.py:164
  70.5 24.9 %all_to_all.37.blocks = bf16[16,200,128]{2,1,0:T(8,128)(2,1)S(1)} all-to-all(bf16[16,200,128]{2,1,0:T(8,128)(2,1)S(1)} %shard_map.53), channel_id=1, replica_groups=mesh['y_hi'=2,'z'=8,'core'=2,'y_lo'=4,'x'=4] {'y_hi','z'}, dimensions={0} | all-to-all | bytes 1638400 | tf_op jit(solution)/shard_map/all_to_all | solution.py:294
  95.4 0.9 shard_map.54
  96.3 3.9 %all-to-all-start.3 = ((bf16[8,24,1024]{2,1,0:T(8,128)(2,1)}), bf16[8,24,1024]{2,1,0:T(8,128)(2,1)S(1)}, u32[]{:S(2)}, u32[]{:S(2)}) async-start(bf16[8,24,1024]{2,1,0:T(8,128)(2,1)} %get-tuple-element.45), calls=%async_computation.3 | async-start | bytes 786432 | tf_op jit(solution)/shard_map/all_to_all | solution.py:294
  100.2 4.1 %collective-permute-start.2 = (bf16[128,1024]{1,0:T(8,128)(2,1)S(1)}, bf16[128,1024]{1,0:T(8,128)(2,1)S(1)}, u32[]{:S(2)}, u32[]{:S(2)}) collective-permute-start(bf16[128,1024]{1,0:T(8,128)(2,1)S(1)} %copy-done.1), channel_id=1, source_target_pairs={{0,268},{4,264},{8,260},{12,256},{256,12},{260,8},{264,4},{268,0},... | collective-permute-start | bytes 786440 | tf_op jit(solution)/shard_map/ppermute | solution.py:343
  104.3 7.3 %all-to-all-done.3 = bf16[8,24,1024]{2,1,0:T(8,128)(2,1)S(1)} async-done(((bf16[8,24,1024]{2,1,0:T(8,128)(2,1)}), bf16[8,24,1024]{2,1,0:T(8,128)(2,1)S(1)}, u32[]{:S(2)}, u32[]{:S(2)}) %all-to-all-start.3) | async-done | bytes 393248 | tf_op jit(solution)/shard_map/all_to_all | solution.py:294
  111.6 6.3 %all_gather.3.fresh = bf16[2,192,1024]{2,1,0:T(8,128)(2,1)S(1)} all-gather(bf16[1,192,1024]{2,1,0:T(8,128)(2,1)S(1)} %bitcast.23), channel_id=1, replica_groups=mesh['y_hi'=2,'z'=8,'core'=2,'y_lo'=4,'x'=4] {'core'}, dimensions={0}, use_global_device_ids=true | all-gather | bytes 1179648 | tf_op jit(solution)/shard_map/all_gather | solution.py:344
  117.8 0.6 shard_map.55
  118.4 0.1 constant_dynamic-slice_fusion.1
  118.5 7.2 %collective-permute-start.3 = (bf16[144,1024]{1,0:T(8,128)(2,1)S(1)}, bf16[144,1024]{1,0:T(8,128)(2,1)S(1)}, u32[]{:S(2)}, u32[]{:S(2)}) collective-permute-start(bf16[144,1024]{1,0:T(8,128)(2,1)S(1)} %constant_dynamic-slice_fusion.1), channel_id=1, source_target_pairs={{0,256},{256,0},{1,257},{257,1},{2,258},{258,2},{3,259},{259,3},{4... | collective-permute-start | bytes 884744 | tf_op jit(solution)/shard_map/ppermute | solution.py:350
  125.8 14.1 %all_to_all.38.trios = f32[16,8,256]{2,1,0:T(8,128)S(1)} all-to-all(f32[16,8,256]{2,1,0:T(8,128)S(1)} %get-tuple-element.51), channel_id=1, replica_groups=mesh['y_hi'=2,'z'=8,'core'=2,'y_lo'=4,'x'=4] {'core','z'}, dimensions={0} | all-to-all | bytes 262144 | tf_op jit(solution)/shard_map/all_to_all | solution.py:294
  139.9 1.3 shard_map.56
  141.2 4.4 %all-to-all-start.5 = ((bf16[32,8,1152]{2,1,0:T(8,128)(2,1)}), bf16[32,8,1152]{2,1,0:T(8,128)(2,1)S(1)}, u32[]{:S(2)}, u32[]{:S(2)}) async-start(bf16[32,8,1152]{2,1,0:T(8,128)(2,1)} %bitcast.7), calls=%async_computation.5 | async-start | bytes 1179648 | tf_op jit(solution)/shard_map/all_to_all | solution.py:294
  145.7 2.9 %collective-permute-start.4 = (bf16[48,1024]{1,0:T(8,128)(2,1)S(1)}, bf16[48,1024]{1,0:T(8,128)(2,1)S(1)}, u32[]{:S(2)}, u32[]{:S(2)}) collective-permute-start(bf16[48,1024]{1,0:T(8,128)(2,1)S(1)} %slice_select_fusion), channel_id=1, source_target_pairs={{0,32},{32,0},{64,96},{96,64},{128,160},{160,128},{192,224},{224,1... | collective-permute-start | bytes 294920 | tf_op jit(solution)/shard_map/ppermute | solution.py:355
  148.5 2.5 %collective-permute-done.4 = bf16[48,1024]{1,0:T(8,128)(2,1)S(1)} collective-permute-done((bf16[48,1024]{1,0:T(8,128)(2,1)S(1)}, bf16[48,1024]{1,0:T(8,128)(2,1)S(1)}, u32[]{:S(2)}, u32[]{:S(2)}) %collective-permute-start.4) | collective-permute-done | bytes 98336 | tf_op jit(solution)/shard_map/ppermute | solution.py:355
  151.0 0.1 maximum_select_fusion
  151.1 5.1 %collective-permute-start.5 = (bf16[192,1024]{1,0:T(8,128)(2,1)S(1)}, bf16[192,1024]{1,0:T(8,128)(2,1)S(1)}, u32[]{:S(2)}, u32[]{:S(2)}) collective-permute-start(bf16[192,1024]{1,0:T(8,128)(2,1)S(1)} %maximum_select_fusion), channel_id=1, source_target_pairs={{0,16},{16,0},{1,17},{17,1},{2,18},{18,2},{3,19},{19,3},{4,20},{20... | collective-permute-start | bytes 1179656 | tf_op jit(solution)/shard_map/ppermute | solution.py:363
  156.2 1.3 collective-permute-done.5
  157.5 0.1 broadcast_select_fusion.5
  157.7 1.3 pad_maximum_fusion
  158.9 3.4 %all-to-all-done.5.blocks = bf16[32,8,1152]{2,1,0:T(8,128)(2,1)S(1)} async-done(((bf16[32,8,1152]{2,1,0:T(8,128)(2,1)}), bf16[32,8,1152]{2,1,0:T(8,128)(2,1)S(1)}, u32[]{:S(2)}, u32[]{:S(2)}) %all-to-all-start.5) | async-done | bytes 589856 | tf_op jit(solution)/shard_map/all_to_all | solution.py:294
  162.4 0.1 shard_map.57
  162.5 12.2 %all_to_all.39 = bf16[16,8,1024]{2,1,0:T(8,128)(2,1)S(1)} all-to-all(bf16[16,8,1024]{2,1,0:T(8,128)(2,1)S(1)} %shard_map.57), channel_id=1, replica_groups=mesh['y_hi'=2,'z'=8,'core'=2,'y_lo'=4,'x'=4] {'x','y_lo'}, dimensions={0} | all-to-all | bytes 524288 | tf_op jit(solution)/shard_map/all_to_all | solution.py:294
  174.7 0.7 copy.6
  (12 shorter events, 0.2 us)
Async XLA Ops:
  0.6 42.2 %copy-start = (bf16[1024,1024]{1,0:T(8,128)(2,1)S(1)}, bf16[1024,1024]{1,0:T(8,128)(2,1)}, u32[]{:S(2)}) copy-start(bf16[1024,1024]{1,0:T(8,128)(2,1)} %points_a.1) | copy-start | bytes 6291460
  0.7 0.9 copy-start.2
  1.7 41.2 %collective-permute-start = (bf16[1024,1024]{1,0:T(8,128)(2,1)}, bf16[1024,1024]{1,0:T(8,128)(2,1)S(1)}, u32[]{:S(2)}, u32[]{:S(2)}) collective-permute-start(bf16[1024,1024]{1,0:T(8,128)(2,1)} %points_a.1), channel_id=1, source_target_pairs={{0,16},{16,0},{1,17},{17,1},{2,18},{18,2},{3,19},{19,3},{4,20},{20... | collective-permute-start | bytes 6291464 | tf_op jit(solution)/shard_map/ppermute | solution.py:330
  62.6 6.1 %collective-permute-start.1 = (f32[4,1024]{1,0:T(4,128)S(1)}, f32[4,1024]{1,0:T(4,128)S(1)}, u32[]{:S(2)}, u32[]{:S(2)}) collective-permute-start(f32[4,1024]{1,0:T(4,128)S(1)} %shard_map.52.mine), channel_id=1, source_target_pairs={{0,16},{16,0},{1,17},{17,1},{2,18},{18,2},{3,19},{19,3},{4,20},{20... | collective-permute-start | bytes 49160 | tf_op jit(solution)/shard_map/ppermute | solution.py:334
  70.5 29.7 %copy-start.1 = (bf16[128,1024]{1,0:T(8,128)(2,1)S(1)}, bf16[128,1024]{1,0:T(8,128)(2,1)}, u32[]{:S(2)}) copy-start(bf16[128,1024]{1,0:T(8,128)(2,1)} %near.1) | copy-start | bytes 786436
  96.3 15.3 %all-to-all-start.3 = ((bf16[8,24,1024]{2,1,0:T(8,128)(2,1)}), bf16[8,24,1024]{2,1,0:T(8,128)(2,1)S(1)}, u32[]{:S(2)}, u32[]{:S(2)}) async-start(bf16[8,24,1024]{2,1,0:T(8,128)(2,1)} %get-tuple-element.45), calls=%async_computation.3 | async-start | bytes 786432 | tf_op jit(solution)/shard_map/all_to_all | solution.py:294
  100.2 17.6 %collective-permute-start.2 = (bf16[128,1024]{1,0:T(8,128)(2,1)S(1)}, bf16[128,1024]{1,0:T(8,128)(2,1)S(1)}, u32[]{:S(2)}, u32[]{:S(2)}) collective-permute-start(bf16[128,1024]{1,0:T(8,128)(2,1)S(1)} %copy-done.1), channel_id=1, source_target_pairs={{0,268},{4,264},{8,260},{12,256},{256,12},{260,8},{264,4},{268,0},... | collective-permute-start | bytes 786440 | tf_op jit(solution)/shard_map/ppermute | solution.py:343
  118.5 22.7 %collective-permute-start.3 = (bf16[144,1024]{1,0:T(8,128)(2,1)S(1)}, bf16[144,1024]{1,0:T(8,128)(2,1)S(1)}, u32[]{:S(2)}, u32[]{:S(2)}) collective-permute-start(bf16[144,1024]{1,0:T(8,128)(2,1)S(1)} %constant_dynamic-slice_fusion.1), channel_id=1, source_target_pairs={{0,256},{256,0},{1,257},{257,1},{2,258},{258,2},{3,259},{259,3},{4... | collective-permute-start | bytes 884744 | tf_op jit(solution)/shard_map/ppermute | solution.py:350
  141.2 21.2 %all-to-all-start.5 = ((bf16[32,8,1152]{2,1,0:T(8,128)(2,1)}), bf16[32,8,1152]{2,1,0:T(8,128)(2,1)S(1)}, u32[]{:S(2)}, u32[]{:S(2)}) async-start(bf16[32,8,1152]{2,1,0:T(8,128)(2,1)} %bitcast.7), calls=%async_computation.5 | async-start | bytes 1179648 | tf_op jit(solution)/shard_map/all_to_all | solution.py:294
  145.7 5.4 %collective-permute-start.4 = (bf16[48,1024]{1,0:T(8,128)(2,1)S(1)}, bf16[48,1024]{1,0:T(8,128)(2,1)S(1)}, u32[]{:S(2)}, u32[]{:S(2)}) collective-permute-start(bf16[48,1024]{1,0:T(8,128)(2,1)S(1)} %slice_select_fusion), channel_id=1, source_target_pairs={{0,32},{32,0},{64,96},{96,64},{128,160},{160,128},{192,224},{224,1... | collective-permute-start | bytes 294920 | tf_op jit(solution)/shard_map/ppermute | solution.py:355
  151.1 6.4 %collective-permute-start.5 = (bf16[192,1024]{1,0:T(8,128)(2,1)S(1)}, bf16[192,1024]{1,0:T(8,128)(2,1)S(1)}, u32[]{:S(2)}, u32[]{:S(2)}) collective-permute-start(bf16[192,1024]{1,0:T(8,128)(2,1)S(1)} %maximum_select_fusion), channel_id=1, source_target_pairs={{0,16},{16,0},{1,17},{17,1},{2,18},{18,2},{3,19},{19,3},{4,20},{20... | collective-permute-start | bytes 1179656 | tf_op jit(solution)/shard_map/ppermute | solution.py:363

commit v9 on v8

--- a/solution.py
+++ b/solution.py
@@ -14,7 +14,7 @@
 SWAP = [(0, 1), (1, 0)]
 D = 1024
 WIDE = 1152
-STEP = 512
+STEP = 1024
 ROWS = 384
 OWN = 24
 PACK = 200

time: 178 us -> 178 us (level)
  no operation moved by 1% of the time
where the time goes in v9:
time: 178 us; the launch traced here: 175 us
  blocking collectives  107 us (60%)
  starting transfers between devices  41.9 us (24%)
  waiting for transfers between devices  15.2 us (9%)
  Pallas kernels  7.11 us (4%)
  local copies, waits for them, and re-layouts  1.78 us (1%)
    all_to_all x5, blocking collectives, exchange(): return lax.all_to_all(blocks, axes, 0, 0)  101 us
    all_to_all x2, waiting for transfers between devices, exchange(): return lax.all_to_all(blocks, axes, 0, 0)  10.6 us
    ppermute x1, starting transfers between devices, on_device(): points_other = lax.ppermute(points, 'core', SWAP)  8.79 us
    all_to_all x2, starting transfers between devices, exchange(): return lax.all_to_all(blocks, axes, 0, 0)  8.33 us
    ppermute x1, starting transfers between devices, on_device(): part = lax.ppermute(part, 'y_hi', SWAP)  7.27 us
    all_gather x1, blocking collectives, on_device(): fresh = lax.all_gather(mine, 'core')  6.29 us
    ppermute x1, starting transfers between devices, on_device(): other = lax.ppermute(mine, 'core', SWAP)  5.44 us
    ppermute x1, starting transfers between devices, on_device(): far_other = lax.ppermute(far_mine, 'core', SWAP)  5.1 us
  transfers between devices with their start and end apart: 8, of which 5 were waited for; matrix products, arithmetic and copies ran while one was open for 1% of the time, Pallas kernels for 1%

profile of v9, /device:TPU:1, one launch (start us, length us, event | category | flops | bytes accessed | tf_op | source)
XLA Modules:
  0.0 175.4 jit_solution(4478825575940675)
XLA Ops:
  0.7 0.9 copy-done.2
  1.7 8.8 %collective-permute-start = (bf16[1024,1024]{1,0:T(8,128)(2,1)}, bf16[1024,1024]{1,0:T(8,128)(2,1)S(1)}, u32[]{:S(2)}, u32[]{:S(2)}) collective-permute-start(bf16[1024,1024]{1,0:T(8,128)(2,1)} %points_a.1), channel_id=1, source_target_pairs={{0,16},{16,0},{1,17},{17,1},{2,18},{18,2},{3,19},{19,3},{4,20},{20... | collective-permute-start | bytes 6291464 | tf_op jit(solution)/shard_map/ppermute | solution.py:330
  10.5 32.4 %all_to_all.35 = bf16[32,32,384]{2,1,0:T(8,128)(2,1)S(1)} all-to-all(bf16[32,32,384]{2,1,0:T(8,128)(2,1)S(1)} %shard_map.50), channel_id=1, replica_groups=mesh['y_hi'=2,'z'=8,'core'=2,'y_lo'=4,'x'=4] {'y_hi','z','core'}, dimensions={0} | all-to-all | bytes 1572864 | tf_op jit(solution)/shard_map/all_to_all | solution.py:294
  42.8 2.2 %shard_map.51 = (bf16[384,1024]{1,0:T(8,128)(2,1)S(1)}, f32[384,1024]{1,0:T(8,128)S(1)}, f32[384,1024]{1,0:T(8,128)S(1)}, f32[16,4,1024]{2,1,0:T(4,128)S(1)}) custom-call(bf16[1024,384]{1,0:T(8,128)(2,1)S(1)} %bitcast.21, bf16[1024,1024]{1,0:T(8,128)(2,1)S(1)} %copy-done, bf16[1024,1024]{1,0:T(8,128)(2,1)S(1)} %collective-permute-done.points_b), custom_call_target="tpu_custom_call" | custom-call | flops 1610612736 | bytes 8388608 | tf_op jit(solution)/shard_map/pallas_call | solution.py:103
  45.1 17.3 %all_to_all.36.pairs = f32[16,4,1024]{2,1,0:T(4,128)S(1)} all-to-all(f32[16,4,1024]{2,1,0:T(4,128)S(1)} %get-tuple-element.37), channel_id=1, replica_groups=mesh['y_hi'=2,'z'=8,'core'=2,'y_lo'=4,'x'=4] {'x','y_lo'}, dimensions={0} | all-to-all | bytes 524288 | tf_op jit(solution)/shard_map/all_to_all | solution.py:294
  62.4 0.1 shard_map.52.mine
  62.5 5.4 %collective-permute-start.1 = (f32[4,1024]{1,0:T(4,128)S(1)}, f32[4,1024]{1,0:T(4,128)S(1)}, u32[]{:S(2)}, u32[]{:S(2)}) collective-permute-start(f32[4,1024]{1,0:T(4,128)S(1)} %shard_map.52.mine), channel_id=1, source_target_pairs={{0,16},{16,0},{1,17},{17,1},{2,18},{18,2},{3,19},{19,3},{4,20},{20... | collective-permute-start | bytes 49160 | tf_op jit(solution)/shard_map/ppermute | solution.py:334
  67.9 0.8 collective-permute-done.1.other
  68.7 1.8 %shard_map.53 = bf16[16,200,128]{2,1,0:T(8,128)(2,1)S(1)} custom-call(f32[4,1024]{1,0:T(4,128)S(1)} %shard_map.52.mine, f32[4,1024]{1,0:T(4,128)S(1)} %collective-permute-done.1.other, f32[384,1024]{1,0:T(8,128)S(1)} %get-tuple-element.38.scores_a, f32[384,1024]{1,0:T(8,128)S(1)} %get-tuple-element.39.scores_b, bf16[1024,1024]{1,0:T(8,128)(2,1)S(1)} %copy-done, ...), custom_call_target="tpu_custom_call" | custom-call | flops 1610612736 | bytes 8388608 | tf_op jit(solution)/shard_map/pallas_call | solution.py:164
  70.5 24.8 %all_to_all.37.blocks = bf16[16,200,128]{2,1,0:T(8,128)(2,1)S(1)} all-to-all(bf16[16,200,128]{2,1,0:T(8,128)(2,1)S(1)} %shard_map.53), channel_id=1, replica_groups=mesh['y_hi'=2,'z'=8,'core'=2,'y_lo'=4,'x'=4] {'y_hi','z'}, dimensions={0} | all-to-all | bytes 1638400 | tf_op jit(solution)/shard_map/all_to_all | solution.py:294
  95.4 0.9 shard_map.54
  96.3 3.9 %all-to-all-start.3 = ((bf16[8,24,1024]{2,1,0:T(8,128)(2,1)}), bf16[8,24,1024]{2,1,0:T(8,128)(2,1)S(1)}, u32[]{:S(2)}, u32[]{:S(2)}) async-start(bf16[8,24,1024]{2,1,0:T(8,128)(2,1)} %get-tuple-element.45), calls=%async_computation.3 | async-start | bytes 786432 | tf_op jit(solution)/shard_map/all_to_all | solution.py:294
  100.2 4.1 %collective-permute-start.2 = (bf16[128,1024]{1,0:T(8,128)(2,1)S(1)}, bf16[128,1024]{1,0:T(8,128)(2,1)S(1)}, u32[]{:S(2)}, u32[]{:S(2)}) collective-permute-start(bf16[128,1024]{1,0:T(8,128)(2,1)S(1)} %copy-done.1), channel_id=1, source_target_pairs={{0,268},{4,264},{8,260},{12,256},{256,12},{260,8},{264,4},{268,0},... | collective-permute-start | bytes 786440 | tf_op jit(solution)/shard_map/ppermute | solution.py:343
  104.3 7.2 %all-to-all-done.3 = bf16[8,24,1024]{2,1,0:T(8,128)(2,1)S(1)} async-done(((bf16[8,24,1024]{2,1,0:T(8,128)(2,1)}), bf16[8,24,1024]{2,1,0:T(8,128)(2,1)S(1)}, u32[]{:S(2)}, u32[]{:S(2)}) %all-to-all-start.3) | async-done | bytes 393248 | tf_op jit(solution)/shard_map/all_to_all | solution.py:294
  111.5 6.3 %all_gather.3.fresh = bf16[2,192,1024]{2,1,0:T(8,128)(2,1)S(1)} all-gather(bf16[1,192,1024]{2,1,0:T(8,128)(2,1)S(1)} %bitcast.23), channel_id=1, replica_groups=mesh['y_hi'=2,'z'=8,'core'=2,'y_lo'=4,'x'=4] {'core'}, dimensions={0}, use_global_device_ids=true | all-gather | bytes 1179648 | tf_op jit(solution)/shard_map/all_gather | solution.py:344
  117.8 0.6 shard_map.55
  118.4 0.1 constant_dynamic-slice_fusion.1
  118.5 7.3 %collective-permute-start.3 = (bf16[144,1024]{1,0:T(8,128)(2,1)S(1)}, bf16[144,1024]{1,0:T(8,128)(2,1)S(1)}, u32[]{:S(2)}, u32[]{:S(2)}) collective-permute-start(bf16[144,1024]{1,0:T(8,128)(2,1)S(1)} %constant_dynamic-slice_fusion.1), channel_id=1, source_target_pairs={{0,256},{256,0},{1,257},{257,1},{2,258},{258,2},{3,259},{259,3},{4... | collective-permute-start | bytes 884744 | tf_op jit(solution)/shard_map/ppermute | solution.py:350
  125.8 14.1 %all_to_all.38.trios = f32[16,8,256]{2,1,0:T(8,128)S(1)} all-to-all(f32[16,8,256]{2,1,0:T(8,128)S(1)} %get-tuple-element.51), channel_id=1, replica_groups=mesh['y_hi'=2,'z'=8,'core'=2,'y_lo'=4,'x'=4] {'core','z'}, dimensions={0} | all-to-all | bytes 262144 | tf_op jit(solution)/shard_map/all_to_all | solution.py:294
  139.9 1.3 shard_map.56
  141.2 4.4 %all-to-all-start.5 = ((bf16[32,8,1152]{2,1,0:T(8,128)(2,1)}), bf16[32,8,1152]{2,1,0:T(8,128)(2,1)S(1)}, u32[]{:S(2)}, u32[]{:S(2)}) async-start(bf16[32,8,1152]{2,1,0:T(8,128)(2,1)} %bitcast.7), calls=%async_computation.5 | async-start | bytes 1179648 | tf_op jit(solution)/shard_map/all_to_all | solution.py:294
  145.7 2.9 %collective-permute-start.4 = (bf16[48,1024]{1,0:T(8,128)(2,1)S(1)}, bf16[48,1024]{1,0:T(8,128)(2,1)S(1)}, u32[]{:S(2)}, u32[]{:S(2)}) collective-permute-start(bf16[48,1024]{1,0:T(8,128)(2,1)S(1)} %slice_select_fusion), channel_id=1, source_target_pairs={{0,32},{32,0},{64,96},{96,64},{128,160},{160,128},{192,224},{224,1... | collective-permute-start | bytes 294920 | tf_op jit(solution)/shard_map/ppermute | solution.py:355
  148.5 2.5 %collective-permute-done.4 = bf16[48,1024]{1,0:T(8,128)(2,1)S(1)} collective-permute-done((bf16[48,1024]{1,0:T(8,128)(2,1)S(1)}, bf16[48,1024]{1,0:T(8,128)(2,1)S(1)}, u32[]{:S(2)}, u32[]{:S(2)}) %collective-permute-start.4) | collective-permute-done | bytes 98336 | tf_op jit(solution)/shard_map/ppermute | solution.py:355
  151.0 0.1 maximum_select_fusion
  151.1 5.1 %collective-permute-start.5 = (bf16[192,1024]{1,0:T(8,128)(2,1)S(1)}, bf16[192,1024]{1,0:T(8,128)(2,1)S(1)}, u32[]{:S(2)}, u32[]{:S(2)}) collective-permute-start(bf16[192,1024]{1,0:T(8,128)(2,1)S(1)} %maximum_select_fusion), channel_id=1, source_target_pairs={{0,16},{16,0},{1,17},{17,1},{2,18},{18,2},{3,19},{19,3},{4,20},{20... | collective-permute-start | bytes 1179656 | tf_op jit(solution)/shard_map/ppermute | solution.py:363
  156.2 1.3 collective-permute-done.5
  157.5 0.1 broadcast_select_fusion.5
  157.7 1.3 pad_maximum_fusion
  158.9 3.4 %all-to-all-done.5.blocks = bf16[32,8,1152]{2,1,0:T(8,128)(2,1)S(1)} async-done(((bf16[32,8,1152]{2,1,0:T(8,128)(2,1)}), bf16[32,8,1152]{2,1,0:T(8,128)(2,1)S(1)}, u32[]{:S(2)}, u32[]{:S(2)}) %all-to-all-start.5) | async-done | bytes 589856 | tf_op jit(solution)/shard_map/all_to_all | solution.py:294
  162.4 0.1 shard_map.57
  162.5 12.2 %all_to_all.39 = bf16[16,8,1024]{2,1,0:T(8,128)(2,1)S(1)} all-to-all(bf16[16,8,1024]{2,1,0:T(8,128)(2,1)S(1)} %shard_map.57), channel_id=1, replica_groups=mesh['y_hi'=2,'z'=8,'core'=2,'y_lo'=4,'x'=4] {'x','y_lo'}, dimensions={0} | all-to-all | bytes 524288 | tf_op jit(solution)/shard_map/all_to_all | solution.py:294
  174.7 0.7 copy.6
  (12 shorter events, 0.2 us)
Async XLA Ops:
  0.6 42.2 %copy-start = (bf16[1024,1024]{1,0:T(8,128)(2,1)S(1)}, bf16[1024,1024]{1,0:T(8,128)(2,1)}, u32[]{:S(2)}) copy-start(bf16[1024,1024]{1,0:T(8,128)(2,1)} %points_a.1) | copy-start | bytes 6291460
  0.7 0.9 copy-start.2
  1.7 41.2 %collective-permute-start = (bf16[1024,1024]{1,0:T(8,128)(2,1)}, bf16[1024,1024]{1,0:T(8,128)(2,1)S(1)}, u32[]{:S(2)}, u32[]{:S(2)}) collective-permute-start(bf16[1024,1024]{1,0:T(8,128)(2,1)} %points_a.1), channel_id=1, source_target_pairs={{0,16},{16,0},{1,17},{17,1},{2,18},{18,2},{3,19},{19,3},{4,20},{20... | collective-permute-start | bytes 6291464 | tf_op jit(solution)/shard_map/ppermute | solution.py:330
  62.5 6.3 %collective-permute-start.1 = (f32[4,1024]{1,0:T(4,128)S(1)}, f32[4,1024]{1,0:T(4,128)S(1)}, u32[]{:S(2)}, u32[]{:S(2)}) collective-permute-start(f32[4,1024]{1,0:T(4,128)S(1)} %shard_map.52.mine), channel_id=1, source_target_pairs={{0,16},{16,0},{1,17},{17,1},{2,18},{18,2},{3,19},{19,3},{4,20},{20... | collective-permute-start | bytes 49160 | tf_op jit(solution)/shard_map/ppermute | solution.py:334
  70.5 29.6 %copy-start.1 = (bf16[128,1024]{1,0:T(8,128)(2,1)S(1)}, bf16[128,1024]{1,0:T(8,128)(2,1)}, u32[]{:S(2)}) copy-start(bf16[128,1024]{1,0:T(8,128)(2,1)} %near.1) | copy-start | bytes 786436
  96.3 15.2 %all-to-all-start.3 = ((bf16[8,24,1024]{2,1,0:T(8,128)(2,1)}), bf16[8,24,1024]{2,1,0:T(8,128)(2,1)S(1)}, u32[]{:S(2)}, u32[]{:S(2)}) async-start(bf16[8,24,1024]{2,1,0:T(8,128)(2,1)} %get-tuple-element.45), calls=%async_computation.3 | async-start | bytes 786432 | tf_op jit(solution)/shard_map/all_to_all | solution.py:294
  100.2 17.6 %collective-permute-start.2 = (bf16[128,1024]{1,0:T(8,128)(2,1)S(1)}, bf16[128,1024]{1,0:T(8,128)(2,1)S(1)}, u32[]{:S(2)}, u32[]{:S(2)}) collective-permute-start(bf16[128,1024]{1,0:T(8,128)(2,1)S(1)} %copy-done.1), channel_id=1, source_target_pairs={{0,268},{4,264},{8,260},{12,256},{256,12},{260,8},{264,4},{268,0},... | collective-permute-start | bytes 786440 | tf_op jit(solution)/shard_map/ppermute | solution.py:343
  118.5 22.7 %collective-permute-start.3 = (bf16[144,1024]{1,0:T(8,128)(2,1)S(1)}, bf16[144,1024]{1,0:T(8,128)(2,1)S(1)}, u32[]{:S(2)}, u32[]{:S(2)}) collective-permute-start(bf16[144,1024]{1,0:T(8,128)(2,1)S(1)} %constant_dynamic-slice_fusion.1), channel_id=1, source_target_pairs={{0,256},{256,0},{1,257},{257,1},{2,258},{258,2},{3,259},{259,3},{4... | collective-permute-start | bytes 884744 | tf_op jit(solution)/shard_map/ppermute | solution.py:350
  141.2 21.2 %all-to-all-start.5 = ((bf16[32,8,1152]{2,1,0:T(8,128)(2,1)}), bf16[32,8,1152]{2,1,0:T(8,128)(2,1)S(1)}, u32[]{:S(2)}, u32[]{:S(2)}) async-start(bf16[32,8,1152]{2,1,0:T(8,128)(2,1)} %bitcast.7), calls=%async_computation.5 | async-start | bytes 1179648 | tf_op jit(solution)/shard_map/all_to_all | solution.py:294
  145.7 5.4 %collective-permute-start.4 = (bf16[48,1024]{1,0:T(8,128)(2,1)S(1)}, bf16[48,1024]{1,0:T(8,128)(2,1)S(1)}, u32[]{:S(2)}, u32[]{:S(2)}) collective-permute-start(bf16[48,1024]{1,0:T(8,128)(2,1)S(1)} %slice_select_fusion), channel_id=1, source_target_pairs={{0,32},{32,0},{64,96},{96,64},{128,160},{160,128},{192,224},{224,1... | collective-permute-start | bytes 294920 | tf_op jit(solution)/shard_map/ppermute | solution.py:355
  151.1 6.4 %collective-permute-start.5 = (bf16[192,1024]{1,0:T(8,128)(2,1)S(1)}, bf16[192,1024]{1,0:T(8,128)(2,1)S(1)}, u32[]{:S(2)}, u32[]{:S(2)}) collective-permute-start(bf16[192,1024]{1,0:T(8,128)(2,1)S(1)} %maximum_select_fusion), channel_id=1, source_target_pairs={{0,16},{16,0},{1,17},{17,1},{2,18},{18,2},{3,19},{19,3},{4,20},{20... | collective-permute-start | bytes 1179656 | tf_op jit(solution)/shard_map/ppermute | solution.py:363
